TPU v7x, 32 devices: a whole 2x2x4 slice. The times are simulated.
32 devices in a mesh: dp: 4 (over x, core), fsdp: 8 (over z, y).
Axes of the slice: x: 2, y: 2, z: 4, core: 2. Of those that a mesh axis runs over, the one named last changes fastest.
Arguments:
- tokens: bfloat16 [32768, 1024], P(('dp', 'fsdp')), may hold values from -6 to 6
- segment_ids: int32 [64, 512], P(('dp', 'fsdp')), may hold values from 0 to 5, never falling along the last dimension, each value on 1 to 200 neighbouring positions
- w_query: bfloat16 [1024, 1024], P(('dp', 'fsdp')), may hold values from -0.1875 to 0.1875
- b_query: bfloat16 [1024], P(('dp', 'fsdp')), may hold values from -3 to 3
- w_key: bfloat16 [1024, 1024], P(('dp', 'fsdp')), may hold values from -0.1875 to 0.1875
- w_value: bfloat16 [1024, 1024], P(('dp', 'fsdp')), may hold values from -0.1875 to 0.1875
- b_value: bfloat16 [1024], P(('dp', 'fsdp')), may hold values from -3 to 3
- w_out: bfloat16 [1024, 1024], P(('dp', 'fsdp')), may hold values from -1.5 to 1.5
- b_out: bfloat16 [1024], P(('dp', 'fsdp')), may hold values from -2 to 2
- ln1_gain: bfloat16 [1024], P(('dp', 'fsdp')), may hold values from 0.5 to 1.5
- ln1_bias: bfloat16 [1024], P(('dp', 'fsdp')), may hold values from -2 to 2
- w_up: bfloat16 [1024, 4096], P(('dp', 'fsdp')), may hold values from -0.1875 to 0.1875
- b_up: bfloat16 [4096], P(('dp', 'fsdp')), may hold values from -3 to 3
- w_down: bfloat16 [4096, 1024], P(('dp', 'fsdp')), may hold values from -0.09375 to 0.09375
- b_down: bfloat16 [1024], P(('dp', 'fsdp')), may hold values from -2 to 2
- ln2_gain: bfloat16 [1024], P(('dp', 'fsdp')), may hold values from 0.5 to 1.5
- ln2_bias: bfloat16 [1024], P(('dp', 'fsdp')), may hold values from -2 to 2
- out_cotangent: float32 [32768, 1024], P(('dp', 'fsdp')), may hold values from -6 to 6
Outputs:
- output: bfloat16 [32768, 1024], P(('dp', 'fsdp'))
- tokens_grad: bfloat16 [32768, 1024], P(('dp', 'fsdp'))
- w_query_grad: float32 [1024, 1024], P(('dp', 'fsdp'))
- b_query_grad: float32 [1024], P(('dp', 'fsdp'))
- w_key_grad: float32 [1024, 1024], P(('dp', 'fsdp'))
- w_value_grad: float32 [1024, 1024], P(('dp', 'fsdp'))
- b_value_grad: float32 [1024], P(('dp', 'fsdp'))
- w_out_grad: float32 [1024, 1024], P(('dp', 'fsdp'))
- b_out_grad: float32 [1024], P(('dp', 'fsdp'))
- ln1_gain_grad: float32 [1024], P(('dp', 'fsdp'))
- ln1_bias_grad: float32 [1024], P(('dp', 'fsdp'))
- w_up_grad: float32 [1024, 4096], P(('dp', 'fsdp'))
- b_up_grad: float32 [4096], P(('dp', 'fsdp'))
- w_down_grad: float32 [4096, 1024], P(('dp', 'fsdp'))
- b_down_grad: float32 [1024], P(('dp', 'fsdp'))
- ln2_gain_grad: float32 [1024], P(('dp', 'fsdp'))
- ln2_bias_grad: float32 [1024], P(('dp', 'fsdp'))
Inputs may be any that keep to these rules, and one draw needn't show every extreme that they name: `segment_ids`: document numbers never fall along a sequence of 512 tokens; a document holds at most 200 tokens.
All inputs are finite; a program needn't handle non-finite values.
Results may differ from a plain program's by a relative error of at most 0.014.
Values may be sent and summed in bfloat16 or wider, within the bound.
No kernel may reach another device: no remote copies, remote signals or barrier semaphores. Data moves between devices by JAX's collectives and lax.ppermute only.
A program may use at most 256 MiB of HBM per device.

v0:
```python
import jax
import jax.numpy as jnp
from jax import lax
from jax.sharding import PartitionSpec as P

D = 1024
H = 16
DH = 64
SEQ_LEN = 512


def matmul(operand, other):
    return jnp.dot(operand, other, preferred_element_type=jnp.float32)


def back_matmul(operand, other):
    return lax.dot_general(
        operand, other, (((1,), (1,)), ((), ())), preferred_element_type=jnp.float32
    )


def outer_sum(operand, other):
    return lax.dot_general(
        operand, other, (((0,), (0,)), ((), ())), preferred_element_type=jnp.float32
    )


def column_sum(values):
    return jnp.sum(values.astype(jnp.float32), axis=0)


def norm_forward(hidden):
    centred = hidden - jnp.mean(hidden, axis=-1, keepdims=True)
    scale_row = lax.rsqrt(jnp.mean(centred * centred, axis=-1, keepdims=True) + 1e-12)
    return (centred * scale_row, scale_row)


def norm_backward(grad_out, normed, scale_row, scaling):
    scaled = grad_out * scaling
    return scale_row * (
        scaled
        - jnp.mean(scaled, axis=-1, keepdims=True)
        - normed * jnp.mean(scaled * normed, axis=-1, keepdims=True)
    )


def gelu_slope(values):
    return (
        0.5 * (1.0 + lax.erf(values * 0.7071067811865476))
        + values * jnp.exp(-0.5 * values * values) * 0.3989422804014327
    )


def masked_scores(query_rows, key_rows, doc_ids):
    scores = (
        jnp.einsum("qhd,khd->hqk", query_rows, key_rows, preferred_element_type=jnp.float32) * 0.125
    )
    same_doc = doc_ids[:, None] == doc_ids[None, :]
    return jnp.where(same_doc[None], scores, -1000000000.0)


def attend_forward(pieces):
    query_rows, key_rows, value_rows, doc_ids = pieces
    scores = masked_scores(query_rows, key_rows, doc_ids)
    row_peak = jnp.max(scores, axis=-1, keepdims=True)
    powers = jnp.exp(scores - row_peak)
    row_total = jnp.sum(powers, axis=-1, keepdims=True)
    probability = (powers / row_total).astype(jnp.bfloat16)
    mixed_heads = jnp.einsum(
        "hqk,khd->qhd", probability, value_rows, preferred_element_type=jnp.float32
    )
    logsum = (row_peak + jnp.log(row_total))[:, :, 0]
    return (mixed_heads.astype(jnp.bfloat16).reshape(mixed_heads.shape[0], H * DH), logsum)


def attend_backward(pieces):
    query_rows, key_rows, value_rows, doc_ids, logsum, grad_heads = pieces
    scores = masked_scores(query_rows, key_rows, doc_ids)
    probability = jnp.exp(scores - logsum[:, :, None])
    grad_prob = jnp.einsum(
        "qhd,khd->hqk", grad_heads, value_rows, preferred_element_type=jnp.float32
    )
    row_delta = jnp.sum(probability * grad_prob, axis=-1, keepdims=True)
    grad_scores = (probability * (grad_prob - row_delta)).astype(jnp.bfloat16)
    grad_query = (
        jnp.einsum("hqk,khd->qhd", grad_scores, key_rows, preferred_element_type=jnp.float32)
        * 0.125
    )
    grad_key = (
        jnp.einsum("hqk,qhd->khd", grad_scores, query_rows, preferred_element_type=jnp.float32)
        * 0.125
    )
    grad_value = jnp.einsum(
        "hqk,qhd->khd",
        probability.astype(jnp.bfloat16),
        grad_heads,
        preferred_element_type=jnp.float32,
    )
    return (
        grad_query.astype(jnp.bfloat16),
        grad_key.astype(jnp.bfloat16),
        grad_value.astype(jnp.bfloat16),
    )


def per_device(
    tokens,
    segment_ids,
    w_query,
    b_query,
    w_key,
    w_value,
    b_value,
    w_out,
    b_out,
    ln1_gain,
    ln1_bias,
    w_up,
    b_up,
    w_down,
    b_down,
    ln2_gain,
    ln2_bias,
    out_cotangent,
):
    (
        full_query,
        full_key,
        full_value,
        full_out,
        bias_query,
        bias_value,
        bias_out,
        gain_one,
        shift_one,
    ) = (
        lax.all_gather(w_query, ("dp", "fsdp"), axis=0, tiled=True),
        lax.all_gather(w_key, ("dp", "fsdp"), axis=0, tiled=True),
        lax.all_gather(w_value, ("dp", "fsdp"), axis=0, tiled=True),
        lax.all_gather(w_out, ("dp", "fsdp"), axis=0, tiled=True),
        lax.all_gather(b_query, ("dp", "fsdp"), axis=0, tiled=True),
        lax.all_gather(b_value, ("dp", "fsdp"), axis=0, tiled=True),
        lax.all_gather(b_out, ("dp", "fsdp"), axis=0, tiled=True),
        lax.all_gather(ln1_gain, ("dp", "fsdp"), axis=0, tiled=True),
        lax.all_gather(ln1_bias, ("dp", "fsdp"), axis=0, tiled=True),
    )
    full_up, full_down, bias_up, bias_down, gain_two, shift_two = (
        lax.all_gather(w_up, ("dp", "fsdp"), axis=0, tiled=True),
        lax.all_gather(w_down, ("dp", "fsdp"), axis=0, tiled=True),
        lax.all_gather(b_up, ("dp", "fsdp"), axis=0, tiled=True),
        lax.all_gather(b_down, ("dp", "fsdp"), axis=0, tiled=True),
        lax.all_gather(ln2_gain, ("dp", "fsdp"), axis=0, tiled=True),
        lax.all_gather(ln2_bias, ("dp", "fsdp"), axis=0, tiled=True),
    )
    seq_count = segment_ids.shape[0]
    row_count = tokens.shape[0]
    head_shape = (seq_count, SEQ_LEN, H, DH)
    inputs = tokens.astype(jnp.float32)
    query_rows = (
        (matmul(tokens, full_query) + bias_query.astype(jnp.float32))
        .astype(jnp.bfloat16)
        .reshape(head_shape)
    )
    key_rows = matmul(tokens, full_key).astype(jnp.bfloat16).reshape(head_shape)
    value_rows = (
        (matmul(tokens, full_value) + bias_value.astype(jnp.float32))
        .astype(jnp.bfloat16)
        .reshape(head_shape)
    )
    mixed_heads, logsum = lax.map(attend_forward, (query_rows, key_rows, value_rows, segment_ids))
    mixed_heads = mixed_heads.reshape(row_count, H * DH)
    hidden = inputs + matmul(mixed_heads, full_out) + bias_out.astype(jnp.float32)
    normed_one, scale_one = norm_forward(hidden)
    first_out = normed_one * gain_one.astype(jnp.float32) + shift_one.astype(jnp.float32)
    first_low = first_out.astype(jnp.bfloat16)
    upward = matmul(first_low, full_up) + bias_up.astype(jnp.float32)
    active = jax.nn.gelu(upward, approximate=False).astype(jnp.bfloat16)
    second = matmul(active, full_down) + bias_down.astype(jnp.float32)
    normed_two, scale_two = norm_forward(first_out + second)
    output = (normed_two * gain_two.astype(jnp.float32) + shift_two.astype(jnp.float32)).astype(
        jnp.bfloat16
    )
    back_up, back_down, back_gain_two = (
        lax.all_gather(w_up, ("dp", "fsdp"), axis=0, tiled=True),
        lax.all_gather(w_down, ("dp", "fsdp"), axis=0, tiled=True),
        lax.all_gather(ln2_gain, ("dp", "fsdp"), axis=0, tiled=True),
    )
    grad_gain_two = jnp.sum(out_cotangent * normed_two, axis=0)
    grad_shift_two = jnp.sum(out_cotangent, axis=0)
    grad_sum_two = norm_backward(
        out_cotangent, normed_two, scale_two, back_gain_two.astype(jnp.float32)
    )
    grad_second = grad_sum_two.astype(jnp.bfloat16)
    grad_down = outer_sum(active, grad_second)
    grad_bias_down = column_sum(grad_second)
    grad_upward = (back_matmul(grad_second, back_down) * gelu_slope(upward)).astype(jnp.bfloat16)
    grad_up = outer_sum(first_low, grad_upward)
    grad_bias_up = column_sum(grad_upward)
    grad_first = grad_sum_two + back_matmul(grad_upward, back_up)
    mlp_shares = (
        lax.psum_scatter(grad_up, ("dp", "fsdp"), scatter_dimension=0, tiled=True),
        lax.psum_scatter(grad_bias_up, ("dp", "fsdp"), scatter_dimension=0, tiled=True),
        lax.psum_scatter(grad_down, ("dp", "fsdp"), scatter_dimension=0, tiled=True),
        lax.psum_scatter(grad_bias_down, ("dp", "fsdp"), scatter_dimension=0, tiled=True),
        lax.psum_scatter(grad_gain_two, ("dp", "fsdp"), scatter_dimension=0, tiled=True),
        lax.psum_scatter(grad_shift_two, ("dp", "fsdp"), scatter_dimension=0, tiled=True),
    )
    back_query, back_key, back_value, back_out, back_gain_one = (
        lax.all_gather(w_query, ("dp", "fsdp"), axis=0, tiled=True),
        lax.all_gather(w_key, ("dp", "fsdp"), axis=0, tiled=True),
        lax.all_gather(w_value, ("dp", "fsdp"), axis=0, tiled=True),
        lax.all_gather(w_out, ("dp", "fsdp"), axis=0, tiled=True),
        lax.all_gather(ln1_gain, ("dp", "fsdp"), axis=0, tiled=True),
    )
    grad_gain_one = jnp.sum(grad_first * normed_one, axis=0)
    grad_shift_one = jnp.sum(grad_first, axis=0)
    grad_hidden = norm_backward(
        grad_first, normed_one, scale_one, back_gain_one.astype(jnp.float32)
    )
    grad_branch = grad_hidden.astype(jnp.bfloat16)
    grad_weight_out = outer_sum(mixed_heads, grad_branch)
    grad_bias_out = column_sum(grad_branch)
    grad_mixed = back_matmul(grad_branch, back_out).astype(jnp.bfloat16).reshape(head_shape)
    grad_query, grad_key, grad_value = lax.map(
        attend_backward, (query_rows, key_rows, value_rows, segment_ids, logsum, grad_mixed)
    )
    grad_query = grad_query.reshape(row_count, D)
    grad_key = grad_key.reshape(row_count, D)
    grad_value = grad_value.reshape(row_count, D)
    grad_weight_query = outer_sum(tokens, grad_query)
    grad_bias_query = column_sum(grad_query)
    grad_weight_key = outer_sum(tokens, grad_key)
    grad_weight_value = outer_sum(tokens, grad_value)
    grad_bias_value = column_sum(grad_value)
    tokens_grad = (
        grad_hidden
        + back_matmul(grad_query, back_query)
        + back_matmul(grad_key, back_key)
        + back_matmul(grad_value, back_value)
    )
    tokens_grad = tokens_grad.astype(jnp.bfloat16)
    attn_shares = (
        lax.psum_scatter(grad_weight_query, ("dp", "fsdp"), scatter_dimension=0, tiled=True),
        lax.psum_scatter(grad_bias_query, ("dp", "fsdp"), scatter_dimension=0, tiled=True),
        lax.psum_scatter(grad_weight_key, ("dp", "fsdp"), scatter_dimension=0, tiled=True),
        lax.psum_scatter(grad_weight_value, ("dp", "fsdp"), scatter_dimension=0, tiled=True),
        lax.psum_scatter(grad_bias_value, ("dp", "fsdp"), scatter_dimension=0, tiled=True),
        lax.psum_scatter(grad_weight_out, ("dp", "fsdp"), scatter_dimension=0, tiled=True),
        lax.psum_scatter(grad_bias_out, ("dp", "fsdp"), scatter_dimension=0, tiled=True),
        lax.psum_scatter(grad_gain_one, ("dp", "fsdp"), scatter_dimension=0, tiled=True),
        lax.psum_scatter(grad_shift_one, ("dp", "fsdp"), scatter_dimension=0, tiled=True),
    )
    shares = attn_shares + mlp_shares
    return (
        output,
        tokens_grad,
        shares[0],
        shares[1],
        shares[2],
        shares[3],
        shares[4],
        shares[5],
        shares[6],
        shares[7],
        shares[8],
        shares[9],
        shares[10],
        shares[11],
        shares[12],
        shares[13],
        shares[14],
    )


def solution(mesh):
    in_specs = (
        P(("dp", "fsdp"), None),
        P(("dp", "fsdp"), None),
        P(("dp", "fsdp"), None),
        P(("dp", "fsdp")),
        P(("dp", "fsdp"), None),
        P(("dp", "fsdp"), None),
        P(("dp", "fsdp")),
        P(("dp", "fsdp"), None),
        P(("dp", "fsdp")),
        P(("dp", "fsdp")),
        P(("dp", "fsdp")),
        P(("dp", "fsdp"), None),
        P(("dp", "fsdp")),
        P(("dp", "fsdp"), None),
        P(("dp", "fsdp")),
        P(("dp", "fsdp")),
        P(("dp", "fsdp")),
        P(("dp", "fsdp"), None),
    )
    out_specs = (
        P(("dp", "fsdp"), None),
        P(("dp", "fsdp"), None),
        P(("dp", "fsdp"), None),
        P(("dp", "fsdp")),
        P(("dp", "fsdp"), None),
        P(("dp", "fsdp"), None),
        P(("dp", "fsdp")),
        P(("dp", "fsdp"), None),
        P(("dp", "fsdp")),
        P(("dp", "fsdp")),
        P(("dp", "fsdp")),
        P(("dp", "fsdp"), None),
        P(("dp", "fsdp")),
        P(("dp", "fsdp"), None),
        P(("dp", "fsdp")),
        P(("dp", "fsdp")),
        P(("dp", "fsdp")),
    )
    return jax.shard_map(
        per_device, mesh=mesh, in_specs=in_specs, out_specs=out_specs, check_vma=False
    )
```

profile of v0, /device:TPU:0, one launch (start us, length us, event | category | flops | bytes accessed | tf_op | source)
XLA Modules:
  0.0 1786.5 jit_solution(15668524781311327682)
XLA Ops:
  18.0 42.3 %all-reduce.18 = (bf16[1024]{0:T(1024)(128)(2,1)S(1)}, bf16[1024]{0:T(1024)(128)(2,1)S(1)}, bf16[1024]{0:T(1024)(128)(2,1)S(1)}, bf16[1024]{0:T(1024)(128)(2,1)S...) all-reduce(bf16[1024]{0:T(1024)(128)(2,1)S(1)} %dynamic-update-slic, ...), channel_id=1, replica_groups=mesh['dp'=4,'fsdp'=8] {'dp','fsdp'}, use_global_device_ids=true, to_apply=%add.2 | all-reduce | flops 8192 | bytes 32768
  66.0 65.7 %all-gather = bf16[32,1,128]{2,1,0:T(2,128)(2,1)S(1)} all-gather(bf16[1,1,128]{2,1,0:T(2,128)(2,1)S(1)} %bitcast.177), channel_id=1, replica_groups=mesh['dp'=4,'fsdp'=8] {'dp','fsdp'}, dimensions={0}, use_global_device_ids=true | all-gather | bytes 8448 | tf_op jit(solution)/shard_map/all_gather | solution.py:150
  167.6 19.7 %all-gather.12.cloned.1.call-done = bf16[1024,1024]{1,0:T(8,128)(2,1)} async-done(((bf16[32,1024]{1,0:T(8,128)(2,1)}), bf16[1024,1024]{1,0:T(8,128)(2,1)}) %all-gather.12.cloned.1.call-update) | async-done | bytes 2097168 | tf_op jit(solution)/shard_map/all_gather | solution.py:138
  200.4 60.0 %while.26 = (s32[]{:T(128)}, bf16[2,512,1024]{2,1,0:T(8,128)(2,1)}, f32[2,16,512]{2,1,0:T(8,128)S(1)}, bf16[2,512,16,64]{1,3,2,0:T(8,128)(2,1)}, s32[2,512]{1,0:...) while((s32[]{:T(128)}, bf16[2,512,1024]{2,1,0:T(8,128)(2,1)}, ...), condition=%wide.region_3.4_spmd, body=%wide.region_0.3_spmd.sunk | while | flops 1124851712 | bytes 60039260 | solution.py:170
  209.6 9.2 fusion.133
  218.8 9.3 fusion.134
  230.9 8.5 fusion.132
  239.3 9.3 fusion.133
  248.6 9.2 fusion.134
  269.6 55.1 %all-gather.16.cloned.1.call-done = bf16[1024,4096]{1,0:T(8,128)(2,1)} async-done(((bf16[32,4096]{1,0:T(8,128)(2,1)}), bf16[1024,4096]{1,0:T(8,128)(2,1)}) %all-gather.16.cloned.1.call-update) | async-done | bytes 8388624 | tf_op jit(solution)/shard_map/all_gather | solution.py:148
  324.7 47.5 %fusion.52 = (bf16[1024,4096]{1,0:T(8,128)(2,1)}, f32[1024,4096]{1,0:T(8,128)}) fusion(f32[4096]{0:T(1024)S(1)} %bitcast.175, bf16[1024,4096]{1,0:T(8,128)(2,1)} %all-gather.16.cloned.1.call-done, bf16[1024,1024]{0,1:T(8,128)(2,1)S(1)} %fusion.76.clone.4), kind=kOutput, calls=%fused_computation.63 | convolution fusion | flops 8866758656 | bytes 35667968 | tf_op jit(solution)/shard_map/dot_general | solution.py:13
  372.2 31.4 %all-gather.18.cloned.1.call-done = bf16[4096,1024]{1,0:T(8,128)(2,1)} async-done(((bf16[128,1024]{1,0:T(8,128)(2,1)}), bf16[4096,1024]{1,0:T(8,128)(2,1)}) %all-gather.18.cloned.1.call-update) | async-done | bytes 8388624 | tf_op jit(solution)/shard_map/all_gather | solution.py:149
  403.6 14.9 fusion.78
  427.0 21.2 %convert_reduce_fusion = (f32[4096]{0:T(1024)}, bf16[1024,4096]{1,0:T(8,128)(2,1)}) fusion(f32[1024,4096]{1,0:T(8,128)} %get-tuple-element.286, f32[4096]{0:T(1024)S(1)} %bitcast.176, bf16[4096,1024]{1,0:T(8,128)(2,1)} %all-gather.18.cloned.1.call-done, f32[1024,1024]{0,1:T(8,128)S(1)} %get-tuple-element.275), kind=kOutput, calls=%fused_computation.70 | convolution fusion | flops 8645505024 | bytes 37781504 | tf_op jit(solution)/shard_map/dot_general | solution.py:17
  448.2 13.7 multiply_reduce_fusion.2
  485.2 98.5 %while.27 = (s32[]{:T(128)}, bf16[2,512,16,64]{1,3,2,0:T(8,128)(2,1)}, bf16[2,512,16,64]{1,3,2,0:T(8,128)(2,1)}, bf16[2,512,16,64]{1,3,2,0:T(8,128)(2,1)}, bf16[...) while((s32[]{:T(128)}, ...), condition=%wide.region_14.15_spmd, body=%wide.region_12.14_spmd.sunk | while | flops 2724978688 | bytes 187346224 | solution.py:224
  485.4 9.8 fusion.143
  495.4 12.1 multiply_reduce_fusion.10
  507.6 11.8 multiply_convert_fusion.4
  524.9 9.5 fusion.146
  534.4 9.8 fusion.143
  544.5 12.0 multiply_reduce_fusion.10
  556.5 11.9 multiply_convert_fusion.4
  573.9 9.6 fusion.146
  631.1 16.7 fusion.73
  648.4 16.6 fusion.70
  670.3 42.5 %all-reduce.17 = (f32[1024]{0:T(1024)S(1)}, f32[1024]{0:T(1024)S(1)}, f32[1024]{0:T(1024)S(1)}, f32[1024]{0:T(1024)S(1)}, f32[1024]{0:T(1024)S(1)}, /*index=5*/f...) all-reduce(f32[1024]{0:T(1024)S(1)} %reduce_sum.184, ...), channel_id=3, replica_groups=mesh['dp'=4,'fsdp'=8] {'dp','fsdp'}, use_global_device_ids=true, to_apply=%region_17.18.clone | all-reduce | flops 12288 | bytes 98304
  736.7 36.2 %reduce-scatter.19.cloned.1.call-done = f32[32,1024]{1,0:T(8,128)} async-done(((f32[1024,1024]{1,0:T(8,128)}), f32[32,1024]{1,0:T(8,128)}) %reduce-scatter.19.cloned.1.call-update) | async-done | bytes 131088
  772.8 143.6 %reduce-scatter.21.cloned.1.call-done = f32[32,1024]{1,0:T(8,128)} async-done(((f32[1024,1024]{1,0:T(8,128)}), f32[32,1024]{1,0:T(8,128)}) %reduce-scatter.21.cloned.1.call-update) | async-done | bytes 131088
  916.5 144.4 %reduce-scatter.23.cloned.1.call-done = f32[32,1024]{1,0:T(8,128)} async-done(((f32[1024,1024]{1,0:T(8,128)}), f32[32,1024]{1,0:T(8,128)}) %reduce-scatter.23.cloned.1.call-update) | async-done | bytes 131088
  1060.9 358.5 %reduce-scatter.15.cloned.1.call-done = f32[32,4096]{1,0:T(8,128)} async-done(((f32[1024,4096]{1,0:T(8,128)}), f32[32,4096]{1,0:T(8,128)}) %reduce-scatter.15.cloned.1.call-update) | async-done | bytes 524304 | tf_op jit(solution)/shard_map/reduce_scatter | solution.py:201
  1419.4 360.1 %reduce-scatter.17.cloned.1.call-done = f32[128,1024]{1,0:T(8,128)} async-done(((f32[4096,1024]{1,0:T(8,128)}), f32[128,1024]{1,0:T(8,128)}) %reduce-scatter.17.cloned.1.call-update) | async-done | bytes 524304 | tf_op jit(solution)/shard_map/reduce_scatter | solution.py:203
  (254 shorter events, 208.3 us)
Async XLA Ops:
  7.2 58.9 %copy-start.45 = (bf16[128]{0:T(256)(128)(2,1)S(1)}, bf16[128]{0:T(256)(128)(2,1)}, u32[]{:S(2)}) copy-start(bf16[128]{0:T(256)(128)(2,1)} %param.34) | copy-start | bytes 772
  7.2 132.3 %all-gather.10.cloned.1.call-start = ((), (), s32[]{:S(2)}) async-start(), calls=%async_computation.7 | async-start | bytes 2162688 | tf_op jit(solution)/shard_map/all_gather | solution.py:137
  7.9 145.6 %all-gather.8.cloned.1.call-start = ((), (), s32[]{:S(2)}) async-start(), calls=%async_computation.6 | async-start | bytes 2162688 | tf_op jit(solution)/shard_map/all_gather | solution.py:139
  8.7 178.6 %all-gather.12.cloned.1.call-start = ((), (), s32[]{:S(2)}) async-start(), calls=%async_computation.8 | async-start | bytes 2162688 | tf_op jit(solution)/shard_map/all_gather | solution.py:138
  9.4 251.0 %all-gather.14.cloned.1.call-start = ((), (), s32[]{:S(2)}) async-start(), calls=%async_computation.9 | async-start | bytes 2162688 | tf_op jit(solution)/shard_map/all_gather | solution.py:140
  10.0 314.7 %all-gather.16.cloned.1.call-start = ((), (), s32[]{:S(2)}) async-start(), calls=%async_computation.10 | async-start | bytes 8650752 | tf_op jit(solution)/shard_map/all_gather | solution.py:148
  10.6 393.0 %all-gather.18.cloned.1.call-start = ((), (), s32[]{:S(2)}) async-start(), calls=%async_computation.11 | async-start | bytes 8650752 | tf_op jit(solution)/shard_map/all_gather | solution.py:149
  11.2 725.5 %reduce-scatter.13.cloned.1.call-start = ((), (), s32[]{:S(2)}) async-start(), calls=%async_computation.12 | async-start | bytes 4325376 | tf_op jit(solution)/shard_map/reduce_scatter | solution.py:248
  200.4 60.0 %copy-start.44 = (f32[1024]{0:T(1024)S(1)}, f32[1024]{0:T(1024)}, u32[]{:S(2)}) copy-start(f32[1024]{0:T(1024)} %convert_element_type.121) | copy-start | bytes 12292
  260.4 6.5 copy-start
  260.4 6.5 copy-start.22
  266.9 194.9 %copy-start.26 = (f32[1024]{0:T(1024)}, f32[1024]{0:T(1024)S(1)}, u32[]{:S(2)}) copy-start(f32[1024]{0:T(1024)S(1)} %broadcast_multiply_fusion.5) | copy-start | bytes 12292
  267.4 57.3 %copy-start.40 = (f32[32,1,128]{2,1,0:T(1,128)S(1)}, f32[32,1,128]{2,1,0:T(1,128)}, u32[]{:S(2)}) copy-start(f32[32,1,128]{2,1,0:T(1,128)} %convert_element_type.141) | copy-start | bytes 49156
  269.0 192.9 %copy-start.31 = (f32[1024]{0:T(1024)}, f32[1024]{0:T(1024)S(1)}, u32[]{:S(2)}) copy-start(f32[1024]{0:T(1024)S(1)} %add_rsqrt_fusion.1) | copy-start | bytes 12292
  324.7 78.9 %copy-start.43 = (f32[1024]{0:T(1024)S(1)}, f32[1024]{0:T(1024)}, u32[]{:S(2)}) copy-start(f32[1024]{0:T(1024)} %convert_element_type.127) | copy-start | bytes 12292
  423.2 25.0 %slice-start = ((s8[8388608]{0:T(1024)(128)(4,1)}), s8[4194304]{0:T(1024)(128)(4,1)S(1)}, s32[]{:S(2)}) async-start(s8[8388608]{0:T(1024)(128)(4,1)} %bitcast.178), calls=%async_computation.18 | async-start | bytes 8388608
  427.0 21.2 %copy-start.11 = (f32[1024,1024]{0,1:T(8,128)}, f32[1024,1024]{0,1:T(8,128)S(1)}, u32[]{:S(2)}) copy-start(f32[1024,1024]{0,1:T(8,128)S(1)} %get-tuple-element.275) | copy-start | bytes 12582916
  427.0 21.2 %copy-start.6 = (f32[1024,1024]{0,1:T(8,128)S(1)}, f32[1024,1024]{0,1:T(8,128)}, u32[]{:S(2)}) copy-start(f32[1024,1024]{0,1:T(8,128)} %copy-done.5) | copy-start | bytes 12582916
  427.0 21.2 %slice-start.1 = ((s8[8388608]{0:T(1024)(128)(4,1)}), s8[4194304]{0:T(1024)(128)(4,1)S(1)}, s32[]{:S(2)}) async-start(s8[8388608]{0:T(1024)(128)(4,1)} %bitcast.178), calls=%async_computation.19 | async-start | bytes 8388608
  479.5 5.7 copy-start.1
  479.5 5.7 copy-start.23
  479.5 5.7 copy-start.25
  485.1 287.7 %reduce-scatter.19.cloned.1.call-start = ((), (), s32[]{:S(2)}) async-start(), calls=%async_computation.15 | async-start | bytes 4325376
  485.4 10.1 copy-start.2
  507.5 11.9 copy-start.15
  534.4 10.1 copy-start.2
  556.5 11.9 copy-start.15
  583.7 5.8 copy-start.14
  599.2 317.2 %reduce-scatter.21.cloned.1.call-start = ((), (), s32[]{:S(2)}) async-start(), calls=%async_computation.16 | async-start | bytes 4325376
  614.7 446.1 %reduce-scatter.23.cloned.1.call-start = ((), (), s32[]{:S(2)}) async-start(), calls=%async_computation.17 | async-start | bytes 4325376
  630.4 788.9 %reduce-scatter.15.cloned.1.call-start = ((), (), s32[]{:S(2)}) async-start(), calls=%async_computation.13 | async-start | bytes 17301504 | tf_op jit(solution)/shard_map/reduce_scatter | solution.py:201
  647.9 1131.6 %reduce-scatter.17.cloned.1.call-start = ((), (), s32[]{:S(2)}) async-start(), calls=%async_computation.14 | async-start | bytes 17301504 | tf_op jit(solution)/shard_map/reduce_scatter | solution.py:203
  (37 other events, 103.5 us)
Sparse Core Ops, SparseCore 0:
  11.0 59.4 all-gather.9
  73.4 55.4 all-gather.7
  131.9 55.3 all-gather.11
  190.1 55.3 all-gather.13
  248.4 76.2 all-gather.15
  327.5 76.0 all-gather.17
  485.2 142.5 reduce-scatter.12
  630.6 142.1 reduce-scatter.18
  775.7 140.7 reduce-scatter.20
  919.1 141.6 reduce-scatter.22
  1063.7 355.5 reduce-scatter.14
  1422.1 357.3 reduce-scatter.16
where the time goes:
time: 1790 us
  waiting for transfers between devices  1150 us (64%)
  matrix products  290 us (16%)
  blocking collectives  151 us (8%)
  local copies, waits for them, and re-layouts  113 us (6%)
  other arithmetic  62.1 us (3%)
    reduce_scatter x1, waiting for transfers between devices, per_device(): lax.psum_scatter(grad_down, ('dp', 'fsdp'), scatter_dimension=0, tiled=True)  360 us
    reduce_scatter x1, waiting for transfers between devices, per_device(): lax.psum_scatter(grad_up, ('dp', 'fsdp'), scatter_dimension=0, tiled=True)  358 us
    unnamed x15, waiting for transfers between devices  328 us
    unnamed x2, blocking collectives  84.8 us
    dot_general x6, matrix products, matmul(): return jnp.dot(operand, other, preferred_element_type=jnp.float32)  82.5 us
    all_gather x1, blocking collectives, per_device(): lax.all_gather(b_up, ('dp', 'fsdp'), axis=0, tiled=True)  65.7 us
    unnamed x125, local copies, waits for them, and re-layouts  56.9 us
    all_gather x1, waiting for transfers between devices, per_device(): lax.all_gather(w_up, ('dp', 'fsdp'), axis=0, tiled=True)  55.1 us
  transfers between devices with their start and end apart: 12, of which 8 were waited for; matrix products, arithmetic and copies ran while one was open for 21% of the time, Pallas kernels for 0%

commit v1 on v0

v1 whole, which is shorter than its diff:
```python
import functools

import jax
import jax.numpy as jnp
from jax import lax
from jax.experimental import pallas as pl
from jax.experimental.pallas import tpu as pltpu
from jax.sharding import PartitionSpec as P

D = 1024
H = 16
DH = 64
SEQ_LEN = 512
AXES = ("dp", "fsdp")
CORES = 2


def matmul(operand, other):
    return jnp.dot(operand, other, preferred_element_type=jnp.float32)


def back_matmul(operand, other):
    return lax.dot_general(
        operand, other, (((1,), (1,)), ((), ())), preferred_element_type=jnp.float32
    )


def outer_sum(operand, other):
    return lax.dot_general(
        operand, other, (((0,), (0,)), ((), ())), preferred_element_type=jnp.float32
    )


def column_sum(values):
    return jnp.sum(values.astype(jnp.float32), axis=0)


def norm_forward(hidden):
    centred = hidden - jnp.mean(hidden, axis=-1, keepdims=True)
    scale_row = lax.rsqrt(jnp.mean(centred * centred, axis=-1, keepdims=True) + 1e-12)
    return (centred * scale_row, scale_row)


def norm_backward(grad_out, normed, scale_row, scaling):
    scaled = grad_out * scaling
    return scale_row * (
        scaled
        - jnp.mean(scaled, axis=-1, keepdims=True)
        - normed * jnp.mean(scaled * normed, axis=-1, keepdims=True)
    )


def gelu_slope(values):
    return (
        0.5 * (1.0 + lax.erf(values * 0.7071067811865476))
        + values * jnp.exp(-0.5 * values * values) * 0.3989422804014327
    )


def masked_scores(query_rows, key_rows, doc_ids):
    scores = (
        jnp.einsum("qhd,khd->hqk", query_rows, key_rows, preferred_element_type=jnp.float32) * 0.125
    )
    same_doc = doc_ids[:, None] == doc_ids[None, :]
    return jnp.where(same_doc[None], scores, -1000000000.0)


def attend_forward(pieces):
    query_rows, key_rows, value_rows, doc_ids = pieces
    scores = masked_scores(query_rows, key_rows, doc_ids)
    row_peak = jnp.max(scores, axis=-1, keepdims=True)
    powers = jnp.exp(scores - row_peak)
    row_total = jnp.sum(powers, axis=-1, keepdims=True)
    probability = (powers / row_total).astype(jnp.bfloat16)
    mixed_heads = jnp.einsum(
        "hqk,khd->qhd", probability, value_rows, preferred_element_type=jnp.float32
    )
    logsum = (row_peak + jnp.log(row_total))[:, :, 0]
    return (mixed_heads.astype(jnp.bfloat16).reshape(mixed_heads.shape[0], H * DH), logsum)


def attend_backward(pieces):
    query_rows, key_rows, value_rows, doc_ids, logsum, grad_heads = pieces
    scores = masked_scores(query_rows, key_rows, doc_ids)
    probability = jnp.exp(scores - logsum[:, :, None])
    grad_prob = jnp.einsum(
        "qhd,khd->hqk", grad_heads, value_rows, preferred_element_type=jnp.float32
    )
    row_delta = jnp.sum(probability * grad_prob, axis=-1, keepdims=True)
    grad_scores = (probability * (grad_prob - row_delta)).astype(jnp.bfloat16)
    grad_query = (
        jnp.einsum("hqk,khd->qhd", grad_scores, key_rows, preferred_element_type=jnp.float32)
        * 0.125
    )
    grad_key = (
        jnp.einsum("hqk,qhd->khd", grad_scores, query_rows, preferred_element_type=jnp.float32)
        * 0.125
    )
    grad_value = jnp.einsum(
        "hqk,qhd->khd",
        probability.astype(jnp.bfloat16),
        grad_heads,
        preferred_element_type=jnp.float32,
    )
    return (
        grad_query.astype(jnp.bfloat16),
        grad_key.astype(jnp.bfloat16),
        grad_value.astype(jnp.bfloat16),
    )


class Grid:
    def __init__(self, mesh):
        self.shape = dict(mesh.shape)
        self.xs = self.shape["dp"] // CORES
        self.ys = self.xs
        self.zs = self.shape["fsdp"] // self.ys
        self.sizes = {"x": self.xs, "c": CORES, "z": self.zs, "y": self.ys}
        self.count = self.shape["dp"] * self.shape["fsdp"]
        self.pairs = self.xs == 2 and self.ys == 2

    def at(self):
        dp, fsdp = lax.axis_index("dp"), lax.axis_index("fsdp")
        return {"x": dp // CORES, "c": dp % CORES, "z": fsdp // self.ys, "y": fsdp % self.ys}

    def shifted(self, axis, step, wrap):
        hops = []
        for x in range(self.xs):
            for c in range(CORES):
                for z in range(self.zs):
                    for y in range(self.ys):
                        to = {"x": x, "c": c, "z": z, "y": y}
                        to[axis] += step
                        if wrap:
                            to[axis] %= self.sizes[axis]
                        elif not 0 <= to[axis] < self.sizes[axis]:
                            continue
                        hops.append((self.number(x, c, z, y), self.number(**to)))
        return hops

    def number(self, x, c, z, y):
        return ((x * CORES + c) * self.zs + z) * self.ys + y

    def swap(self, values, axis):
        return lax.ppermute(values, AXES, self.shifted(axis, 1, True))

    def along(self, values, axis, step):
        return lax.ppermute(values, AXES, self.shifted(axis, step, False))


def line_gather(grid, at, shard):
    up, down = [shard], [shard]
    for _ in range(grid.zs - 1):
        up.append(grid.along(up[-1], "z", 1))
        down.append(grid.along(down[-1], "z", -1))
    line = jnp.stack(up[:0:-1] + [shard] + down[1:])
    return lax.dynamic_slice_in_dim(line, grid.zs - 1 - at["z"], grid.zs, 0)


def pair_gather(grid, block, first, second):
    near = grid.swap(block, first)
    pieces = {(0, 0): block, (1, 0): near}
    pieces[(0, 1)] = grid.swap(block, second)
    pieces[(1, 1)] = grid.swap(near, second)
    found = {}
    for (one, two), piece in pieces.items():
        flips = {first: one, second: two}
        found[(flips["x"], 0, flips["y"])] = piece
        found[(flips["x"], 1, flips["y"])] = grid.swap(piece, "c")
    return found


def assemble_kernel(plan, grid, count, outs, spot, *refs):
    pieces, whole, sem = refs[:count], refs[count : count + outs], refs[-1]
    copies = []
    for source, (flip, out, rows, columns, start) in enumerate_plan(plan):
        x, c, y = ((spot[i] + flip[i]) % 2 for i in range(3))
        copies.append(
            pltpu.make_async_copy(
                pieces[source].at[:, pl.ds(start, rows), :],
                whole[out].at[x, c, :, y, :, pl.ds(columns[0], columns[1])],
                sem.at[len(copies)],
            )
        )
    for copy in copies:
        copy.start()
    for copy in copies:
        copy.wait()


def enumerate_plan(plan):
    for source, (flip, targets) in enumerate(plan):
        for out, rows, columns, start in targets:
            yield source, (flip, out, rows, columns, start)


def assemble(grid, at, parts, shapes):
    plan, arrays = [], []
    for pieces, targets in parts:
        for flip, piece in pieces.items():
            plan.append((flip, targets))
            arrays.append(piece)
    copies = sum(len(targets) for _, targets in plan)
    spot = jnp.stack([at["x"], at["c"], at["y"]]).astype(jnp.int32)
    outs = [
        jax.ShapeDtypeStruct((grid.xs, CORES, grid.zs, grid.ys) + shape, jnp.bfloat16)
        for shape in shapes
    ]
    size = sum(2 * piece.size for piece in arrays)
    whole = pl.pallas_call(
        functools.partial(assemble_kernel, plan, grid, len(arrays), len(outs)),
        out_shape=outs,
        in_specs=[pl.BlockSpec(memory_space=pltpu.SMEM)]
        + [pl.BlockSpec(memory_space=pl.ANY)] * len(arrays),
        out_specs=[pl.BlockSpec(memory_space=pl.ANY)] * len(outs),
        scratch_shapes=[pltpu.SemaphoreType.DMA((copies,))],
        cost_estimate=pl.CostEstimate(flops=0, bytes_accessed=2 * size, transcendentals=0),
        compiler_params=pltpu.CompilerParams(vmem_limit_bytes=1 << 20),
    )(spot, *arrays)
    return [w.reshape(grid.count * s[0], s[1]) for w, s in zip(whole, shapes)]


def take(values, index, axis):
    return lax.dynamic_index_in_dim(values, index, axis, keepdims=False)


def total(terms):
    result = terms[0].astype(jnp.float32)
    for term in terms[1:]:
        result = result + term.astype(jnp.float32)
    return result


def swap_reduce(grid, at, terms, name, axis):
    sent = total([take(term, 1 - at[name], axis) for term in terms]).astype(terms[0].dtype)
    got = grid.swap(sent, name)
    return [take(term, at[name], axis) for term in terms] + [got]


def line_reduce(grid, at, terms):
    size, kind = grid.zs, terms[0].dtype

    def own(index):
        index = jnp.clip(index, 0, size - 1)
        return total([take(term, index, 0) for term in terms])

    up = down = None
    for step in range(1, size):
        up_sum, down_sum = own(at["z"] + size - step), own(at["z"] - size + step)
        if step > 1:
            up_sum, down_sum = up_sum + up.astype(jnp.float32), down_sum + down.astype(jnp.float32)
        up = grid.along(up_sum.astype(kind), "z", 1)
        down = grid.along(down_sum.astype(kind), "z", -1)
    return own(at["z"]) + up.astype(jnp.float32) + down.astype(jnp.float32)


def chip_reduce(grid, at, terms, order):
    if order == "xy":
        terms = swap_reduce(grid, at, terms, "x", 0)
        terms = swap_reduce(grid, at, terms, "y", 1)
    else:
        terms = swap_reduce(grid, at, terms, "y", 2)
        terms = swap_reduce(grid, at, terms, "x", 0)
    return line_reduce(grid, at, terms)


def product_reduce(grid, at, left, right, cuts):
    rows = left.shape[1] // grid.count
    split = left.reshape(left.shape[0], grid.xs, CORES, -1)

    def half(core):
        part = take(split, core, 2).reshape(left.shape[0], -1)
        return outer_sum(part, right).astype(jnp.bfloat16)

    sent, kept = half(1 - at["c"]), half(at["c"])
    got = grid.swap(sent, "c")
    shape = (grid.xs, grid.zs, grid.ys, rows)
    results, start = [], 0
    for width, order in cuts:
        terms = [
            part[:, start : start + width].reshape(shape + (width,)) for part in (kept, got)
        ]
        results.append(chip_reduce(grid, at, terms, order))
        start += width
    return jnp.concatenate(results, axis=1) if len(results) > 1 else results[0]


def small_reduce(grid, at, vectors):
    packed = jnp.concatenate([v.reshape(grid.count, -1) for v in vectors], axis=1)
    width = packed.shape[1]
    lines = -(-width // 128)
    packed = jnp.pad(packed, ((0, 0), (0, lines * 128 - width)))
    packed = packed.reshape(grid.xs, CORES, grid.zs, grid.ys, lines, 128)
    terms = swap_reduce(grid, at, [packed], "c", 1)
    flat = chip_reduce(grid, at, terms, "xy").reshape(-1)
    results, start = [], 0
    for vector in vectors:
        size = vector.size // grid.count
        results.append(flat[start : start + size])
        start += size
    return results


def gather_weights(grid, at, attn, smalls, w_out, w_up, w_down):
    rows = attn[0].shape[0]
    widths = [small.shape[0] for small in smalls]
    if not grid.pairs:
        whole = [lax.all_gather(w, AXES, axis=0, tiled=True) for w in (*attn, w_out, w_up, w_down)]
        small = lax.all_gather(jnp.concatenate(smalls), AXES, axis=0, tiled=True)
        small = small.reshape(grid.count, -1)
        return jnp.concatenate(whole[:3], axis=1), split_small(small, widths), *whole[3:]
    packed = jnp.pad(jnp.concatenate(smalls), (0, rows * 128 - sum(widths))).reshape(rows, 128)
    first = line_gather(grid, at, jnp.concatenate([*attn, packed], axis=1))
    columns = first.shape[2]
    cut = (columns // 256) * 128
    left = pair_gather(grid, first[:, :, :cut], "y", "x")
    right = pair_gather(grid, first[:, :, cut:], "x", "y")
    (wide,) = assemble(
        grid,
        at,
        [(left, [(0, rows, (0, cut), 0)]), (right, [(0, rows, (cut, columns - cut), 0)])],
        [(rows, columns)],
    )
    small = wide[:, 3 * D :].reshape(grid.count, -1)
    second = line_gather(grid, at, jnp.concatenate([w_out, w_down], axis=0))
    third = line_gather(grid, at, w_up)
    second = pair_gather(grid, second, "y", "x")
    third = pair_gather(grid, third, "x", "y")
    lower = w_down.shape[0]
    (full_up,) = assemble(
        grid, at, [(third, [(0, rows, (0, w_up.shape[1]), 0)])], [(rows, w_up.shape[1])]
    )
    full_out, full_down = assemble(
        grid,
        at,
        [(second, [(0, rows, (0, D), 0), (1, lower, (0, D), rows)])],
        [(rows, D), (lower, D)],
    )
    return wide[:, : 3 * D], split_small(small, widths), full_out, full_up, full_down


def split_small(small, widths):
    results, start = [], 0
    for width in widths:
        results.append(small[:, start : start + width].reshape(-1).astype(jnp.float32))
        start += width
    return results


def reduce_product(grid, at, left, right, cuts):
    if grid.pairs:
        return product_reduce(grid, at, left, right, cuts)
    return lax.psum_scatter(outer_sum(left, right), AXES, scatter_dimension=0, tiled=True)


def per_device(
    grid,
    tokens,
    segment_ids,
    w_query,
    b_query,
    w_key,
    w_value,
    b_value,
    w_out,
    b_out,
    ln1_gain,
    ln1_bias,
    w_up,
    b_up,
    w_down,
    b_down,
    ln2_gain,
    ln2_bias,
    out_cotangent,
):
    at = grid.at()
    full_qkv, smalls, full_out, full_up, full_down = gather_weights(
        grid,
        at,
        (w_query, w_key, w_value),
        (b_query, b_value, b_out, ln1_gain, ln1_bias, b_up, b_down, ln2_gain, ln2_bias),
        w_out,
        w_up,
        w_down,
    )
    bias_query, bias_value, bias_out, gain_one, shift_one = smalls[:5]
    bias_up, bias_down, gain_two, shift_two = smalls[5:]
    seq_count = segment_ids.shape[0]
    row_count = tokens.shape[0]
    head_shape = (seq_count, SEQ_LEN, H, DH)
    inputs = tokens.astype(jnp.float32)
    bias_qkv = jnp.concatenate([bias_query, jnp.zeros_like(bias_query), bias_value])
    qkv = (matmul(tokens, full_qkv) + bias_qkv).astype(jnp.bfloat16)
    query_rows, key_rows, value_rows = (
        qkv[:, i * D : (i + 1) * D].reshape(head_shape) for i in range(3)
    )
    mixed_heads, logsum = lax.map(attend_forward, (query_rows, key_rows, value_rows, segment_ids))
    mixed_heads = mixed_heads.reshape(row_count, H * DH)
    hidden = inputs + matmul(mixed_heads, full_out) + bias_out
    normed_one, scale_one = norm_forward(hidden)
    first_out = normed_one * gain_one + shift_one
    first_low = first_out.astype(jnp.bfloat16)
    upward = matmul(first_low, full_up) + bias_up
    active = jax.nn.gelu(upward, approximate=False).astype(jnp.bfloat16)
    second = matmul(active, full_down) + bias_down
    normed_two, scale_two = norm_forward(first_out + second)
    output = (normed_two * gain_two + shift_two).astype(jnp.bfloat16)
    grad_gain_two = jnp.sum(out_cotangent * normed_two, axis=0)
    grad_shift_two = jnp.sum(out_cotangent, axis=0)
    grad_sum_two = norm_backward(out_cotangent, normed_two, scale_two, gain_two)
    grad_second = grad_sum_two.astype(jnp.bfloat16)
    share_down = reduce_product(grid, at, active, grad_second, [(D, "xy")])
    grad_bias_down = column_sum(grad_second)
    grad_upward = (back_matmul(grad_second, full_down) * gelu_slope(upward)).astype(jnp.bfloat16)
    share_up = reduce_product(grid, at, first_low, grad_upward, [(grad_upward.shape[1], "yx")])
    grad_bias_up = column_sum(grad_upward)
    grad_first = grad_sum_two + back_matmul(grad_upward, full_up)
    grad_gain_one = jnp.sum(grad_first * normed_one, axis=0)
    grad_shift_one = jnp.sum(grad_first, axis=0)
    grad_hidden = norm_backward(grad_first, normed_one, scale_one, gain_one)
    grad_branch = grad_hidden.astype(jnp.bfloat16)
    share_out = reduce_product(grid, at, mixed_heads, grad_branch, [(D, "xy")])
    grad_bias_out = column_sum(grad_branch)
    grad_mixed = back_matmul(grad_branch, full_out).astype(jnp.bfloat16).reshape(head_shape)
    grads = lax.map(
        attend_backward, (query_rows, key_rows, value_rows, segment_ids, logsum, grad_mixed)
    )
    grad_qkv = jnp.concatenate([grad.reshape(row_count, D) for grad in grads], axis=1)
    share_qkv = reduce_product(grid, at, tokens, grad_qkv, [(D * 3 // 2, "xy"), (D * 3 // 2, "yx")])
    tokens_grad = (grad_hidden + back_matmul(grad_qkv, full_qkv)).astype(jnp.bfloat16)
    grad_bias_qkv = column_sum(grad_qkv)
    vectors = [
        grad_bias_qkv[:D],
        grad_bias_qkv[2 * D :],
        grad_bias_out,
        grad_gain_one,
        grad_shift_one,
        grad_bias_up,
        grad_bias_down,
        grad_gain_two,
        grad_shift_two,
    ]
    if grid.pairs:
        shares = small_reduce(grid, at, vectors)
    else:
        shares = [lax.psum_scatter(v, AXES, scatter_dimension=0, tiled=True) for v in vectors]
    return (
        output,
        tokens_grad,
        share_qkv[:, :D],
        shares[0],
        share_qkv[:, D : 2 * D],
        share_qkv[:, 2 * D :],
        shares[1],
        share_out,
        *shares[2:5],
        share_up,
        shares[5],
        share_down,
        *shares[6:],
    )


def solution(mesh):
    rows, flat = P(AXES, None), P(AXES)
    in_specs = (rows,) * 3 + (flat, rows, rows, flat, rows, flat, flat, flat, rows, flat, rows)
    in_specs += (flat,) * 3 + (rows,)
    out_specs = (rows,) * 3 + (flat, rows, rows, flat, rows, flat, flat, flat, rows, flat, rows)
    out_specs += (flat,) * 3
    return jax.shard_map(
        functools.partial(per_device, Grid(mesh)),
        mesh=mesh,
        in_specs=in_specs,
        out_specs=out_specs,
        check_vma=False,
    )
```

time: 1790 us -> 918 us (0.51)
  waiting for transfers between devices: 1150 us -> 119 us
  starting transfers between devices: 1.19 us -> 172 us
  blocking collectives: 151 us -> 0 us
  local copies, waits for them, and re-layouts: 113 us -> 224 us
  other arithmetic: 62.1 us -> 97.3 us
    reduce_scatter x3 -> x0, waiting for transfers between devices: 719 us -> none  [the longest x1 360 us: per_device(): lax.psum_scatter(grad_down, ('dp', 'fsdp'), scatter_dimension=0, tiled=True)]
    unnamed x15 -> x0, waiting for transfers between devices: 328 us -> none
    ppermute x0 -> x99, starting transfers between devices: none -> 172 us  [the longest x54 147 us: along(): return lax.ppermute(values, AXES, self.shifted(axis, step, False))]
    ppermute x0 -> x99, waiting for transfers between devices: none -> 119 us  [the longest x45 65.4 us: swap(): return lax.ppermute(values, AXES, self.shifted(axis, 1, True))]
    all_gather x6 -> x0, waiting for transfers between devices: 106 us -> none  [the longest x1 55.1 us: per_device(): lax.all_gather(w_up, ('dp', 'fsdp'), axis=0, tiled=True)]
    unnamed x2 -> x0, blocking collectives: 84.8 us -> none
    all_gather x1 -> x0, blocking collectives: 65.7 us -> none  [per_device(): lax.all_gather(b_up, ('dp', 'fsdp'), axis=0, tiled=True)]
    dynamic_slice x0 -> x7, local copies, waits for them, and re-layouts: none -> 42.1 us  [the longest x5 40.7 us: take(): return lax.dynamic_index_in_dim(values, index, axis, keepdims=False)]
  transfers between devices with their start and end apart: 12 -> 99, of which waited for: 8 -> 28; matrix products, arithmetic and copies ran while one was open for 21% -> 25% of each run, Pallas kernels for 0% -> 1%
where the time goes in v1:
time: 918 us; the launch traced here: 909 us
  matrix products  280 us (31%)
  local copies, waits for them, and re-layouts  224 us (24%)
  starting transfers between devices  172 us (19%)
  waiting for transfers between devices  119 us (13%)
  other arithmetic  97.3 us (11%)
  Pallas kernels  13.9 us (2%)
    ppermute x54, starting transfers between devices, along(): return lax.ppermute(values, AXES, self.shifted(axis, step, False))  147 us
    unnamed x231, local copies, waits for them, and re-layouts  91.6 us
    dot_general x4, matrix products, matmul(): return jnp.dot(operand, other, preferred_element_type=jnp.float32)  74.2 us
    ppermute x45, waiting for transfers between devices, swap(): return lax.ppermute(values, AXES, self.shifted(axis, 1, True))  65.4 us
    ppermute x54, waiting for transfers between devices, along(): return lax.ppermute(values, AXES, self.shifted(axis, step, False))  53.6 us
    dot_general x4, matrix products, back_matmul(): lax.dot_general(operand, other, (((1,), (1,)), ((), ())), preferred_eleme...  48.6 us
    dot_general x8, matrix products, outer_sum(): lax.dot_general(operand, other, (((0,), (0,)), ((), ())), preferred_eleme...  47.3 us
    dot_general x4, matrix products, masked_scores(): jnp.einsum('qhd,khd->hqk', query_rows, key_rows, preferred_element_type=j...  44.1 us
  transfers between devices with their start and end apart: 99, of which 28 were waited for; matrix products, arithmetic and copies ran while one was open for 25% of the time, Pallas kernels for 1%

profile of v1, /device:TPU:0, one launch (start us, length us, event | category | flops | bytes accessed | tf_op | source)
XLA Modules:
  0.0 909.3 jit_solution(2720419934557496424)
XLA Ops:
  83.1 9.0 collective-permute-done.25
  149.9 15.9 %collective-permute-done.42.refs_4_ = bf16[4,32,4096]{2,1,0:T(8,128)(2,1)} collective-permute-done((bf16[4,32,4096]{2,1,0:T(8,128)(2,1)S(1)}, bf16[4,32,4096]{2,1,0:T(8,128)(2,1)}, u32[]{:S(2)}, u32[]{:S(2)}) %collective-permute-start.42) | collective-permute-done | bytes 1048608 | tf_op jit(solution)/shard_map/ppermute | solution.py:145
  166.3 10.5 %fusion.66 = bf16[1024,3072]{0,1:T(8,128)(2,1)S(1)} fusion(f32[3072]{0:T(1024)S(1)} %pad_maximum_fusion.2, bf16[1024,1024]{1,0:T(8,128)(2,1)} %param.22, bf16[1024,3200]{1,0:T(8,128)(2,1)} %bitcast.741), kind=kOutput, calls=%fused_computation.88 | convolution fusion | flops 6448742400 | bytes 14692352 | tf_op jit(solution)/shard_map/dot_general | solution.py:19
  204.8 62.3 %while.26 = (s32[]{:T(128)}, bf16[2,512,1024]{2,1,0:T(8,128)(2,1)}, f32[2,16,512]{2,1,0:T(8,128)S(1)}, bf16[2,512,16,64]{1,3,2,0:T(8,128)(2,1)}, s32[2,512]{1,0:...) while((s32[]{:T(128)}, bf16[2,512,1024]{2,1,0:T(8,128)(2,1)}, ...), condition=%wide.region_3.4_spmd, body=%wide.region_0.3_spmd.sunk | while | flops 1124851712 | bytes 60039260 | solution.py:398
  205.2 9.9 %fusion.273 = (f32[16,512]{1,0:T(8,128)S(1)}, f32[16,512,512]{1,2,0:T(8,128)}) fusion(pred[512,512]{0,1:T(8,128)(4,1)S(1)} %broadcast_compare_fusion.4, bf16[2,512,16,64]{1,3,2,0:T(8,128)(2,1)} %get-tuple-element.465, s32[]{:T(128)} %get-tuple-element.451, bf16[2,512,16,64]{1,3,2,0:T(8,128)(2,1)} %get-tuple-element.464), kind=kOutput, calls=%fused_computation.3.clone.1 | convolution fusion | flops 549445632 | bytes 19170304 | tf_op jit(solution)/shard_map/while/body/eval_jaxpr/qhd,khd->hqk/dot_general | solution.py:62
  215.1 9.2 %fusion.274 = f32[16,512]{1,0:T(8,128)S(1)} fusion(f32[16,512,512]{1,2,0:T(8,128)} %get-tuple-element.429, f32[16,512]{1,0:T(8,128)S(1)} %get-tuple-element.430, pred[512,512]{0,1:T(8,128)(4,1)S(1)} %broadcast_compare_fusion.4), kind=kLoop, calls=%fused_computation.4.clone.1 | loop fusion | flops 16769024 | bytes 17104896 | tf_op jit(solution)/shard_map/while/body/eval_jaxpr/reduce_sum | solution.py:73
  224.3 9.2 %fusion.275 = bf16[16,64,512]{2,1,0:T(8,128)(2,1)} fusion(f32[16,512,512]{1,2,0:T(8,128)} %get-tuple-element.429, f32[16,512]{1,0:T(8,128)S(1)} %fusion.274, f32[16,512]{1,0:T(8,128)S(1)} %get-tuple-element.430, pred[512,512]{0,1:T(8,128)(4,1)S(1)} %broadcast_compare_fusion.4, bf16[2,512,16,64]{1,3,2,0:T(8,128)(2,1)} %get-tuple-element.462, ...), kind=kOutput, calls=%fused_computation.6.clone.1 | convolution fusion | flops 558366720 | bytes 19202560 | tf_op jit(solution)/shard_map/while/body/eval_jaxpr/hqk,khd->qhd/dot_general | solution.py:75
  236.3 9.9 %fusion.273 = (f32[16,512]{1,0:T(8,128)S(1)}, f32[16,512,512]{1,2,0:T(8,128)}) fusion(pred[512,512]{0,1:T(8,128)(4,1)S(1)} %broadcast_compare_fusion.4, bf16[2,512,16,64]{1,3,2,0:T(8,128)(2,1)} %get-tuple-element.465, s32[]{:T(128)} %get-tuple-element.451, bf16[2,512,16,64]{1,3,2,0:T(8,128)(2,1)} %get-tuple-element.464), kind=kOutput, calls=%fused_computation.3.clone.1 | convolution fusion | flops 549445632 | bytes 19170304 | tf_op jit(solution)/shard_map/while/body/eval_jaxpr/qhd,khd->hqk/dot_general | solution.py:62
  246.2 9.2 %fusion.274 = f32[16,512]{1,0:T(8,128)S(1)} fusion(f32[16,512,512]{1,2,0:T(8,128)} %get-tuple-element.429, f32[16,512]{1,0:T(8,128)S(1)} %get-tuple-element.430, pred[512,512]{0,1:T(8,128)(4,1)S(1)} %broadcast_compare_fusion.4), kind=kLoop, calls=%fused_computation.4.clone.1 | loop fusion | flops 16769024 | bytes 17104896 | tf_op jit(solution)/shard_map/while/body/eval_jaxpr/reduce_sum | solution.py:73
  255.4 9.2 %fusion.275 = bf16[16,64,512]{2,1,0:T(8,128)(2,1)} fusion(f32[16,512,512]{1,2,0:T(8,128)} %get-tuple-element.429, f32[16,512]{1,0:T(8,128)S(1)} %fusion.274, f32[16,512]{1,0:T(8,128)S(1)} %get-tuple-element.430, pred[512,512]{0,1:T(8,128)(4,1)S(1)} %broadcast_compare_fusion.4, bf16[2,512,16,64]{1,3,2,0:T(8,128)(2,1)} %get-tuple-element.462, ...), kind=kOutput, calls=%fused_computation.6.clone.1 | convolution fusion | flops 558366720 | bytes 19202560 | tf_op jit(solution)/shard_map/while/body/eval_jaxpr/hqk,khd->qhd/dot_general | solution.py:75
  312.6 46.0 %fusion.52 = (bf16[1024,4096]{1,0:T(8,128)(2,1)}, f32[1024,4096]{1,0:T(8,128)}) fusion(f32[4096]{0:T(1024)S(1)} %fusion.155, bf16[1024,1024]{0,1:T(8,128)(2,1)S(1)} %fusion.73, bf16[1024,4096]{1,0:T(8,128)(2,1)S(1)} %bitcast.736), kind=kOutput, calls=%fused_computation.63 | convolution fusion | flops 8866758656 | bytes 35667968 | tf_op jit(solution)/shard_map/dot_general | solution.py:19
  358.6 14.9 %reshape.1024 = bf16[1024,2,2,1024]{3,2,1,0:T(2,128)(2,1)} reshape(bf16[1024,4096]{1,0:T(8,128)(2,1)} %get-tuple-element.320) | data formatting | bytes 16777216 | tf_op jit(solution)/shard_map/reshape | solution.py:269
  373.5 14.9 %fusion.223 = (f32[1024]{0:T(1024)S(1)}, f32[1024,1024]{0,1:T(8,128)S(1)}) fusion(f32[1024]{0:T(1024)S(1)} %copy-done.96, bf16[1024,4096]{1,0:T(8,128)(2,1)} %get-tuple-element.320, bf16[4096,1024]{1,0:T(8,128)(2,1)} %bitcast.745, f32[1024]{0:T(1024)S(1)} %reshape.1033, f32[1024]{0:T(1024)S(1)} %reshape.1032, f32[1024]{0:T(1024)S(1)} %add_rsqrt_fusion.1, ...), kind=kOutput, calls=%fused_computation.442 | convolution fusion | flops 8597273600 | bytes 25190400 | tf_op jit(solution)/shard_map/dot_general | solution.py:19
  396.9 19.8 %convert_reduce_fusion = (f32[4096]{0:T(1024)}, bf16[1024,4096]{1,0:T(8,128)(2,1)}) fusion(f32[1024,4096]{1,0:T(8,128)} %get-tuple-element.321, f32[4096]{0:T(1024)S(1)} %fusion.155, bf16[1024,1024]{0,1:T(8,128)(2,1)S(1)} %get-tuple-element.262, bf16[4096,1024]{1,0:T(8,128)(2,1)S(1)} %bitcast.748), kind=kOutput, calls=%fused_computation.70 | convolution fusion | flops 8644456448 | bytes 35684352 | tf_op jit(solution)/shard_map/dot_general | solution.py:23
  416.7 16.2 %multiply_reduce_fusion.2 = (f32[1024]{0:T(1024)}, f32[1024]{0:T(1024)S(1)}, f32[1024]{0:T(1024)S(1)}, f32[1024]{0:T(1024)}, f32[1024,1024]{0,1:T(8,128)}) fusion(f32[1024,1024]{0,1:T(8,128)} %copy-done.33, f32[1024]{0:T(1024)S(1)} %add_rsqrt_fusion.1, f32[1024]{0:T(1024)S(1)} %broadcast_multiply_fusion.5, f32[1024]{0:T(1024)S(1)} %reshape.1032, ...), kind=kOutput, calls=%fused_computation.101 | convolution fusion | flops 8607756288 | bytes 33603584 | tf_op jit(solution)/shard_map/dot_general | solution.py:23
  451.9 98.7 %while.27 = (s32[]{:T(128)}, bf16[2,512,16,64]{1,3,2,0:T(8,128)(2,1)}, bf16[2,512,16,64]{1,3,2,0:T(8,128)(2,1)}, bf16[2,512,16,64]{1,3,2,0:T(8,128)(2,1)}, bf16[...) while((s32[]{:T(128)}, ...), condition=%wide.region_14.15_spmd, body=%wide.region_12.14_spmd.sunk | while | flops 2724978688 | bytes 187346224 | solution.py:426
  452.1 9.9 %fusion.284 = f32[16,512,512]{1,2,0:T(8,128)} fusion(bf16[2,512,16,64]{1,3,2,0:T(8,128)(2,1)} %get-tuple-element.498, s32[]{:T(128)} %get-tuple-element.478, bf16[2,512,16,64]{1,3,2,0:T(8,128)(2,1)} %get-tuple-element.497), kind=kOutput, calls=%fused_computation.36.clone.1 | convolution fusion | flops 536870912 | bytes 18875392 | tf_op jit(solution)/shard_map/while/body/eval_jaxpr/qhd,khd->hqk/dot_general | solution.py:86
  462.3 12.1 %multiply_reduce_fusion.10 = (f32[16,512]{1,0:T(8,128)S(1)}, f32[16,512,512]{1,2,0:T(8,128)}) fusion(f32[16,512,512]{1,2,0:T(8,128)} %fusion.284, f32[16,512]{1,0:T(8,128)S(1)} %dynamic-slice_bitcast_fusion.2, bf16[2,512,16,64]{1,3,2,0:T(8,128)(2,1)S(1)} %get-tuple-element.493, s32[]{:T(128)} %get-tuple-element.478, ...), kind=kOutput, calls=%fused_computation.23.clone.1 | convolution fusion | flops 557834240 | bytes 35980288 | tf_op jit(solution)/shard_map/while/body/eval_jaxpr/qhd,khd->hqk/dot_general | solution.py:62
  474.4 11.7 %multiply_convert_fusion.4 = bf16[16,512,512]{1,2,0:T(8,128)(2,1)S(1)} fusion(f32[16,512,512]{1,2,0:T(8,128)} %get-tuple-element.441, f32[16,512,512]{1,2,0:T(8,128)} %fusion.284, f32[16,512]{1,0:T(8,128)S(1)} %get-tuple-element.442), kind=kLoop, calls=%fused_computation.22.clone.1 | loop fusion | flops 12582912 | bytes 41975808 | tf_op jit(solution)/shard_map/while/body/eval_jaxpr/convert_element_type | solution.py:90
  491.7 9.5 %fusion.287 = bf16[2,512,16,64]{1,3,2,0:T(8,128)(2,1)} fusion(bf16[2,512,16,64]{1,3,2,0:T(8,128)(2,1)} %get-tuple-element.481, s32[]{:T(128)} %get-tuple-element.478, f32[16,512,512]{1,2,0:T(8,128)} %get-tuple-element.441, bf16[2,512,16,64]{1,3,2,0:T(8,128)(2,1)S(1)} %copy-done.31), kind=kOutput, calls=%fused_computation.35.clone.1 | convolution fusion | flops 541589504 | bytes 18875392 | tf_op jit(solution)/shard_map/while/body/eval_jaxpr/hqk,qhd->khd/dot_general | solution.py:99
  501.1 9.9 %fusion.284 = f32[16,512,512]{1,2,0:T(8,128)} fusion(bf16[2,512,16,64]{1,3,2,0:T(8,128)(2,1)} %get-tuple-element.498, s32[]{:T(128)} %get-tuple-element.478, bf16[2,512,16,64]{1,3,2,0:T(8,128)(2,1)} %get-tuple-element.497), kind=kOutput, calls=%fused_computation.36.clone.1 | convolution fusion | flops 536870912 | bytes 18875392 | tf_op jit(solution)/shard_map/while/body/eval_jaxpr/qhd,khd->hqk/dot_general | solution.py:86
  511.3 12.1 %multiply_reduce_fusion.10 = (f32[16,512]{1,0:T(8,128)S(1)}, f32[16,512,512]{1,2,0:T(8,128)}) fusion(f32[16,512,512]{1,2,0:T(8,128)} %fusion.284, f32[16,512]{1,0:T(8,128)S(1)} %dynamic-slice_bitcast_fusion.2, bf16[2,512,16,64]{1,3,2,0:T(8,128)(2,1)S(1)} %get-tuple-element.493, s32[]{:T(128)} %get-tuple-element.478, ...), kind=kOutput, calls=%fused_computation.23.clone.1 | convolution fusion | flops 557834240 | bytes 35980288 | tf_op jit(solution)/shard_map/while/body/eval_jaxpr/qhd,khd->hqk/dot_general | solution.py:62
  523.5 11.7 %multiply_convert_fusion.4 = bf16[16,512,512]{1,2,0:T(8,128)(2,1)S(1)} fusion(f32[16,512,512]{1,2,0:T(8,128)} %get-tuple-element.441, f32[16,512,512]{1,2,0:T(8,128)} %fusion.284, f32[16,512]{1,0:T(8,128)S(1)} %get-tuple-element.442), kind=kLoop, calls=%fused_computation.22.clone.1 | loop fusion | flops 12582912 | bytes 41975808 | tf_op jit(solution)/shard_map/while/body/eval_jaxpr/convert_element_type | solution.py:90
  540.7 9.5 %fusion.287 = bf16[2,512,16,64]{1,3,2,0:T(8,128)(2,1)} fusion(bf16[2,512,16,64]{1,3,2,0:T(8,128)(2,1)} %get-tuple-element.481, s32[]{:T(128)} %get-tuple-element.478, f32[16,512,512]{1,2,0:T(8,128)} %get-tuple-element.441, bf16[2,512,16,64]{1,3,2,0:T(8,128)(2,1)S(1)} %copy-done.31), kind=kOutput, calls=%fused_computation.35.clone.1 | convolution fusion | flops 541589504 | bytes 18875392 | tf_op jit(solution)/shard_map/while/body/eval_jaxpr/hqk,qhd->khd/dot_general | solution.py:99
  569.5 10.3 %add_convert_fusion.3 = bf16[1024,1024]{0,1:T(8,128)(2,1)} fusion(bf16[1024,3072]{0,1:T(8,128)(2,1)S(1)} %constant_dynamic-update-slice_fusion.3, bf16[1024,3200]{1,0:T(8,128)(2,1)S(1)} %bitcast.744, f32[1024]{0:T(1024)S(1)} %copy-done.90, f32[1024,1024]{0,1:T(8,128)S(1)} %copy-done.34, f32[1024]{0:T(1024)S(1)} %copy-done.79, f32[1024]{0:T(1024)S(1)} %copy-done.92, ...), kind=kOutput, calls=%fused_computation.103 | convolution fusion | flops 6451888128 | bytes 23089152 | tf_op jit(solution)/shard_map/dot_general | solution.py:23
  579.8 18.8 %constant_dynamic-slice_fusion.42 = (bf16[1024,2,1,1024]{3,2,1,0:T(2,128)(2,1)}, bf16[1024,2,1,1024]{3,2,1,0:T(2,128)(2,1)}) fusion(bf16[1024,2,2,1024]{3,2,1,0:T(2,128)(2,1)S(1)} %bitcast.752, s32[]{:T(128)S(6)} %select_n.315, s32[]{:T(128)S(6)} %select_n.320), kind=kLoop, calls=%fused_computation.341 | loop fusion | bytes 16777224 | tf_op jit(solution)/shard_map/jit(dynamic_index_in_dim)/dynamic_slice | solution.py:224
  598.6 20.1 %copy.135 = bf16[1024,2,1,1024]{0,3,1,2:T(8,128)(2,1)} copy(bf16[1024,2,1,1024]{3,2,1,0:T(2,128)(2,1)} %get-tuple-element.273) | data formatting | bytes 8388608
  627.1 20.0 %copy.136 = bf16[1024,2,1,1024]{0,3,1,2:T(8,128)(2,1)} copy(bf16[1024,2,1,1024]{3,2,1,0:T(2,128)(2,1)} %get-tuple-element.274) | data formatting | bytes 8388608
  647.1 8.6 convolution_convert_fusion.4
  657.9 9.6 %convolution_convert_fusion.1 = bf16[512,4096]{1,0:T(8,128)(2,1)} fusion(bf16[1024,512]{0,1:T(8,128)(2,1)S(1)} %bitcast.836, bf16[1024,4096]{1,0:T(8,128)(2,1)} %get-tuple-element.326), kind=kOutput, calls=%fused_computation.90 | convolution fusion | flops 4297064448 | bytes 13631488 | tf_op jit(solution)/shard_map/dot_general | solution.py:29
  668.3 9.7 %convolution_convert_fusion = bf16[512,4096]{1,0:T(8,128)(2,1)} fusion(bf16[1024,512]{0,1:T(8,128)(2,1)S(1)} %bitcast.835, bf16[1024,4096]{1,0:T(8,128)(2,1)} %get-tuple-element.326), kind=kOutput, calls=%fused_computation.89 | convolution fusion | flops 4297064448 | bytes 13631488 | tf_op jit(solution)/shard_map/dot_general | solution.py:29
  796.9 15.5 %collective-permute-done.91 = bf16[4,2,128,1024]{3,2,1,0:T(8,128)(2,1)S(1)} collective-permute-done((bf16[4,2,128,1024]{3,2,1,0:T(8,128)(2,1)S(1)}, bf16[4,2,128,1024]{3,2,1,0:T(8,128)(2,1)S(1)}, u32[]{:S(2)}, u32[]{:S(2)}) %collective-permute-start.91) | collective-permute-done | bytes 2097184 | tf_op jit(solution)/shard_map/ppermute | solution.py:145
  (613 shorter events, 502.5 us)
Async XLA Ops:
  15.8 24.7 %collective-permute-start.20 = (bf16[160,1024]{1,0:T(8,128)(2,1)S(1)}, bf16[160,1024]{1,0:T(8,128)(2,1)S(1)}, u32[]{:S(2)}, u32[]{:S(2)}) collective-permute-start(bf16[160,1024]{1,0:T(8,128)(2,1)S(1)} %constant_dynamic-update-slice_fusion.1), channel_id=1, source_target_pairs={{0,2},{1,3},{2,4},{3,5},{4,6},{5,7},{8,10},{9,11},{10,12},{11,13},... | collective-permute-start | bytes 983048 | tf_op jit(solution)/shard_map/ppermute | solution.py:148
  47.1 22.3 %collective-permute-start.21 = (bf16[160,1024]{1,0:T(8,128)(2,1)S(1)}, bf16[160,1024]{1,0:T(8,128)(2,1)S(1)}, u32[]{:S(2)}, u32[]{:S(2)}) collective-permute-start(bf16[160,1024]{1,0:T(8,128)(2,1)S(1)} %collective-permute-done.20), channel_id=1, source_target_pairs={{0,2},{1,3},{2,4},{3,5},{4,6},{5,7},{8,10},{9,11},{10,12},{11,13},... | collective-permute-start | bytes 983048 | tf_op jit(solution)/shard_map/ppermute | solution.py:148
  65.1 27.5 %collective-permute-start.7 = (bf16[4,32,1536]{2,1,0:T(8,128)(2,1)S(1)}, bf16[4,32,1536]{2,1,0:T(8,128)(2,1)S(1)}, u32[]{:S(2)}, u32[]{:S(2)}) collective-permute-start(bf16[4,32,1536]{2,1,0:T(8,128)(2,1)S(1)} %constant_dynamic-slice_fusion.2.refs_0_), channel_id=1, source_target_pairs={{0,1},{1,0},{2,3},{3,2},{4,5},{5,4},{6,7},{7,6},{8,9},{9,8},{10,11... | collective-permute-start | bytes 1179656 | tf_op jit(solution)/shard_map/ppermute | solution.py:145
  66.7 25.9 %collective-permute-start.9 = (bf16[4,32,1536]{2,1,0:T(8,128)(2,1)S(1)}, bf16[4,32,1536]{2,1,0:T(8,128)(2,1)S(1)}, u32[]{:S(2)}, u32[]{:S(2)}) collective-permute-start(bf16[4,32,1536]{2,1,0:T(8,128)(2,1)S(1)} %constant_dynamic-slice_fusion.2.refs_0_), channel_id=1, source_target_pairs={{0,16},{1,17},{2,18},{3,19},{4,20},{5,21},{6,22},{7,23},{8,24},{9,... | collective-permute-start | bytes 1179656 | tf_op jit(solution)/shard_map/ppermute | solution.py:145
  69.4 24.5 %collective-permute-start.6 = (bf16[4,32,1536]{2,1,0:T(8,128)(2,1)S(1)}, bf16[4,32,1536]{2,1,0:T(8,128)(2,1)S(1)}, u32[]{:S(2)}, u32[]{:S(2)}) collective-permute-start(bf16[4,32,1536]{2,1,0:T(8,128)(2,1)S(1)} %constant_dynamic-slice_fusion.2.refs_0_), channel_id=1, source_target_pairs={{0,8},{1,9},{2,10},{3,11},{4,12},{5,13},{6,14},{7,15},{8,0},{9,1},... | collective-permute-start | bytes 1179656 | tf_op jit(solution)/shard_map/ppermute | solution.py:145
  105.6 25.2 %collective-permute-start.40 = (bf16[4,32,4096]{2,1,0:T(8,128)(2,1)S(1)}, bf16[4,32,4096]{2,1,0:T(8,128)(2,1)S(1)}, u32[]{:S(2)}, u32[]{:S(2)}) collective-permute-start(bf16[4,32,4096]{2,1,0:T(8,128)(2,1)S(1)} %constant_dynamic-slice_fusion.45.refs_0_), channel_id=1, source_target_pairs={{0,16},{1,17},{2,18},{3,19},{4,20},{5,21},{6,22},{7,23},{8,24},{9,... | collective-permute-start | bytes 3145736 | tf_op jit(solution)/shard_map/ppermute | solution.py:145
  107.9 58.4 %collective-permute-start.27 = (bf16[4,160,1024]{2,1,0:T(8,128)(2,1)}, bf16[4,160,1024]{2,1,0:T(8,128)(2,1)}, u32[]{:S(2)}, u32[]{:S(2)}) collective-permute-start(bf16[4,160,1024]{2,1,0:T(8,128)(2,1)} %constant_dynamic-slice_fusion.46.refs_0_), channel_id=1, source_target_pairs={{0,1},{1,0},{2,3},{3,2},{4,5},{5,4},{6,7},{7,6},{8,9},{9,8},{10,11... | collective-permute-start | bytes 3932168 | tf_op jit(solution)/shard_map/ppermute | solution.py:145
  116.0 49.8 %collective-permute-start.42 = (bf16[4,32,4096]{2,1,0:T(8,128)(2,1)S(1)}, bf16[4,32,4096]{2,1,0:T(8,128)(2,1)}, u32[]{:S(2)}, u32[]{:S(2)}) collective-permute-start(bf16[4,32,4096]{2,1,0:T(8,128)(2,1)S(1)} %constant_dynamic-slice_fusion.45.refs_0_), channel_id=1, source_target_pairs={{0,1},{1,0},{2,3},{3,2},{4,5},{5,4},{6,7},{7,6},{8,9},{9,8},{10,11... | collective-permute-start | bytes 3145736 | tf_op jit(solution)/shard_map/ppermute | solution.py:145
  116.8 49.0 %collective-permute-start.39 = (bf16[4,32,4096]{2,1,0:T(8,128)(2,1)S(1)}, bf16[4,32,4096]{2,1,0:T(8,128)(2,1)}, u32[]{:S(2)}, u32[]{:S(2)}) collective-permute-start(bf16[4,32,4096]{2,1,0:T(8,128)(2,1)S(1)} %constant_dynamic-slice_fusion.45.refs_0_), channel_id=1, source_target_pairs={{0,8},{1,9},{2,10},{3,11},{4,12},{5,13},{6,14},{7,15},{8,0},{9,1},... | collective-permute-start | bytes 3145736 | tf_op jit(solution)/shard_map/ppermute | solution.py:145
  130.7 72.9 %collective-permute-start.29 = (bf16[4,160,1024]{2,1,0:T(8,128)(2,1)}, bf16[4,160,1024]{2,1,0:T(8,128)(2,1)}, u32[]{:S(2)}, u32[]{:S(2)}) collective-permute-start(bf16[4,160,1024]{2,1,0:T(8,128)(2,1)} %constant_dynamic-slice_fusion.46.refs_0_), channel_id=1, source_target_pairs={{0,16},{1,17},{2,18},{3,19},{4,20},{5,21},{6,22},{7,23},{8,24},{9,... | collective-permute-start | bytes 3932168 | tf_op jit(solution)/shard_map/ppermute | solution.py:145
  131.1 72.6 %collective-permute-start.44 = (bf16[4,32,4096]{2,1,0:T(8,128)(2,1)S(1)}, bf16[4,32,4096]{2,1,0:T(8,128)(2,1)}, u32[]{:S(2)}, u32[]{:S(2)}) collective-permute-start(bf16[4,32,4096]{2,1,0:T(8,128)(2,1)S(1)} %collective-permute-done.40.refs_2_), channel_id=1, source_target_pairs={{0,1},{1,0},{2,3},{3,2},{4,5},{5,4},{6,7},{7,6},{8,9},{9,8},{10,11... | collective-permute-start | bytes 3145736 | tf_op jit(solution)/shard_map/ppermute | solution.py:145
  165.8 38.3 %collective-permute-start.41 = (bf16[4,32,4096]{2,1,0:T(8,128)(2,1)S(1)}, bf16[4,32,4096]{2,1,0:T(8,128)(2,1)}, u32[]{:S(2)}, u32[]{:S(2)}) collective-permute-start(bf16[4,32,4096]{2,1,0:T(8,128)(2,1)S(1)} %collective-permute-done.40.refs_2_), channel_id=1, source_target_pairs={{0,8},{1,9},{2,10},{3,11},{4,12},{5,13},{6,14},{7,15},{8,0},{9,1},... | collective-permute-start | bytes 3145736 | tf_op jit(solution)/shard_map/ppermute | solution.py:145
  165.8 38.4 %collective-permute-start.43 = (bf16[4,32,4096]{2,1,0:T(8,128)(2,1)}, bf16[4,32,4096]{2,1,0:T(8,128)(2,1)}, u32[]{:S(2)}, u32[]{:S(2)}) collective-permute-start(bf16[4,32,4096]{2,1,0:T(8,128)(2,1)} %collective-permute-done.42.refs_4_), channel_id=1, source_target_pairs={{0,8},{1,9},{2,10},{3,11},{4,12},{5,13},{6,14},{7,15},{8,0},{9,1},... | collective-permute-start | bytes 3145736 | tf_op jit(solution)/shard_map/ppermute | solution.py:145
  166.3 38.3 %collective-permute-start.31 = (bf16[4,160,1024]{2,1,0:T(8,128)(2,1)}, bf16[4,160,1024]{2,1,0:T(8,128)(2,1)}, u32[]{:S(2)}, u32[]{:S(2)}) collective-permute-start(bf16[4,160,1024]{2,1,0:T(8,128)(2,1)} %collective-permute-done.27.refs_2_), channel_id=1, source_target_pairs={{0,16},{1,17},{2,18},{3,19},{4,20},{5,21},{6,22},{7,23},{8,24},{9,... | collective-permute-start | bytes 3932168 | tf_op jit(solution)/shard_map/ppermute | solution.py:145
  203.6 95.0 %collective-permute-start.26 = (bf16[4,160,1024]{2,1,0:T(8,128)(2,1)}, bf16[4,160,1024]{2,1,0:T(8,128)(2,1)}, u32[]{:S(2)}, u32[]{:S(2)}) collective-permute-start(bf16[4,160,1024]{2,1,0:T(8,128)(2,1)} %constant_dynamic-slice_fusion.46.refs_0_), channel_id=1, source_target_pairs={{0,8},{1,9},{2,10},{3,11},{4,12},{5,13},{6,14},{7,15},{8,0},{9,1},... | collective-permute-start | bytes 3932168 | tf_op jit(solution)/shard_map/ppermute | solution.py:145
  203.7 94.9 %collective-permute-start.28 = (bf16[4,160,1024]{2,1,0:T(8,128)(2,1)}, bf16[4,160,1024]{2,1,0:T(8,128)(2,1)}, u32[]{:S(2)}, u32[]{:S(2)}) collective-permute-start(bf16[4,160,1024]{2,1,0:T(8,128)(2,1)} %collective-permute-done.27.refs_2_), channel_id=1, source_target_pairs={{0,8},{1,9},{2,10},{3,11},{4,12},{5,13},{6,14},{7,15},{8,0},{9,1},... | collective-permute-start | bytes 3932168 | tf_op jit(solution)/shard_map/ppermute | solution.py:145
  204.1 94.5 %collective-permute-start.30 = (bf16[4,160,1024]{2,1,0:T(8,128)(2,1)}, bf16[4,160,1024]{2,1,0:T(8,128)(2,1)}, u32[]{:S(2)}, u32[]{:S(2)}) collective-permute-start(bf16[4,160,1024]{2,1,0:T(8,128)(2,1)} %collective-permute-done.29.refs_4_), channel_id=1, source_target_pairs={{0,8},{1,9},{2,10},{3,11},{4,12},{5,13},{6,14},{7,15},{8,0},{9,1},... | collective-permute-start | bytes 3932168 | tf_op jit(solution)/shard_map/ppermute | solution.py:145
  204.2 90.8 %collective-permute-start.45 = (bf16[4,32,4096]{2,1,0:T(8,128)(2,1)}, bf16[4,32,4096]{2,1,0:T(8,128)(2,1)}, u32[]{:S(2)}, u32[]{:S(2)}) collective-permute-start(bf16[4,32,4096]{2,1,0:T(8,128)(2,1)} %collective-permute-done.44.refs_6_), channel_id=1, source_target_pairs={{0,8},{1,9},{2,10},{3,11},{4,12},{5,13},{6,14},{7,15},{8,0},{9,1},... | collective-permute-start | bytes 3145736 | tf_op jit(solution)/shard_map/ppermute | solution.py:145
  204.6 94.0 %collective-permute-start.32 = (bf16[4,160,1024]{2,1,0:T(8,128)(2,1)}, bf16[4,160,1024]{2,1,0:T(8,128)(2,1)}, u32[]{:S(2)}, u32[]{:S(2)}) collective-permute-start(bf16[4,160,1024]{2,1,0:T(8,128)(2,1)} %collective-permute-done.31.refs_6_), channel_id=1, source_target_pairs={{0,8},{1,9},{2,10},{3,11},{4,12},{5,13},{6,14},{7,15},{8,0},{9,1},... | collective-permute-start | bytes 3932168 | tf_op jit(solution)/shard_map/ppermute | solution.py:145
  655.6 108.3 %collective-permute-start.90 = (bf16[2048,1024]{1,0:T(8,128)(2,1)}, bf16[2048,1024]{1,0:T(8,128)(2,1)}, u32[]{:S(2)}, u32[]{:S(2)}) collective-permute-start(bf16[2048,1024]{1,0:T(8,128)(2,1)} %convolution_convert_fusion.4), channel_id=1, source_target_pairs={{0,8},{1,9},{2,10},{3,11},{4,12},{5,13},{6,14},{7,15},{8,0},{9,1},... | collective-permute-start | bytes 12582920 | tf_op jit(solution)/shard_map/ppermute | solution.py:145
  678.0 89.0 %collective-permute-start.81 = (bf16[512,4096]{1,0:T(8,128)(2,1)}, bf16[512,4096]{1,0:T(8,128)(2,1)}, u32[]{:S(2)}, u32[]{:S(2)}) collective-permute-start(bf16[512,4096]{1,0:T(8,128)(2,1)} %convolution_convert_fusion), channel_id=1, source_target_pairs={{0,8},{1,9},{2,10},{3,11},{4,12},{5,13},{6,14},{7,15},{8,0},{9,1},... | collective-permute-start | bytes 12582920 | tf_op jit(solution)/shard_map/ppermute | solution.py:145
  691.6 51.2 %collective-permute-start.46 = (bf16[512,3072]{1,0:T(8,128)(2,1)}, bf16[512,3072]{1,0:T(8,128)(2,1)}, u32[]{:S(2)}, u32[]{:S(2)}) collective-permute-start(bf16[512,3072]{1,0:T(8,128)(2,1)} %convolution_convert_fusion.2), channel_id=1, source_target_pairs={{0,8},{1,9},{2,10},{3,11},{4,12},{5,13},{6,14},{7,15},{8,0},{9,1},... | collective-permute-start | bytes 9437192 | tf_op jit(solution)/shard_map/ppermute | solution.py:145
  767.0 45.4 %collective-permute-start.91 = (bf16[4,2,128,1024]{3,2,1,0:T(8,128)(2,1)S(1)}, bf16[4,2,128,1024]{3,2,1,0:T(8,128)(2,1)S(1)}, u32[]{:S(2)}, u32[]{:S(2)}) collective-permute-start(bf16[4,2,128,1024]{3,2,1,0:T(8,128)(2,1)S(1)} %fusion.75), channel_id=1, source_target_pairs={{0,16},{1,17},{2,18},{3,19},{4,20},{5,21},{6,22},{7,23},{8,24},{9,... | collective-permute-start | bytes 6291464 | tf_op jit(solution)/shard_map/ppermute | solution.py:145
  771.0 48.5 %collective-permute-start.82 = (bf16[2,4,32,4096]{3,2,1,0:T(8,128)(2,1)S(1)}, bf16[2,4,32,4096]{3,2,1,0:T(8,128)(2,1)S(1)}, u32[]{:S(2)}, u32[]{:S(2)}) collective-permute-start(bf16[2,4,32,4096]{3,2,1,0:T(8,128)(2,1)S(1)} %fusion.74), channel_id=1, source_target_pairs={{0,1},{1,0},{2,3},{3,2},{4,5},{5,4},{6,7},{7,6},{8,9},{9,8},{10,11... | collective-permute-start | bytes 6291464 | tf_op jit(solution)/shard_map/ppermute | solution.py:145
  788.1 33.2 %collective-permute-start.67 = (bf16[32,1536]{1,0:T(8,128)(2,1)S(1)}, bf16[32,1536]{1,0:T(8,128)(2,1)S(1)}, u32[]{:S(2)}, u32[]{:S(2)}) collective-permute-start(bf16[32,1536]{1,0:T(8,128)(2,1)S(1)} %fusion.117), channel_id=1, source_target_pairs={{0,2},{1,3},{2,4},{3,5},{4,6},{5,7},{8,10},{9,11},{10,12},{11,13},... | collective-permute-start | bytes 294920 | tf_op jit(solution)/shard_map/ppermute | solution.py:148
  790.8 32.0 %collective-permute-start.52 = (bf16[32,1536]{1,0:T(8,128)(2,1)S(1)}, bf16[32,1536]{1,0:T(8,128)(2,1)S(1)}, u32[]{:S(2)}, u32[]{:S(2)}) collective-permute-start(bf16[32,1536]{1,0:T(8,128)(2,1)S(1)} %get-tuple-element.281), channel_id=1, source_target_pairs={{2,0},{3,1},{4,2},{5,3},{6,4},{7,5},{10,8},{11,9},{12,10},{13,11},... | collective-permute-start | bytes 294920 | tf_op jit(solution)/shard_map/ppermute | solution.py:148
  792.1 78.9 %collective-permute-start.51 = (bf16[32,1536]{1,0:T(8,128)(2,1)S(1)}, bf16[32,1536]{1,0:T(8,128)(2,1)S(1)}, u32[]{:S(2)}, u32[]{:S(2)}) collective-permute-start(bf16[32,1536]{1,0:T(8,128)(2,1)S(1)} %get-tuple-element.280), channel_id=1, source_target_pairs={{0,2},{1,3},{2,4},{3,5},{4,6},{5,7},{8,10},{9,11},{10,12},{11,13},... | collective-permute-start | bytes 294920 | tf_op jit(solution)/shard_map/ppermute | solution.py:148
  814.3 21.9 %collective-permute-start.92 = (bf16[4,128,1024]{2,1,0:T(8,128)(2,1)S(1)}, bf16[4,128,1024]{2,1,0:T(8,128)(2,1)S(1)}, u32[]{:S(2)}, u32[]{:S(2)}) collective-permute-start(bf16[4,128,1024]{2,1,0:T(8,128)(2,1)S(1)} %fusion.76), channel_id=1, source_target_pairs={{0,1},{1,0},{2,3},{3,2},{4,5},{5,4},{6,7},{7,6},{8,9},{9,8},{10,11... | collective-permute-start | bytes 3145736 | tf_op jit(solution)/shard_map/ppermute | solution.py:145
  822.8 63.5 %collective-permute-start.68 = (bf16[32,1536]{1,0:T(8,128)(2,1)S(1)}, bf16[32,1536]{1,0:T(8,128)(2,1)S(1)}, u32[]{:S(2)}, u32[]{:S(2)}) collective-permute-start(bf16[32,1536]{1,0:T(8,128)(2,1)S(1)} %get-tuple-element.278), channel_id=1, source_target_pairs={{0,2},{1,3},{2,4},{3,5},{4,6},{5,7},{8,10},{9,11},{10,12},{11,13},... | collective-permute-start | bytes 294920 | tf_op jit(solution)/shard_map/ppermute | solution.py:148
  836.2 23.9 %collective-permute-start.70 = (bf16[32,1536]{1,0:T(8,128)(2,1)S(1)}, bf16[32,1536]{1,0:T(8,128)(2,1)S(1)}, u32[]{:S(2)}, u32[]{:S(2)}) collective-permute-start(bf16[32,1536]{1,0:T(8,128)(2,1)S(1)} %fusion.112), channel_id=1, source_target_pairs={{2,0},{3,1},{4,2},{5,3},{6,4},{7,5},{10,8},{11,9},{12,10},{13,11},... | collective-permute-start | bytes 294920 | tf_op jit(solution)/shard_map/ppermute | solution.py:148
  848.8 23.5 %collective-permute-start.54 = (bf16[32,1536]{1,0:T(8,128)(2,1)S(1)}, bf16[32,1536]{1,0:T(8,128)(2,1)S(1)}, u32[]{:S(2)}, u32[]{:S(2)}) collective-permute-start(bf16[32,1536]{1,0:T(8,128)(2,1)S(1)} %fusion.126), channel_id=1, source_target_pairs={{2,0},{3,1},{4,2},{5,3},{6,4},{7,5},{10,8},{11,9},{12,10},{13,11},... | collective-permute-start | bytes 294920 | tf_op jit(solution)/shard_map/ppermute | solution.py:148
  864.6 21.7 %collective-permute-start.71 = (bf16[32,1536]{1,0:T(8,128)(2,1)S(1)}, bf16[32,1536]{1,0:T(8,128)(2,1)S(1)}, u32[]{:S(2)}, u32[]{:S(2)}) collective-permute-start(bf16[32,1536]{1,0:T(8,128)(2,1)S(1)} %fusion.114), channel_id=1, source_target_pairs={{2,0},{3,1},{4,2},{5,3},{6,4},{7,5},{10,8},{11,9},{12,10},{13,11},... | collective-permute-start | bytes 294920 | tf_op jit(solution)/shard_map/ppermute | solution.py:148
  (180 other events, 2580.2 us)

commit v2 on v1

v2 whole, which is shorter than its diff:
```python
import functools

import jax
import jax.numpy as jnp
from jax import lax
from jax.experimental import pallas as pl
from jax.experimental.pallas import tpu as pltpu
from jax.sharding import PartitionSpec as P

D = 1024
H = 16
DH = 64
SEQ_LEN = 512
AXES = ("dp", "fsdp")
CORES = 2


def matmul(operand, other):
    return jnp.dot(operand, other, preferred_element_type=jnp.float32)


def back_matmul(operand, other):
    return lax.dot_general(
        operand, other, (((1,), (1,)), ((), ())), preferred_element_type=jnp.float32
    )


def outer_sum(operand, other):
    return lax.dot_general(
        operand, other, (((0,), (0,)), ((), ())), preferred_element_type=jnp.float32
    )


def column_sum(values):
    return jnp.sum(values.astype(jnp.float32), axis=0)


def norm_forward(hidden):
    centred = hidden - jnp.mean(hidden, axis=-1, keepdims=True)
    scale_row = lax.rsqrt(jnp.mean(centred * centred, axis=-1, keepdims=True) + 1e-12)
    return (centred * scale_row, scale_row)


def norm_backward(grad_out, normed, scale_row, scaling):
    scaled = grad_out * scaling
    return scale_row * (
        scaled
        - jnp.mean(scaled, axis=-1, keepdims=True)
        - normed * jnp.mean(scaled * normed, axis=-1, keepdims=True)
    )


def across(operand, other):
    return lax.dot_general(
        operand, other, (((1,), (1,)), ((), ())), preferred_element_type=jnp.float32
    )


def down(operand, other):
    return lax.dot_general(
        operand, other, (((0,), (0,)), ((), ())), preferred_element_type=jnp.float32
    )


def attend_forward_kernel(query, key, value, doc_column, doc_row, mixed):
    same = doc_column[0] == doc_row[0]
    heads = []
    for head in range(2):
        lanes = slice(head * DH, (head + 1) * DH)
        scores = across(key[:, lanes], query[:, lanes] * jnp.bfloat16(0.125))
        scores = jnp.where(same, scores, -1000000000.0)
        powers = jnp.exp(scores - jnp.max(scores, axis=0, keepdims=True))
        row_total = jnp.sum(powers, axis=0, keepdims=True)
        heads.append(down(value[:, lanes], powers.astype(jnp.bfloat16)) * (1.0 / row_total))
    mixed[...] = jnp.concatenate(heads, axis=0).T.astype(jnp.bfloat16)


def attend_backward_kernel(query, key, value, grad, doc_column, doc_row, out, sums):
    same = doc_column[0] == doc_row[0]
    step = pl.program_id(1)
    found = ([], [], [])
    for head in range(2):
        lanes = slice(head * DH, (head + 1) * DH)
        scaled = query[:, lanes] * jnp.bfloat16(0.125)
        scores = jnp.where(same, across(key[:, lanes], scaled), -1000000000.0)
        powers = jnp.exp(scores - jnp.max(scores, axis=0, keepdims=True))
        probability = powers * (1.0 / jnp.sum(powers, axis=0, keepdims=True))
        grad_prob = across(value[:, lanes], grad[:, lanes])
        delta = jnp.sum(probability * grad_prob, axis=0, keepdims=True)
        grad_scores = (probability * (grad_prob - delta)).astype(jnp.bfloat16)
        found[0].append(down(key[:, lanes], grad_scores) * 0.125)
        found[1].append(matmul(grad_scores, scaled))
        found[2].append(matmul(probability.astype(jnp.bfloat16), grad[:, lanes]))
    grads = (
        jnp.concatenate(found[0], axis=0).T,
        jnp.concatenate(found[1], axis=1),
        jnp.concatenate(found[2], axis=1),
    )
    first = pl.program_id(0) == 0
    for index, value_of in enumerate(grads):
        rounded = value_of.astype(jnp.bfloat16)
        place = pl.ds(pl.multiple_of(index * HALF + step * 128, 128), 128)
        out[:, place] = rounded
        if index != 1:
            more = jnp.sum(rounded.astype(jnp.float32), axis=0, keepdims=True)
            sums[:, place] = jnp.where(first, 0.0, sums[:, place]) + more


HALF = D // 2
PAIRS = HALF // 128


def head_specs(start):
    def block(part):
        def index(seq, pair):
            pair = pair + start
            return seq, pair // PAIRS * (3 * PAIRS) + part * PAIRS + pair % PAIRS

        return pl.BlockSpec((SEQ_LEN, 128), index)

    docs = [
        pl.BlockSpec((1, SEQ_LEN, 1), lambda seq, pair: (seq, 0, 0)),
        pl.BlockSpec((1, 1, SEQ_LEN), lambda seq, pair: (seq, 0, 0)),
    ]
    return [block(i) for i in range(3)], docs


def attend_forward(qkv, doc_column, doc_row):
    seqs = doc_row.shape[0]
    heads, docs = head_specs(0)
    work = seqs * H * SEQ_LEN * SEQ_LEN
    return pl.pallas_call(
        attend_forward_kernel,
        grid=(seqs, 2 * PAIRS),
        out_shape=jax.ShapeDtypeStruct((seqs * SEQ_LEN, D), jnp.bfloat16),
        in_specs=heads + docs,
        out_specs=pl.BlockSpec((SEQ_LEN, 128), lambda seq, pair: (seq, pair)),
        cost_estimate=pl.CostEstimate(
            flops=16 * DH * work, bytes_accessed=8 * qkv.size, transcendentals=work
        ),
        compiler_params=pltpu.CompilerParams(vmem_limit_bytes=40 << 20),
    )(qkv, qkv, qkv, doc_column, doc_row)


def attend_backward(qkv, grad_mixed, doc_column, doc_row, half):
    seqs = doc_row.shape[0]
    heads, docs = head_specs(half * PAIRS)
    work = seqs * H * SEQ_LEN * SEQ_LEN // 2
    return pl.pallas_call(
        attend_backward_kernel,
        grid=(seqs, PAIRS),
        out_shape=[
            jax.ShapeDtypeStruct((seqs * SEQ_LEN, 3 * HALF), jnp.bfloat16),
            jax.ShapeDtypeStruct((1, 3 * HALF), jnp.float32),
        ],
        in_specs=heads
        + [pl.BlockSpec((SEQ_LEN, 128), lambda seq, pair: (seq, half * PAIRS + pair))]
        + docs,
        out_specs=[
            pl.BlockSpec((SEQ_LEN, 3 * HALF), lambda seq, pair: (seq, 0)),
            pl.BlockSpec((1, 3 * HALF), lambda seq, pair: (0, 0)),
        ],
        cost_estimate=pl.CostEstimate(
            flops=40 * DH * work, bytes_accessed=8 * qkv.size, transcendentals=work
        ),
        compiler_params=pltpu.CompilerParams(vmem_limit_bytes=50 << 20),
    )(qkv, qkv, qkv, grad_mixed, doc_column, doc_row)


CHUNK = 512
TILE = 256


def part_out(spot, values, parted, blocks):
    width = values.shape[1] // blocks
    for block in range(blocks):
        half = (block % 2 + spot[0] + 1) % 2
        start = block // 2 * width
        parted[half, :, start : start + width] = values[:, block * width : (block + 1) * width]


def middle_forward_kernel(
    blocks,
    spot,
    mixed,
    tokens,
    cotangent,
    w_out,
    w_up,
    w_down,
    vectors,
    bias_up,
    output,
    grad_sum,
    grad_low,
    normed,
    scale,
    active_parts,
    slope,
    first_parts,
    mixed_parts,
    token_parts,
    sums,
):
    bias_out, gain_one, shift_one, bias_down, gain_two, shift_two = (
        vectors[i : i + 1, :] for i in range(6)
    )
    part_out(spot, mixed[...], mixed_parts, blocks)
    part_out(spot, tokens[...], token_parts, blocks)
    hidden = tokens[...].astype(jnp.float32) + matmul(mixed[...], w_out[...]) + bias_out
    normed_one, scale_one = norm_forward(hidden)
    normed[...] = normed_one
    scale[...] = jnp.broadcast_to(scale_one, scale.shape)
    first_out = normed_one * gain_one + shift_one
    first_low = first_out.astype(jnp.bfloat16)
    part_out(spot, first_low, first_parts, blocks)
    width = w_up.shape[1] // blocks
    second = first_out + bias_down
    for start in range(0, w_up.shape[1], CHUNK):
        at = slice(start, start + CHUNK)
        upward = matmul(first_low, w_up[:, at]) + bias_up[:, at]
        phi = 0.5 * (1.0 + lax.erf(upward * 0.7071067811865476))
        active = (upward * phi).astype(jnp.bfloat16)
        slope[:, at] = (
            phi + upward * jnp.exp(-0.5 * upward * upward) * 0.3989422804014327
        ).astype(jnp.bfloat16)
        block, inside = start // width, start % width
        half = (block % 2 + spot[0] + 1) % 2
        place = block // 2 * width + inside
        active_parts[half, :, place : place + CHUNK] = active
        second = second + matmul(active, w_down[at, :])
    normed_two, scale_two = norm_forward(second)
    output[...] = (normed_two * gain_two + shift_two).astype(jnp.bfloat16)
    grad = cotangent[...]
    grad_second = norm_backward(grad, normed_two, scale_two, gain_two)
    grad_sum[...] = grad_second
    rounded = grad_second.astype(jnp.bfloat16)
    grad_low[...] = rounded

    @pl.when(pl.program_id(0) == 0)
    def _():
        sums[...] = jnp.zeros_like(sums)

    sums[0:1, :] += jnp.sum(grad * normed_two, axis=0, keepdims=True)
    sums[1:2, :] += jnp.sum(grad, axis=0, keepdims=True)
    sums[2:3, :] += jnp.sum(rounded.astype(jnp.float32), axis=0, keepdims=True)


def middle_backward_kernel(
    grad_low,
    grad_sum,
    slope,
    normed,
    scale,
    w_out,
    w_up,
    w_down,
    vectors,
    grad_up,
    grad_hidden,
    branch,
    grad_mixed,
    sums,
    sums_up,
):
    @pl.when(pl.program_id(0) == 0)
    def _():
        sums[...] = jnp.zeros_like(sums)
        sums_up[...] = jnp.zeros_like(sums_up)

    grad_first = grad_sum[...]
    low = grad_low[...]
    for start in range(0, w_up.shape[1], CHUNK):
        at = slice(start, start + CHUNK)
        part = (across(low, w_down[at, :]) * slope[:, at].astype(jnp.float32)).astype(jnp.bfloat16)
        grad_up[:, at] = part
        sums_up[:, at] += jnp.sum(part.astype(jnp.float32), axis=0, keepdims=True)
        grad_first = grad_first + across(part, w_up[:, at])
    normed_one = normed[...]
    sums[0:1, :] += jnp.sum(grad_first * normed_one, axis=0, keepdims=True)
    sums[1:2, :] += jnp.sum(grad_first, axis=0, keepdims=True)
    hidden = norm_backward(grad_first, normed_one, scale[:, 0:1], vectors[1:2, :])
    grad_hidden[...] = hidden
    rounded = hidden.astype(jnp.bfloat16)
    branch[...] = rounded
    sums[2:3, :] += jnp.sum(rounded.astype(jnp.float32), axis=0, keepdims=True)
    grad_mixed[...] = across(rounded, w_out[...]).astype(jnp.bfloat16)


def tiled(columns):
    return pl.BlockSpec((TILE, columns), lambda i: (i, 0))


def parted(columns):
    return pl.BlockSpec((2, TILE, columns), lambda i: (0, i, 0))


def resident(shape):
    return pl.BlockSpec(shape, lambda i: (0,) * len(shape), pipeline_mode=pl.Buffered(1))


def middle_forward(core, blocks, mixed, tokens, cotangent, w_out, w_up, w_down, vectors, bias_up):
    rows, wide = tokens.shape[0], w_up.shape[1]
    shapes = [
        ((rows, D), jnp.bfloat16),
        ((rows, D), jnp.float32),
        ((rows, D), jnp.bfloat16),
        ((rows, D), jnp.float32),
        ((rows, 128), jnp.float32),
        ((2, rows, wide // 2), jnp.bfloat16),
        ((rows, wide), jnp.bfloat16),
        ((2, rows, D // 2), jnp.bfloat16),
        ((2, rows, D // 2), jnp.bfloat16),
        ((2, rows, D // 2), jnp.bfloat16),
        ((8, D), jnp.float32),
    ]
    specs = [parted(s[2]) if len(s) == 3 else tiled(s[1]) for s, _ in shapes[:-1]]
    return pl.pallas_call(
        functools.partial(middle_forward_kernel, blocks),
        grid=(rows // TILE,),
        out_shape=[jax.ShapeDtypeStruct(*s) for s in shapes],
        in_specs=[pl.BlockSpec(memory_space=pltpu.SMEM)]
        + [tiled(D)] * 3
        + [resident(w.shape) for w in (w_out, w_up, w_down, vectors, bias_up)],
        out_specs=specs + [pl.BlockSpec((8, D), lambda i: (0, 0))],
        cost_estimate=pl.CostEstimate(
            flops=2 * rows * (D * D + 2 * D * wide),
            bytes_accessed=60 << 20,
            transcendentals=2 * rows * wide,
        ),
        compiler_params=pltpu.CompilerParams(vmem_limit_bytes=60 << 20),
    )(core, mixed, tokens, cotangent, w_out, w_up, w_down, vectors, bias_up)


def middle_backward(grad_low, grad_sum, slope, normed, scale, w_out, w_up, w_down, vectors):
    rows, wide = grad_low.shape[0], w_up.shape[1]
    shapes = [
        ((rows, wide), jnp.bfloat16),
        ((rows, D), jnp.float32),
        ((rows, D), jnp.bfloat16),
        ((rows, D), jnp.bfloat16),
    ]
    last = [((8, D), jnp.float32), ((1, wide), jnp.float32)]
    return pl.pallas_call(
        middle_backward_kernel,
        grid=(rows // TILE,),
        out_shape=[jax.ShapeDtypeStruct(*s) for s in shapes + last],
        in_specs=[tiled(v.shape[1]) for v in (grad_low, grad_sum, slope, normed, scale)]
        + [resident(w.shape) for w in (w_out, w_up, w_down, vectors)],
        out_specs=[tiled(s[1]) for s, _ in shapes]
        + [pl.BlockSpec(s, lambda i: (0, 0)) for s, _ in last],
        cost_estimate=pl.CostEstimate(
            flops=2 * rows * (D * D + 2 * D * wide), bytes_accessed=60 << 20, transcendentals=0
        ),
        compiler_params=pltpu.CompilerParams(vmem_limit_bytes=60 << 20),
    )(grad_low, grad_sum, slope, normed, scale, w_out, w_up, w_down, vectors)


class Grid:
    def __init__(self, mesh):
        self.shape = dict(mesh.shape)
        self.xs = self.shape["dp"] // CORES
        self.ys = self.xs
        self.zs = self.shape["fsdp"] // self.ys
        self.sizes = {"x": self.xs, "c": CORES, "z": self.zs, "y": self.ys}
        self.count = self.shape["dp"] * self.shape["fsdp"]
        self.pairs = self.xs == 2 and self.ys == 2

    def at(self):
        dp, fsdp = lax.axis_index("dp"), lax.axis_index("fsdp")
        return {"x": dp // CORES, "c": dp % CORES, "z": fsdp // self.ys, "y": fsdp % self.ys}

    def shifted(self, axis, step, wrap):
        hops = []
        for x in range(self.xs):
            for c in range(CORES):
                for z in range(self.zs):
                    for y in range(self.ys):
                        to = {"x": x, "c": c, "z": z, "y": y}
                        to[axis] += step
                        if wrap:
                            to[axis] %= self.sizes[axis]
                        elif not 0 <= to[axis] < self.sizes[axis]:
                            continue
                        hops.append((self.number(x, c, z, y), self.number(**to)))
        return hops

    def number(self, x, c, z, y):
        return ((x * CORES + c) * self.zs + z) * self.ys + y

    def swap(self, values, axis):
        return lax.ppermute(values, AXES, self.shifted(axis, 1, True))

    def along(self, values, axis, step):
        return lax.ppermute(values, AXES, self.shifted(axis, step, False))


def line_gather(grid, at, shard):
    up, down = [shard], [shard]
    for _ in range(grid.zs - 1):
        up.append(grid.along(up[-1], "z", 1))
        down.append(grid.along(down[-1], "z", -1))
    line = jnp.stack(up[:0:-1] + [shard] + down[1:])
    return lax.dynamic_slice_in_dim(line, grid.zs - 1 - at["z"], grid.zs, 0)


def own_swaps(grid, block, first, second):
    return grid.swap(block, first), grid.swap(block, second)


def pair_gather(grid, block, swapped, first, second):
    near, far = swapped
    pieces = {(0, 0): block, (1, 0): near, (0, 1): far, (1, 1): grid.swap(near, second)}
    found = {}
    for (one, two), piece in pieces.items():
        flips = {first: one, second: two}
        found[(flips["x"], 0, flips["y"])] = piece
        found[(flips["x"], 1, flips["y"])] = grid.swap(piece, "c")
    return found


def assemble_kernel(plan, grid, count, outs, spot, *refs):
    pieces, whole, sem = refs[:count], refs[count : count + outs], refs[-1]
    copies = []
    for source, (flip, out, rows, columns, start) in enumerate_plan(plan):
        x, c, y = ((spot[i] + flip[i]) % 2 for i in range(3))
        copies.append(
            pltpu.make_async_copy(
                pieces[source].at[:, pl.ds(start, rows), :],
                whole[out].at[x, c, :, y, :, pl.ds(columns[0], columns[1])],
                sem.at[len(copies)],
            )
        )
    for copy in copies:
        copy.start()
    for copy in copies:
        copy.wait()


def enumerate_plan(plan):
    for source, (flip, targets) in enumerate(plan):
        for out, rows, columns, start in targets:
            yield source, (flip, out, rows, columns, start)


def assemble(grid, at, parts, shapes):
    plan, arrays = [], []
    for pieces, targets in parts:
        for flip, piece in pieces.items():
            plan.append((flip, targets))
            arrays.append(piece)
    copies = sum(len(targets) for _, targets in plan)
    spot = jnp.stack([at["x"], at["c"], at["y"]]).astype(jnp.int32)
    outs = [
        jax.ShapeDtypeStruct((grid.xs, CORES, grid.zs, grid.ys) + shape, jnp.bfloat16)
        for shape in shapes
    ]
    size = sum(2 * piece.size for piece in arrays)
    whole = pl.pallas_call(
        functools.partial(assemble_kernel, plan, grid, len(arrays), len(outs)),
        out_shape=outs,
        in_specs=[pl.BlockSpec(memory_space=pltpu.SMEM)]
        + [pl.BlockSpec(memory_space=pl.ANY)] * len(arrays),
        out_specs=[pl.BlockSpec(memory_space=pl.ANY)] * len(outs),
        scratch_shapes=[pltpu.SemaphoreType.DMA((copies,))],
        cost_estimate=pl.CostEstimate(flops=0, bytes_accessed=2 * size, transcendentals=0),
        compiler_params=pltpu.CompilerParams(vmem_limit_bytes=1 << 20),
    )(spot, *arrays)
    return [w.reshape(grid.count * s[0], s[1]) for w, s in zip(whole, shapes)]


def take(values, index, axis):
    return lax.dynamic_index_in_dim(values, index, axis, keepdims=False)


def total(terms):
    result = terms[0].astype(jnp.float32)
    for term in terms[1:]:
        result = result + term.astype(jnp.float32)
    return result


class Chain:
    def __init__(self, grid, at, sent, kept):
        self.grid, self.at = grid, at
        got = grid.swap(sent, "c")
        shape = (grid.xs, grid.zs, grid.ys, -1, sent.shape[1])
        self.terms = [kept.reshape(shape), got.reshape(shape)]
        self.cut = sent.shape[1] // 256 * 128

    def first(self):
        self.left = [term[..., : self.cut] for term in self.terms]
        self.right = [term[..., self.cut :] for term in self.terms]
        return self.give("x", 0, "y", 2)

    def give(self, left_name, left_axis, right_name, right_axis):
        self.names = (left_name, left_axis, right_name, right_axis)
        sent = []
        for terms, name, axis in (
            (self.left, left_name, left_axis),
            (self.right, right_name, right_axis),
        ):
            values = total([take(term, 1 - self.at[name], axis) for term in terms])
            sent.append(values.astype(jnp.bfloat16))
        return tuple(sent)

    def get(self, sent):
        left_name, left_axis, right_name, right_axis = self.names
        self.left = [take(term, self.at[left_name], left_axis) for term in self.left]
        self.left.append(self.grid.swap(sent[0], left_name))
        self.right = [take(term, self.at[right_name], right_axis) for term in self.right]
        self.right.append(self.grid.swap(sent[1], right_name))

    def second(self, sent):
        self.get(sent)
        return self.give("y", 1, "x", 0)

    def line(self, sent):
        self.get(sent)
        joined = jnp.concatenate([total(self.left), total(self.right)], axis=-1)
        return joined.astype(jnp.bfloat16)


def line_reduce(grid, at, block):
    size = grid.zs

    def own(index):
        return take(block, jnp.clip(index, 0, size - 1), 0).astype(jnp.float32)

    up = low = None
    for step in range(1, size):
        up_sum, low_sum = own(at["z"] + size - step), own(at["z"] - size + step)
        if step > 1:
            up_sum, low_sum = up_sum + up.astype(jnp.float32), low_sum + low.astype(jnp.float32)
        up = grid.along(up_sum.astype(jnp.bfloat16), "z", 1)
        low = grid.along(low_sum.astype(jnp.bfloat16), "z", -1)
    return own(at["z"]) + up.astype(jnp.float32) + low.astype(jnp.float32)


def by_halves(parts):
    return jnp.concatenate([p[:, i : i + HALF] for i in (0, HALF) for p in parts], axis=1)


def pack_small(smalls, rows):
    flat = jnp.concatenate(smalls)
    return jnp.pad(flat, (0, rows * 128 - flat.size)).reshape(rows, 128)


def gather_first(grid, at, attn, smalls):
    rows = attn[0].shape[0]
    line = line_gather(
        grid, at, jnp.concatenate([by_halves(attn), pack_small(smalls, rows)], axis=1)
    )
    return line


def gather_attention(grid, at, line, rows):
    columns = line.shape[2]
    cut = (columns // 256) * 128
    left, right = line[:, :, :cut], line[:, :, cut:]
    left = pair_gather(grid, left, own_swaps(grid, left, "y", "x"), "y", "x")
    right = pair_gather(grid, right, own_swaps(grid, right, "x", "y"), "x", "y")
    (full,) = assemble(
        grid,
        at,
        [(left, [(0, rows, (0, cut), 0)]), (right, [(0, rows, (cut, columns - cut), 0)])],
        [(rows, columns)],
    )
    return full[:, : 3 * D], full[:, 3 * D :].reshape(grid.count, -1)


def gather_rest(grid, at, line, swaps, rows, lower, wide):
    split = rows + lower
    down_part = pair_gather(grid, line[:, :split], swaps[0], "y", "x")
    up_part = pair_gather(grid, line[:, split:], swaps[1], "x", "y")
    up_targets = [(1, rows, (i * D, D), i * rows) for i in range(wide // D)]
    return assemble(
        grid,
        at,
        [
            (down_part, [(0, rows, (0, D), 0), (2, lower, (0, D), rows)]),
            (up_part, up_targets),
        ],
        [(rows, D), (rows, wide), (lower, D)],
    )


def split_small(small, widths):
    results, start = [], 0
    for width in widths:
        results.append(small[:, start : start + width].reshape(-1).astype(jnp.float32))
        start += width
    return results


def hold(later, *ready):
    return lax.optimization_barrier((later, *ready))


def halves(parts, right):
    return tuple(outer_sum(parts[i], right).astype(jnp.bfloat16) for i in range(2))


def plain_reduce(grid, parts, right):
    both = [outer_sum(parts[i], right).reshape(grid.xs, -1, right.shape[1]) for i in (1, 0)]
    whole = jnp.stack(both, axis=1).reshape(-1, right.shape[1])
    return lax.psum_scatter(whole, AXES, scatter_dimension=0, tiled=True)


def per_device(
    grid,
    tokens,
    segment_ids,
    w_query,
    b_query,
    w_key,
    w_value,
    b_value,
    w_out,
    b_out,
    ln1_gain,
    ln1_bias,
    w_up,
    b_up,
    w_down,
    b_down,
    ln2_gain,
    ln2_bias,
    out_cotangent,
):
    at = grid.at()
    rows, wide = w_up.shape
    lower = w_down.shape[0]
    smalls = (b_query, b_value, b_out, ln1_gain, ln1_bias, b_down, ln2_gain, ln2_bias, b_up)
    widths = [small.shape[0] for small in smalls]
    attn = (w_query, w_key, w_value)
    low_tokens = tokens
    if grid.pairs:
        first = gather_first(grid, at, attn, smalls)
        rest = [w_out, w_down] + [w_up[:, i : i + D] for i in range(0, wide, D)]
        rest, first = hold(jnp.concatenate(rest, axis=0), first)
        line = line_gather(grid, at, rest)
        full_qkv, small = gather_attention(grid, at, first, rows)
        low_tokens, line = hold(tokens, line)
        split = rows + lower
        swaps = [
            own_swaps(grid, line[:, :split], "y", "x"),
            own_swaps(grid, line[:, split:], "x", "y"),
        ]
    else:
        full_qkv, full_out, full_up, full_down = (
            lax.all_gather(w, AXES, axis=0, tiled=True)
            for w in (by_halves(attn), w_out, w_up, w_down)
        )
        small = lax.all_gather(jnp.concatenate(smalls), AXES, axis=0, tiled=True)
        small = small.reshape(grid.count, -1)
    bias_query, bias_value, *others, bias_up = split_small(small, widths)
    vectors = jnp.stack(others + [jnp.zeros_like(bias_query)] * 2)
    doc_row, doc_column = segment_ids[:, None, :], segment_ids[:, :, None]
    biases = (bias_query, jnp.zeros_like(bias_query), bias_value)
    bias_qkv = by_halves([bias[None] for bias in biases])
    qkv = (matmul(low_tokens, full_qkv) + bias_qkv).astype(jnp.bfloat16)
    mixed = attend_forward(qkv, doc_column, doc_row)
    if grid.pairs:
        swaps, mixed = hold(swaps, mixed)
        full_out, full_up, full_down = gather_rest(grid, at, line, swaps, rows, lower, wide)
    core = at["c"] if grid.pairs else at["c"] * 0
    blocks = grid.xs * CORES
    (
        output,
        grad_sum,
        grad_low,
        normed,
        scale,
        active_parts,
        slope,
        first_parts,
        mixed_parts,
        token_parts,
        sums_two,
    ) = middle_forward(
        core.reshape(1).astype(jnp.int32),
        blocks,
        mixed,
        tokens,
        out_cotangent,
        full_out,
        full_up,
        full_down,
        vectors,
        bias_up.reshape(1, -1),
    )
    kept = (slope, normed, scale, full_out, full_up, full_down, vectors)
    if grid.pairs:
        down_chain = Chain(grid, at, *halves(active_parts, grad_low))
        down_sent = down_chain.first()
        grad_low, down_sent = hold(grad_low, down_sent)
    grad_up, grad_hidden, branch, grad_mixed, sums_one, sums_up = middle_backward(
        grad_low, grad_sum, *kept
    )
    if grid.pairs:
        up_chain = Chain(grid, at, *halves(first_parts, grad_up))
        down_sent = down_chain.second(down_sent)
        up_sent = up_chain.first()
        grad_mixed, up_sent, down_sent = hold(grad_mixed, up_sent, down_sent)
    one, sums_first = attend_backward(qkv, grad_mixed, doc_column, doc_row, 0)
    if grid.pairs:
        up_sent = up_chain.second(up_sent)
        of_qkv, of_out = halves(token_parts, one), halves(mixed_parts, branch)
        early = [jnp.concatenate([of_qkv[i], of_out[i]], axis=1) for i in range(2)]
        early_chain = Chain(grid, at, *early)
        early_sent = early_chain.first()
        grad_mixed, up_sent, early_sent = hold(grad_mixed, up_sent, early_sent)
    two, sums_second = attend_backward(qkv, grad_mixed, doc_column, doc_row, 1)
    sums_first, sums_second = sums_first[0], sums_second[0]
    totals = [
        jnp.concatenate([sums_first[:HALF], sums_second[:HALF]]),
        jnp.concatenate([sums_first[2 * HALF :], sums_second[2 * HALF :]]),
        sums_one[2],
        sums_one[0],
        sums_one[1],
        sums_up[0],
        sums_two[2],
        sums_two[0],
        sums_two[1],
    ]
    if grid.pairs:
        packed = jnp.concatenate([v.reshape(grid.count, -1) for v in totals], axis=1)
        widths = [v.size // grid.count for v in totals]
        packed = jnp.pad(packed, ((0, 0), (0, rows * 128 - sum(widths)))).astype(jnp.bfloat16)
        packed = packed.reshape(grid.xs, CORES, -1, 128)
        ends = [take(packed, core_at, 1).reshape(-1, 128) for core_at in (1 - at["c"], at["c"])]
        of_qkv = halves(token_parts, two)
        late = [jnp.concatenate([of_qkv[i], ends[i]], axis=1) for i in range(2)]
        late_chain = Chain(grid, at, *late)
        late_sent = late_chain.first()
        two, late_sent = hold(two, late_sent)
        down_block, up_block = down_chain.line(down_sent), up_chain.line(up_sent)
        up_rows = [up_block[:, :, i : i + D] for i in range(0, wide, D)]
        block = line_reduce(grid, at, jnp.concatenate([down_block] + up_rows, axis=1))
        share_down = block[:lower]
        up_rows = [block[i : i + rows] for i in range(lower, lower + rows * wide // D, rows)]
        share_up = jnp.concatenate(up_rows, axis=1)
        early_block = early_chain.line(early_chain.second(early_sent))
        late_block = late_chain.line(late_chain.second(late_sent))
        block = line_reduce(grid, at, jnp.concatenate([early_block, late_block], axis=2))
        early, share_out = block[:, : 3 * HALF], block[:, 3 * HALF : 5 * HALF]
        late = block[:, 5 * HALF :]
        flat = late[:, 3 * HALF :].reshape(-1)
        shares, start = [], 0
        for width in widths:
            shares.append(flat[start : start + width])
            start += width
    else:
        share_down = plain_reduce(grid, active_parts, grad_low)
        share_up = plain_reduce(grid, first_parts, grad_up)
        share_out = plain_reduce(grid, mixed_parts, branch)
        early, late = plain_reduce(grid, token_parts, one), plain_reduce(grid, token_parts, two)
        shares = [lax.psum_scatter(v, AXES, scatter_dimension=0, tiled=True) for v in totals]
    share_query, share_key, share_value = (
        jnp.concatenate([part[:, i : i + HALF] for part in (early, late)], axis=1)
        for i in range(0, 3 * HALF, HALF)
    )
    tokens_grad = (
        grad_hidden
        + back_matmul(one, full_qkv[:, : 3 * HALF])
        + back_matmul(two, full_qkv[:, 3 * HALF :])
    ).astype(jnp.bfloat16)
    return (
        output,
        tokens_grad,
        share_query,
        shares[0],
        share_key,
        share_value,
        shares[1],
        share_out,
        *shares[2:5],
        share_up,
        shares[5],
        share_down,
        *shares[6:],
    )


def solution(mesh):
    rows, flat = P(AXES, None), P(AXES)
    in_specs = (rows,) * 3 + (flat, rows, rows, flat, rows, flat, flat, flat, rows, flat, rows)
    in_specs += (flat,) * 3 + (rows,)
    out_specs = (rows,) * 3 + (flat, rows, rows, flat, rows, flat, flat, flat, rows, flat, rows)
    out_specs += (flat,) * 3
    return jax.shard_map(
        functools.partial(per_device, Grid(mesh)),
        mesh=mesh,
        in_specs=in_specs,
        out_specs=out_specs,
        check_vma=False,
    )
```

time: 918 us -> 601 us (0.65)
  matrix products: 280 us -> 71.9 us
  local copies, waits for them, and re-layouts: 224 us -> 73.8 us
  Pallas kernels: 13.9 us -> 156 us
  starting transfers between devices: 172 us -> 98.9 us
  other arithmetic: 97.3 us -> 33.7 us
  waiting for transfers between devices: 119 us -> 155 us
    pallas_call x0 -> x5, Pallas kernels: none -> 148 us  [the longest x2 47 us: attend_backward(): pl.pallas_call(attend_backward_kernel, grid=(seqs, PAIRS), out_shape=[jax...]
    dot_general x14 -> x0, matrix products: 109 us -> none  [the longest x4 44.1 us: masked_scores(): jnp.einsum('qhd,khd->hqk', query_rows, key_rows, preferred_element_type=j...]
    ppermute x54 -> x24, starting transfers between devices: 147 us -> 68.7 us  [along(): return lax.ppermute(values, AXES, self.shifted(axis, step, False))]
    dot_general x4 -> x1, matrix products: 74.2 us -> 7.07 us  [matmul(): return jnp.dot(operand, other, preferred_element_type=jnp.float32)]
    ppermute x45 -> x48, waiting for transfers between devices: 65.4 us -> 119 us  [swap(): return lax.ppermute(values, AXES, self.shifted(axis, 1, True))]
    unnamed x231 -> x163, local copies, waits for them, and re-layouts: 91.6 us -> 44.7 us
    dynamic_slice x5 -> x2, local copies, waits for them, and re-layouts: 40.7 us -> 0.11 us  [take(): return lax.dynamic_index_in_dim(values, index, axis, keepdims=False)]
    dot_general x4 -> x2, matrix products: 48.6 us -> 13.5 us  [back_matmul(): lax.dot_general(operand, other, (((1,), (1,)), ((), ())), preferred_eleme...]
  transfers between devices with their start and end apart: 99 -> 72, of which waited for: 28 -> 31; matrix products, arithmetic and copies ran while one was open for 25% -> 14% of each run, Pallas kernels for 1% -> 4%
where the time goes in v2:
time: 601 us; the launch traced here: 592 us
  Pallas kernels  156 us (26%)
  waiting for transfers between devices  155 us (26%)
  starting transfers between devices  98.9 us (16%)
  local copies, waits for them, and re-layouts  73.8 us (12%)
  matrix products  71.9 us (12%)
  other arithmetic  33.7 us (6%)
    ppermute x48, waiting for transfers between devices, swap(): return lax.ppermute(values, AXES, self.shifted(axis, 1, True))  119 us
    ppermute x24, starting transfers between devices, along(): return lax.ppermute(values, AXES, self.shifted(axis, step, False))  68.7 us
    dot_general x10, matrix products, outer_sum(): lax.dot_general(operand, other, (((0,), (0,)), ((), ())), preferred_eleme...  51.3 us
    pallas_call x2, Pallas kernels, attend_backward(): pl.pallas_call(attend_backward_kernel, grid=(seqs, PAIRS), out_shape=[jax...  47 us
    unnamed x163, local copies, waits for them, and re-layouts  44.7 us
    pallas_call x1, Pallas kernels, middle_forward(): pl.pallas_call(functools.partial(middle_forward_kernel, blocks), grid=(ro...  43.9 us
    ppermute x24, waiting for transfers between devices, along(): return lax.ppermute(values, AXES, self.shifted(axis, step, False))  35.6 us
    pallas_call x1, Pallas kernels, middle_backward(): pl.pallas_call(middle_backward_kernel, grid=(rows // TILE,), out_shape=[j...  34.6 us
  transfers between devices with their start and end apart: 72, of which 31 were waited for; matrix products, arithmetic and copies ran while one was open for 14% of the time, Pallas kernels for 4%

profile of v2, /device:TPU:0, one launch (start us, length us, event | category | flops | bytes accessed | tf_op | source)
XLA Modules:
  0.0 592.0 jit_solution(6177088908505289381)
XLA Ops:
  5.2 6.1 %concatenate.81 = bf16[384]{0:T(512)(128)(2,1)S(1)} concatenate(bf16[32]{0:T(256)(128)(2,1)} %param.21, bf16[32]{0:T(256)(128)(2,1)} %param.24, bf16[32]{0:T(256)(128)(2,1)} %param.26, bf16[32]{0:T(256)(128)(2,1)} %param.27, bf16[32]{0:T(256)(128)(2,1)} %param.28, bf16[32]{0:T(256)(128)(2,1)} %param.32, bf16[32]{0:T(256)(128)(2,1)} %param.33, bf16[32]{0:T(256)(128)(2,1)} %param.34, ...), dimensions={0} | concatenate | bytes 1536 | tf_op jit(solution)/shard_map/concatenate | solution.py:545
  12.6 5.6 collective-permute-start
  38.1 5.1 collective-permute-done.5
  47.6 4.9 collective-permute-done.19.refs_4_
  68.7 5.5 collective-permute-done.21.refs_6_
  80.9 5.2 collective-permute-done.10
  90.4 5.2 collective-permute-start.8
  118.3 7.1 %add_convert_fusion.query.key.value = bf16[1024,3072]{1,0:T(8,128)(2,1)S(1)} fusion(f32[3072]{0:T(1024)S(1)} %bitcast.346, bf16[1024,1024]{1,0:T(8,128)(2,1)S(1)} %copy-done.54, bf16[1024,3200]{1,0:T(8,128)(2,1)S(1)} %bitcast.323), kind=kOutput, calls=%fused_computation | convolution fusion | flops 6448742400 | bytes 14692352 | tf_op jit(solution)/shard_map/dot_general | solution.py:19
  125.4 22.9 %shard_map.306.mixed = bf16[1024,1024]{1,0:T(8,128)(2,1)S(1)} custom-call(bf16[1024,3072]{1,0:T(8,128)(2,1)S(1)} %add_convert_fusion.query.key.value, bf16[1024,3072]{1,0:T(8,128)(2,1)S(1)} %add_convert_fusion.query.key.value, bf16[1024,3072]{1,0:T(8,128)(2,1)S(1)} %add_convert_fusion.query.key.value, s32[2,512,1]{2,1,0:T(8,128)S(1)} %copy-done.7, ...), custom_call_target="tpu_custom_call" | custom-call | flops 8589934592 | bytes 25165824 | tf_op jit(solution)/shard_map/pallas_call | solution.py:132
  149.7 17.3 %collective-permute-done.13.refs_4_ = bf16[4,160,1024]{2,1,0:T(8,128)(2,1)} collective-permute-done((bf16[4,160,1024]{2,1,0:T(8,128)(2,1)S(1)}, bf16[4,160,1024]{2,1,0:T(8,128)(2,1)}, u32[]{:S(2)}, u32[]{:S(2)}) %collective-permute-start.13) | collective-permute-done | bytes 1310752 | tf_op jit(solution)/shard_map/ppermute | solution.py:392
  172.7 22.0 %collective-permute-done.33.refs_6_ = bf16[4,160,1024]{2,1,0:T(8,128)(2,1)} collective-permute-done((bf16[4,160,1024]{2,1,0:T(8,128)(2,1)}, bf16[4,160,1024]{2,1,0:T(8,128)(2,1)}, u32[]{:S(2)}, u32[]{:S(2)}) %collective-permute-start.33) | collective-permute-done | bytes 1310752 | tf_op jit(solution)/shard_map/ppermute | solution.py:392
  204.9 5.7 shard_map.307
  218.6 43.9 %shard_map.308 = (bf16[1024,1024]{1,0:T(8,128)(2,1)}, f32[1024,1024]{1,0:T(8,128)}, bf16[1024,1024]{1,0:T(8,128)(2,1)}, f32[1024,1024]{1,0:T(8,128)}, f32[1024,1...) custom-call(s32[1]{0:T(128)} %bitcast.spot, ...), custom_call_target="tpu_custom_call" | custom-call | flops 19327352832 | bytes 62914560 | tf_op jit(solution)/shard_map/pallas_call | solution.py:318
  262.5 9.5 %fusion.13 = bf16[2048,1024]{1,0:T(8,128)(2,1)} fusion(bf16[1024,1024]{1,0:T(8,128)(2,1)} %get-tuple-element.81.grad_low, bf16[2,1024,2048]{2,1,0:T(8,128)(2,1)} %get-tuple-element.80), kind=kOutput, calls=%fused_computation.13 | convolution fusion | flops 4297064448 | bytes 10485760 | tf_op jit(solution)/shard_map/dot_general | solution.py:29
  272.2 7.4 %fusion.10 = bf16[2048,1024]{1,0:T(8,128)(2,1)S(1)} fusion(bf16[1024,1024]{1,0:T(8,128)(2,1)S(1)} %copy-done.63, bf16[2,1024,2048]{2,1,0:T(8,128)(2,1)} %get-tuple-element.80), kind=kOutput, calls=%fused_computation.12 | convolution fusion | flops 4297064448 | bytes 10485760 | tf_op jit(solution)/shard_map/dot_general | solution.py:29
  286.5 34.6 %shard_map.309 = (bf16[1024,4096]{1,0:T(8,128)(2,1)}, f32[1024,1024]{1,0:T(8,128)}, bf16[1024,1024]{1,0:T(8,128)(2,1)}, bf16[1024,1024]{1,0:T(8,128)(2,1)}, f32[8,1024]{1,0:T(8,128)}, /*index=5*/f32[1,4096]{1,0:T(1,128)}) custom-call(bf16[1024,1024]{1,0:T(8,128)(2,1)} %get-tuple-element.81.grad_low, f32[1024,1024]{1,0:T(8,128)} %get-tuple-element.82.grad_sum, ...), custom_call_target="tpu_custom_call" | custom-call | flops 19327352832 | bytes 62914560 | tf_op jit(solution)/shard_map/pallas_call | solution.py:344
  321.2 10.4 %convolution_convert_fusion = bf16[512,4096]{1,0:T(8,128)(2,1)} fusion(bf16[1024,4096]{1,0:T(8,128)(2,1)} %get-tuple-element.89, bf16[2,1024,512]{2,1,0:T(8,128)(2,1)} %get-tuple-element.88), kind=kOutput, calls=%fused_computation.3 | convolution fusion | flops 4297064448 | bytes 13631488 | tf_op jit(solution)/shard_map/dot_general | solution.py:29
  336.3 8.3 %convolution_convert_fusion.1 = bf16[512,4096]{1,0:T(8,128)(2,1)S(1)} fusion(bf16[1024,4096]{1,0:T(8,128)(2,1)} %get-tuple-element.89, bf16[2,1024,512]{2,1,0:T(8,128)(2,1)S(1)} %copy-done.60), kind=kOutput, calls=%fused_computation.4 | convolution fusion | flops 4297064448 | bytes 13631488 | tf_op jit(solution)/shard_map/dot_general | solution.py:29
  346.7 11.3 %collective-permute-done.42 = bf16[4,2,128,512]{3,2,0,1:T(8,128)(2,1)S(1)} collective-permute-done((bf16[4,2,128,512]{3,2,0,1:T(8,128)(2,1)}, bf16[4,2,128,512]{3,2,0,1:T(8,128)(2,1)S(1)}, u32[]{:S(2)}, u32[]{:S(2)}) %collective-permute-start.42) | collective-permute-done | bytes 1048608 | tf_op jit(solution)/shard_map/ppermute | solution.py:392
  369.1 23.4 %shard_map.310 = (bf16[1024,1536]{1,0:T(8,128)(2,1)}, f32[1,1536]{1,0:T(1,128)S(1)}) custom-call(bf16[1024,3072]{1,0:T(8,128)(2,1)} %copy-done.22, bf16[1024,3072]{1,0:T(8,128)(2,1)} %copy-done.22, bf16[1024,3072]{1,0:T(8,128)(2,1)} %copy-done.22, bf16[1024,1024]{1,0:T(8,128)(2,1)S(1)} %copy-done.24, s32[2,512,1]{2,1,0:T(8,128)S(1)} %copy-done.8, ...), custom_call_target="tpu_custom_call" | custom-call | flops 10737418240 | bytes 25165824 | tf_op jit(solution)/shard_map/pallas_call | solution.py:149
  404.5 6.9 %fusion.18 = f32[1024,1024]{1,0:T(8,128)} fusion(bf16[1024,1536]{1,0:T(8,128)(2,1)S(1)} %copy-done.57, bf16[1024,3200]{1,0:T(8,128)(2,1)} %bitcast.319), kind=kOutput, calls=%fused_computation.16 | convolution fusion | flops 3221225472 | bytes 10485760 | tf_op jit(solution)/shard_map/dot_general | solution.py:23
  418.3 16.2 %collective-permute-done.44 = bf16[4,2,32,2048]{3,2,0,1:T(8,128)(2,1)} collective-permute-done((bf16[4,2,32,2048]{3,2,0,1:T(8,128)(2,1)}, bf16[4,2,32,2048]{3,2,0,1:T(8,128)(2,1)}, u32[]{:S(2)}, u32[]{:S(2)}) %collective-permute-start.44) | collective-permute-done | bytes 1048608 | tf_op jit(solution)/shard_map/ppermute | solution.py:392
  444.8 23.6 %shard_map.311 = (bf16[1024,1536]{1,0:T(8,128)(2,1)}, f32[1,1536]{1,0:T(1,128)S(1)}) custom-call(bf16[1024,3072]{1,0:T(8,128)(2,1)} %copy-done.22, bf16[1024,3072]{1,0:T(8,128)(2,1)} %copy-done.22, bf16[1024,3072]{1,0:T(8,128)(2,1)} %copy-done.22, bf16[1024,1024]{1,0:T(8,128)(2,1)S(1)} %copy-done.24, s32[2,512,1]{2,1,0:T(8,128)S(1)} %copy-done.8, ...), custom_call_target="tpu_custom_call" | custom-call | flops 10737418240 | bytes 25165824 | tf_op jit(solution)/shard_map/pallas_call | solution.py:149
  480.7 8.7 %collective-permute-done.64 = bf16[4,32,2048]{2,1,0:T(8,128)(2,1)} collective-permute-done((bf16[4,32,2048]{2,1,0:T(8,128)(2,1)}, bf16[4,32,2048]{2,1,0:T(8,128)(2,1)}, u32[]{:S(2)}, u32[]{:S(2)}) %collective-permute-start.64) | collective-permute-done | bytes 524320 | tf_op jit(solution)/shard_map/ppermute | solution.py:392
  494.7 9.0 %collective-permute-done.48 = bf16[4,2,32,1280]{3,2,0,1:T(8,128)(2,1)S(1)} collective-permute-done((bf16[4,2,32,1280]{3,2,0,1:T(8,128)(2,1)}, bf16[4,2,32,1280]{3,2,0,1:T(8,128)(2,1)S(1)}, u32[]{:S(2)}, u32[]{:S(2)}) %collective-permute-start.48) | collective-permute-done | bytes 655392 | tf_op jit(solution)/shard_map/ppermute | solution.py:392
  504.5 4.4 collective-permute-start.66
  514.6 6.0 %collective-permute-done.51 = bf16[4,32,1280]{2,1,0:T(8,128)(2,1)S(1)} collective-permute-done((bf16[4,32,1280]{2,1,0:T(8,128)(2,1)S(1)}, bf16[4,32,1280]{2,1,0:T(8,128)(2,1)S(1)}, u32[]{:S(2)}, u32[]{:S(2)}) %collective-permute-start.51) | collective-permute-done | bytes 327712 | tf_op jit(solution)/shard_map/ppermute | solution.py:392
  531.9 5.3 collective-permute-done.55
  548.6 5.1 collective-permute-start.57
  553.8 6.6 %add_convert_fusion.1 = bf16[1024,1024]{1,0:T(8,128)(2,1)} fusion(f32[1024,1024]{1,0:T(8,128)S(1)} %copy-done.62, f32[1024,1024]{1,0:T(8,128)S(1)} %copy-done.61, bf16[1024,1536]{1,0:T(8,128)(2,1)S(1)} %copy-done.56, bf16[1024,3200]{1,0:T(8,128)(2,1)} %bitcast.320), kind=kOutput, calls=%fused_computation.9 | convolution fusion | flops 3224371200 | bytes 16777216 | tf_op jit(solution)/shard_map/dot_general | solution.py:23
  564.7 9.9 %collective-permute-done.71 = bf16[256,1024]{1,0:T(8,128)(2,1)S(1)} collective-permute-done((bf16[256,1024]{1,0:T(8,128)(2,1)S(1)}, bf16[256,1024]{1,0:T(8,128)(2,1)S(1)}, u32[]{:S(2)}, u32[]{:S(2)}) %collective-permute-start.71) | collective-permute-done | bytes 524320 | tf_op jit(solution)/shard_map/ppermute | solution.py:395
  583.1 4.5 collective-permute-done.61
  (411 shorter events, 221.8 us)
Async XLA Ops:
  11.3 16.4 %collective-permute-start.3 = (bf16[32,3200]{1,0:T(8,128)(2,1)S(1)}, bf16[32,3200]{1,0:T(8,128)(2,1)S(1)}, u32[]{:S(2)}, u32[]{:S(2)}) collective-permute-start(bf16[32,3200]{1,0:T(8,128)(2,1)S(1)} %constant_dynamic-update-slice_fusion.6), channel_id=1, source_target_pairs={{2,0},{3,1},{4,2},{5,3},{6,4},{7,5},{10,8},{11,9},{12,10},{13,11},... | collective-permute-start | bytes 614408 | tf_op jit(solution)/shard_map/ppermute | solution.py:395
  67.4 18.8 %collective-permute-start.10 = (bf16[288,1024]{1,0:T(8,128)(2,1)}, bf16[288,1024]{1,0:T(8,128)(2,1)}, u32[]{:S(2)}, u32[]{:S(2)}) collective-permute-start(bf16[288,1024]{1,0:T(8,128)(2,1)} %collective-permute-done.9), channel_id=1, source_target_pairs={{2,0},{3,1},{4,2},{5,3},{6,4},{7,5},{10,8},{11,9},{12,10},{13,11},... | collective-permute-start | bytes 1769480 | tf_op jit(solution)/shard_map/ppermute | solution.py:395
  74.2 16.2 %collective-permute-start.7 = (bf16[288,1024]{1,0:T(8,128)(2,1)}, bf16[288,1024]{1,0:T(8,128)(2,1)}, u32[]{:S(2)}, u32[]{:S(2)}) collective-permute-start(bf16[288,1024]{1,0:T(8,128)(2,1)} %collective-permute-done.6), channel_id=1, source_target_pairs={{0,2},{1,3},{2,4},{3,5},{4,6},{5,7},{8,10},{9,11},{10,12},{11,13},... | collective-permute-start | bytes 1769480 | tf_op jit(solution)/shard_map/ppermute | solution.py:395
  79.2 16.4 %collective-permute-start.25 = (bf16[4,32,1664]{2,1,0:T(8,128)(2,1)S(1)}, bf16[4,32,1664]{2,1,0:T(8,128)(2,1)S(1)}, u32[]{:S(2)}, u32[]{:S(2)}) collective-permute-start(bf16[4,32,1664]{2,1,0:T(8,128)(2,1)S(1)} %collective-permute-done.24.refs_10_), channel_id=1, source_target_pairs={{0,8},{1,9},{2,10},{3,11},{4,12},{5,13},{6,14},{7,15},{8,0},{9,1},... | collective-permute-start | bytes 1277960 | tf_op jit(solution)/shard_map/ppermute | solution.py:392
  79.2 16.4 %collective-permute-start.29 = (bf16[4,32,1664]{2,1,0:T(8,128)(2,1)S(1)}, bf16[4,32,1664]{2,1,0:T(8,128)(2,1)}, u32[]{:S(2)}, u32[]{:S(2)}) collective-permute-start(bf16[4,32,1664]{2,1,0:T(8,128)(2,1)S(1)} %collective-permute-done.28.refs_14_), channel_id=1, source_target_pairs={{0,8},{1,9},{2,10},{3,11},{4,12},{5,13},{6,14},{7,15},{8,0},{9,1},... | collective-permute-start | bytes 1277960 | tf_op jit(solution)/shard_map/ppermute | solution.py:392
  86.2 26.3 %collective-permute-start.11 = (bf16[288,1024]{1,0:T(8,128)(2,1)}, bf16[288,1024]{1,0:T(8,128)(2,1)}, u32[]{:S(2)}, u32[]{:S(2)}) collective-permute-start(bf16[288,1024]{1,0:T(8,128)(2,1)} %collective-permute-done.10), channel_id=1, source_target_pairs={{2,0},{3,1},{4,2},{5,3},{6,4},{7,5},{10,8},{11,9},{12,10},{13,11},... | collective-permute-start | bytes 1769480 | tf_op jit(solution)/shard_map/ppermute | solution.py:395
  90.4 16.3 %collective-permute-start.8 = (bf16[288,1024]{1,0:T(8,128)(2,1)}, bf16[288,1024]{1,0:T(8,128)(2,1)}, u32[]{:S(2)}, u32[]{:S(2)}) collective-permute-start(bf16[288,1024]{1,0:T(8,128)(2,1)} %collective-permute-done.7), channel_id=1, source_target_pairs={{0,2},{1,3},{2,4},{3,5},{4,6},{5,7},{8,10},{9,11},{10,12},{11,13},... | collective-permute-start | bytes 1769480 | tf_op jit(solution)/shard_map/ppermute | solution.py:395
  114.2 35.5 %collective-permute-start.15 = (bf16[4,128,1024]{2,1,0:T(8,128)(2,1)S(1)}, bf16[4,128,1024]{2,1,0:T(8,128)(2,1)S(1)}, u32[]{:S(2)}, u32[]{:S(2)}) collective-permute-start(bf16[4,128,1024]{2,1,0:T(8,128)(2,1)S(1)} %slice.318.refs_8_), channel_id=1, source_target_pairs={{0,1},{1,0},{2,3},{3,2},{4,5},{5,4},{6,7},{7,6},{8,9},{9,8},{10,11... | collective-permute-start | bytes 3145736 | tf_op jit(solution)/shard_map/ppermute | solution.py:392
  115.8 33.9 %collective-permute-start.14 = (bf16[4,128,1024]{2,1,0:T(8,128)(2,1)S(1)}, bf16[4,128,1024]{2,1,0:T(8,128)(2,1)}, u32[]{:S(2)}, u32[]{:S(2)}) collective-permute-start(bf16[4,128,1024]{2,1,0:T(8,128)(2,1)S(1)} %slice.318.refs_8_), channel_id=1, source_target_pairs={{0,16},{1,17},{2,18},{3,19},{4,20},{5,21},{6,22},{7,23},{8,24},{9,... | collective-permute-start | bytes 3145736 | tf_op jit(solution)/shard_map/ppermute | solution.py:392
  116.3 55.0 %collective-permute-start.30 = (bf16[4,160,1024]{2,1,0:T(8,128)(2,1)S(1)}, bf16[4,160,1024]{2,1,0:T(8,128)(2,1)S(1)}, u32[]{:S(2)}, u32[]{:S(2)}) collective-permute-start(bf16[4,160,1024]{2,1,0:T(8,128)(2,1)S(1)} %slice.317.refs_0_), channel_id=1, source_target_pairs={{0,8},{1,9},{2,10},{3,11},{4,12},{5,13},{6,14},{7,15},{8,0},{9,1},... | collective-permute-start | bytes 3932168 | tf_op jit(solution)/shard_map/ppermute | solution.py:392
  116.3 50.7 %collective-permute-start.13 = (bf16[4,160,1024]{2,1,0:T(8,128)(2,1)S(1)}, bf16[4,160,1024]{2,1,0:T(8,128)(2,1)}, u32[]{:S(2)}, u32[]{:S(2)}) collective-permute-start(bf16[4,160,1024]{2,1,0:T(8,128)(2,1)S(1)} %slice.317.refs_0_), channel_id=1, source_target_pairs={{0,16},{1,17},{2,18},{3,19},{4,20},{5,21},{6,22},{7,23},{8,24},{9,... | collective-permute-start | bytes 3932168 | tf_op jit(solution)/shard_map/ppermute | solution.py:392
  117.8 49.2 %collective-permute-start.12 = (bf16[4,160,1024]{2,1,0:T(8,128)(2,1)S(1)}, bf16[4,160,1024]{2,1,0:T(8,128)(2,1)}, u32[]{:S(2)}, u32[]{:S(2)}) collective-permute-start(bf16[4,160,1024]{2,1,0:T(8,128)(2,1)S(1)} %slice.317.refs_0_), channel_id=1, source_target_pairs={{0,1},{1,0},{2,3},{3,2},{4,5},{5,4},{6,7},{7,6},{8,9},{9,8},{10,11... | collective-permute-start | bytes 3932168 | tf_op jit(solution)/shard_map/ppermute | solution.py:392
  167.0 27.8 %collective-permute-start.33 = (bf16[4,160,1024]{2,1,0:T(8,128)(2,1)}, bf16[4,160,1024]{2,1,0:T(8,128)(2,1)}, u32[]{:S(2)}, u32[]{:S(2)}) collective-permute-start(bf16[4,160,1024]{2,1,0:T(8,128)(2,1)} %collective-permute-done.12.refs_2_), channel_id=1, source_target_pairs={{0,16},{1,17},{2,18},{3,19},{4,20},{5,21},{6,22},{7,23},{8,24},{9,... | collective-permute-start | bytes 3932168 | tf_op jit(solution)/shard_map/ppermute | solution.py:392
  167.5 27.2 %collective-permute-start.37 = (bf16[4,128,1024]{2,1,0:T(8,128)(2,1)S(1)}, bf16[4,128,1024]{2,1,0:T(8,128)(2,1)S(1)}, u32[]{:S(2)}, u32[]{:S(2)}) collective-permute-start(bf16[4,128,1024]{2,1,0:T(8,128)(2,1)S(1)} %collective-permute-done.15.refs_12_), channel_id=1, source_target_pairs={{0,8},{1,9},{2,10},{3,11},{4,12},{5,13},{6,14},{7,15},{8,0},{9,1},... | collective-permute-start | bytes 3145736 | tf_op jit(solution)/shard_map/ppermute | solution.py:392
  168.0 28.3 %collective-permute-start.38 = (bf16[4,128,1024]{2,1,0:T(8,128)(2,1)}, bf16[4,128,1024]{2,1,0:T(8,128)(2,1)}, u32[]{:S(2)}, u32[]{:S(2)}) collective-permute-start(bf16[4,128,1024]{2,1,0:T(8,128)(2,1)} %collective-permute-done.14.refs_10_), channel_id=1, source_target_pairs={{0,1},{1,0},{2,3},{3,2},{4,5},{5,4},{6,7},{7,6},{8,9},{9,8},{10,11... | collective-permute-start | bytes 3145736 | tf_op jit(solution)/shard_map/ppermute | solution.py:392
  171.2 28.5 %collective-permute-start.32 = (bf16[4,160,1024]{2,1,0:T(8,128)(2,1)}, bf16[4,160,1024]{2,1,0:T(8,128)(2,1)}, u32[]{:S(2)}, u32[]{:S(2)}) collective-permute-start(bf16[4,160,1024]{2,1,0:T(8,128)(2,1)} %collective-permute-done.13.refs_4_), channel_id=1, source_target_pairs={{0,8},{1,9},{2,10},{3,11},{4,12},{5,13},{6,14},{7,15},{8,0},{9,1},... | collective-permute-start | bytes 3932168 | tf_op jit(solution)/shard_map/ppermute | solution.py:392
  172.4 27.3 %collective-permute-start.31 = (bf16[4,160,1024]{2,1,0:T(8,128)(2,1)}, bf16[4,160,1024]{2,1,0:T(8,128)(2,1)}, u32[]{:S(2)}, u32[]{:S(2)}) collective-permute-start(bf16[4,160,1024]{2,1,0:T(8,128)(2,1)} %collective-permute-done.12.refs_2_), channel_id=1, source_target_pairs={{0,8},{1,9},{2,10},{3,11},{4,12},{5,13},{6,14},{7,15},{8,0},{9,1},... | collective-permute-start | bytes 3932168 | tf_op jit(solution)/shard_map/ppermute | solution.py:392
  331.6 30.8 %collective-permute-start.41 = (bf16[512,4096]{1,0:T(8,128)(2,1)}, bf16[512,4096]{1,0:T(8,128)(2,1)}, u32[]{:S(2)}, u32[]{:S(2)}) collective-permute-start(bf16[512,4096]{1,0:T(8,128)(2,1)} %convolution_convert_fusion), channel_id=1, source_target_pairs={{0,8},{1,9},{2,10},{3,11},{4,12},{5,13},{6,14},{7,15},{8,0},{9,1},... | collective-permute-start | bytes 12582920 | tf_op jit(solution)/shard_map/ppermute | solution.py:392
  332.6 25.4 %collective-permute-start.42 = (bf16[4,2,128,512]{3,2,0,1:T(8,128)(2,1)}, bf16[4,2,128,512]{3,2,0,1:T(8,128)(2,1)S(1)}, u32[]{:S(2)}, u32[]{:S(2)}) collective-permute-start(bf16[4,2,128,512]{3,2,0,1:T(8,128)(2,1)} %fusion.22), channel_id=1, source_target_pairs={{0,16},{1,17},{2,18},{3,19},{4,20},{5,21},{6,22},{7,23},{8,24},{9,... | collective-permute-start | bytes 3145736 | tf_op jit(solution)/shard_map/ppermute | solution.py:392
  333.1 27.5 %collective-permute-start.43 = (bf16[2,4,128,512]{3,2,1,0:T(8,128)(2,1)S(1)}, bf16[2,4,128,512]{3,2,1,0:T(8,128)(2,1)S(1)}, u32[]{:S(2)}, u32[]{:S(2)}) collective-permute-start(bf16[2,4,128,512]{3,2,1,0:T(8,128)(2,1)S(1)} %fusion.23), channel_id=1, source_target_pairs={{0,1},{1,0},{2,3},{3,2},{4,5},{5,4},{6,7},{7,6},{8,9},{9,8},{10,11... | collective-permute-start | bytes 3145736 | tf_op jit(solution)/shard_map/ppermute | solution.py:392
  399.1 16.5 %collective-permute-start.63 = (bf16[4,128,512]{2,1,0:T(8,128)(2,1)S(1)}, bf16[4,128,512]{2,1,0:T(8,128)(2,1)}, u32[]{:S(2)}, u32[]{:S(2)}) collective-permute-start(bf16[4,128,512]{2,1,0:T(8,128)(2,1)S(1)} %fusion.41), channel_id=1, source_target_pairs={{0,16},{1,17},{2,18},{3,19},{4,20},{5,21},{6,22},{7,23},{8,24},{9,... | collective-permute-start | bytes 1572872 | tf_op jit(solution)/shard_map/ppermute | solution.py:392
  399.6 34.9 %collective-permute-start.44 = (bf16[4,2,32,2048]{3,2,0,1:T(8,128)(2,1)}, bf16[4,2,32,2048]{3,2,0,1:T(8,128)(2,1)}, u32[]{:S(2)}, u32[]{:S(2)}) collective-permute-start(bf16[4,2,32,2048]{3,2,0,1:T(8,128)(2,1)} %fusion.24), channel_id=1, source_target_pairs={{0,16},{1,17},{2,18},{3,19},{4,20},{5,21},{6,22},{7,23},{8,24},{9,... | collective-permute-start | bytes 3145736 | tf_op jit(solution)/shard_map/ppermute | solution.py:392
  401.1 35.8 %collective-permute-start.45 = (bf16[2,4,32,2048]{3,2,1,0:T(8,128)(2,1)}, bf16[2,4,32,2048]{3,2,1,0:T(8,128)(2,1)}, u32[]{:S(2)}, u32[]{:S(2)}) collective-permute-start(bf16[2,4,32,2048]{3,2,1,0:T(8,128)(2,1)} %fusion.25), channel_id=1, source_target_pairs={{0,1},{1,0},{2,3},{3,2},{4,5},{5,4},{6,7},{7,6},{8,9},{9,8},{10,11... | collective-permute-start | bytes 3145736 | tf_op jit(solution)/shard_map/ppermute | solution.py:392
  404.3 35.0 %collective-permute-start.46 = (bf16[512,2560]{1,0:T(8,128)(2,1)}, bf16[512,2560]{1,0:T(8,128)(2,1)}, u32[]{:S(2)}, u32[]{:S(2)}) collective-permute-start(bf16[512,2560]{1,0:T(8,128)(2,1)} %pad_maximum_fusion.1), channel_id=1, source_target_pairs={{0,8},{1,9},{2,10},{3,11},{4,12},{5,13},{6,14},{7,15},{8,0},{9,1},... | collective-permute-start | bytes 7864328 | tf_op jit(solution)/shard_map/ppermute | solution.py:392
  478.3 25.4 %collective-permute-start.48 = (bf16[4,2,32,1280]{3,2,0,1:T(8,128)(2,1)}, bf16[4,2,32,1280]{3,2,0,1:T(8,128)(2,1)S(1)}, u32[]{:S(2)}, u32[]{:S(2)}) collective-permute-start(bf16[4,2,32,1280]{3,2,0,1:T(8,128)(2,1)} %fusion.59), channel_id=1, source_target_pairs={{0,16},{1,17},{2,18},{3,19},{4,20},{5,21},{6,22},{7,23},{8,24},{9,... | collective-permute-start | bytes 1966088 | tf_op jit(solution)/shard_map/ppermute | solution.py:392
  479.8 30.4 %collective-permute-start.50 = (bf16[2,4,32,1280]{3,2,1,0:T(8,128)(2,1)}, bf16[2,4,32,1280]{3,2,1,0:T(8,128)(2,1)S(1)}, u32[]{:S(2)}, u32[]{:S(2)}) collective-permute-start(bf16[2,4,32,1280]{3,2,1,0:T(8,128)(2,1)} %fusion.60), channel_id=1, source_target_pairs={{0,1},{1,0},{2,3},{3,2},{4,5},{5,4},{6,7},{7,6},{8,9},{9,8},{10,11... | collective-permute-start | bytes 1966088 | tf_op jit(solution)/shard_map/ppermute | solution.py:392
  480.6 30.6 %collective-permute-start.47 = (bf16[512,1664]{1,0:T(8,128)(2,1)S(1)}, bf16[512,1664]{1,0:T(8,128)(2,1)S(1)}, u32[]{:S(2)}, u32[]{:S(2)}) collective-permute-start(bf16[512,1664]{1,0:T(8,128)(2,1)S(1)} %pad_maximum_fusion.2), channel_id=1, source_target_pairs={{0,8},{1,9},{2,10},{3,11},{4,12},{5,13},{6,14},{7,15},{8,0},{9,1},... | collective-permute-start | bytes 5111816 | tf_op jit(solution)/shard_map/ppermute | solution.py:392
  504.5 22.0 %collective-permute-start.66 = (bf16[256,1024]{1,0:T(8,128)(2,1)S(1)}, bf16[256,1024]{1,0:T(8,128)(2,1)S(1)}, u32[]{:S(2)}, u32[]{:S(2)}) collective-permute-start(bf16[256,1024]{1,0:T(8,128)(2,1)S(1)} %get-tuple-element.139), channel_id=1, source_target_pairs={{0,2},{1,3},{2,4},{3,5},{4,6},{5,7},{8,10},{9,11},{10,12},{11,13},... | collective-permute-start | bytes 1572872 | tf_op jit(solution)/shard_map/ppermute | solution.py:395
  508.9 32.8 %collective-permute-start.69 = (bf16[256,1024]{1,0:T(8,128)(2,1)S(1)}, bf16[256,1024]{1,0:T(8,128)(2,1)S(1)}, u32[]{:S(2)}, u32[]{:S(2)}) collective-permute-start(bf16[256,1024]{1,0:T(8,128)(2,1)S(1)} %get-tuple-element.140), channel_id=1, source_target_pairs={{2,0},{3,1},{4,2},{5,3},{6,4},{7,5},{10,8},{11,9},{12,10},{13,11},... | collective-permute-start | bytes 1572872 | tf_op jit(solution)/shard_map/ppermute | solution.py:395
  513.1 17.8 %collective-permute-start.54 = (bf16[2,4,32,896]{3,2,1,0:T(8,128)(2,1)S(1)}, bf16[2,4,32,896]{3,2,1,0:T(8,128)(2,1)S(1)}, u32[]{:S(2)}, u32[]{:S(2)}) collective-permute-start(bf16[2,4,32,896]{3,2,1,0:T(8,128)(2,1)S(1)} %fusion.72), channel_id=1, source_target_pairs={{0,1},{1,0},{2,3},{3,2},{4,5},{5,4},{6,7},{7,6},{8,9},{9,8},{10,11... | collective-permute-start | bytes 1376264 | tf_op jit(solution)/shard_map/ppermute | solution.py:392
  542.1 22.6 %collective-permute-start.68 = (bf16[256,1024]{1,0:T(8,128)(2,1)S(1)}, bf16[256,1024]{1,0:T(8,128)(2,1)S(1)}, u32[]{:S(2)}, u32[]{:S(2)}) collective-permute-start(bf16[256,1024]{1,0:T(8,128)(2,1)S(1)} %get-tuple-element.137), channel_id=1, source_target_pairs={{0,2},{1,3},{2,4},{3,5},{4,6},{5,7},{8,10},{9,11},{10,12},{11,13},... | collective-permute-start | bytes 1572872 | tf_op jit(solution)/shard_map/ppermute | solution.py:395
  547.2 16.1 %collective-permute-start.59 = (bf16[32,4224]{1,0:T(8,128)(2,1)S(1)}, bf16[32,4224]{1,0:T(8,128)(2,1)S(1)}, u32[]{:S(2)}, u32[]{:S(2)}) collective-permute-start(bf16[32,4224]{1,0:T(8,128)(2,1)S(1)} %get-tuple-element.144), channel_id=1, source_target_pairs={{2,0},{3,1},{4,2},{5,3},{6,4},{7,5},{10,8},{11,9},{12,10},{13,11},... | collective-permute-start | bytes 811016 | tf_op jit(solution)/shard_map/ppermute | solution.py:395
  (106 other events, 872.9 us)

commit v3 on v2

--- a/solution.py
+++ b/solution.py
@@ -171,64 +171,92 @@
 TILE = 256
 
 
-def part_out(spot, values, parted, blocks):
+def part_out(core, values, parted, blocks):
     width = values.shape[1] // blocks
     for block in range(blocks):
-        half = (block % 2 + spot[0] + 1) % 2
+        half = (block % 2 + core + 1) % 2
         start = block // 2 * width
         parted[half, :, start : start + width] = values[:, block * width : (block + 1) * width]
 
 
-def middle_forward_kernel(
-    blocks,
-    spot,
-    mixed,
-    tokens,
-    cotangent,
-    w_out,
-    w_up,
-    w_down,
-    vectors,
-    bias_up,
-    output,
-    grad_sum,
-    grad_low,
-    normed,
-    scale,
-    active_parts,
-    slope,
-    first_parts,
-    mixed_parts,
-    token_parts,
-    sums,
-):
-    bias_out, gain_one, shift_one, bias_down, gain_two, shift_two = (
-        vectors[i : i + 1, :] for i in range(6)
-    )
-    part_out(spot, mixed[...], mixed_parts, blocks)
-    part_out(spot, tokens[...], token_parts, blocks)
-    hidden = tokens[...].astype(jnp.float32) + matmul(mixed[...], w_out[...]) + bias_out
+def load(plan, spot, pieces, whole, sem):
+    copies = []
+    for source, flip, out, rows, columns, start in plan:
+        if flip is None:
+            target = whole[out]
+        else:
+            x, c, y = ((spot[i] + flip[i]) % 2 for i in range(3))
+            target = whole[out].at[x, c, :, y, :, pl.ds(columns[0], columns[1])]
+        part = pieces[source] if flip is None else pieces[source].at[:, pl.ds(start, rows), :]
+        copies.append(pltpu.make_async_copy(part, target, sem.at[len(copies)]))
+    return copies
+
+
+def fetch(plan, spot, pieces, whole, sem):
+    @pl.when(pl.program_id(0) == 0)
+    def _():
+        copies = load(plan, spot, pieces, whole, sem)
+        for copy in copies:
+            copy.start()
+        for copy in copies:
+            copy.wait()
+
+
+def columns_of(weight, start, size):
+    return weight[..., start : start + size].reshape(-1, size)
+
+
+def block_of(weight, block):
+    return weight[block // CORES, block % CORES].reshape(-1, weight.shape[-1])
+
+
+def middle_up_kernel(plan, blocks, count, spot, *refs):
+    pieces, refs = refs[:count], refs[count:]
+    mixed, tokens, vectors, bias_up = refs[:4]
+    first_full, normed, scale, active_parts, slope, first_parts, mixed_parts, token_parts = refs[4:12]
+    w_out, w_up, sem = refs[12:]
+    fetch(plan, spot, pieces, (w_out, w_up), sem)
+    core = spot[1]
+    bias_out, gain_one, shift_one = (vectors[i : i + 1, :] for i in range(3))
+    part_out(core, mixed[...], mixed_parts, blocks)
+    part_out(core, tokens[...], token_parts, blocks)
+    hidden = tokens[...].astype(jnp.float32) + matmul(mixed[...], columns_of(w_out, 0, D)) + bias_out
     normed_one, scale_one = norm_forward(hidden)
     normed[...] = normed_one
     scale[...] = jnp.broadcast_to(scale_one, scale.shape)
     first_out = normed_one * gain_one + shift_one
+    first_full[...] = first_out
     first_low = first_out.astype(jnp.bfloat16)
-    part_out(spot, first_low, first_parts, blocks)
-    width = w_up.shape[1] // blocks
-    second = first_out + bias_down
-    for start in range(0, w_up.shape[1], CHUNK):
+    part_out(core, first_low, first_parts, blocks)
+    wide = w_up.shape[-1]
+    width = wide // blocks
+    for start in range(0, wide, CHUNK):
         at = slice(start, start + CHUNK)
-        upward = matmul(first_low, w_up[:, at]) + bias_up[:, at]
+        upward = matmul(first_low, columns_of(w_up, start, CHUNK)) + bias_up[:, at]
         phi = 0.5 * (1.0 + lax.erf(upward * 0.7071067811865476))
         active = (upward * phi).astype(jnp.bfloat16)
         slope[:, at] = (
             phi + upward * jnp.exp(-0.5 * upward * upward) * 0.3989422804014327
         ).astype(jnp.bfloat16)
         block, inside = start // width, start % width
-        half = (block % 2 + spot[0] + 1) % 2
+        half = (block % 2 + core + 1) % 2
         place = block // 2 * width + inside
         active_parts[half, :, place : place + CHUNK] = active
-        second = second + matmul(active, w_down[at, :])
+
+
+def middle_down_kernel(plan, blocks, count, spot, *refs):
+    pieces, refs = refs[:count], refs[count:]
+    first_full, active_parts, cotangent, vectors = refs[:4]
+    output, grad_sum, grad_low, sums, w_down, sem = refs[4:]
+    fetch(plan, spot, pieces, (w_down,), sem)
+    bias_down, gain_two, shift_two = (vectors[i : i + 1, :] for i in range(3, 6))
+    second = first_full[...] + bias_down
+    width = active_parts.shape[2] * 2 // blocks
+    for block in range(blocks):
+        half = (block % 2 + spot[1] + 1) % 2
+        place = block // 2 * width
+        part = active_parts[half, :, place : place + width]
+        second = second + matmul(part, block_of(w_down, block))
     normed_two, scale_two = norm_forward(second)
     output[...] = (normed_two * gain_two + shift_two).astype(jnp.bfloat16)
     grad = cotangent[...]
@@ -246,23 +274,13 @@
     sums[2:3, :] += jnp.sum(rounded.astype(jnp.float32), axis=0, keepdims=True)
 
 
-def middle_backward_kernel(
-    grad_low,
-    grad_sum,
-    slope,
-    normed,
-    scale,
-    w_out,
-    w_up,
-    w_down,
-    vectors,
-    grad_up,
-    grad_hidden,
-    branch,
-    grad_mixed,
-    sums,
-    sums_up,
-):
+def middle_backward_kernel(plan, count, spot, *refs):
+    pieces, refs = refs[:count], refs[count:]
+    grad_low, grad_sum, slope, normed, scale, vectors = refs[:6]
+    grad_up, grad_hidden, branch, grad_mixed, sums, sums_up = refs[6:12]
+    w_out, w_up, w_down, sem = refs[12:]
+    fetch(plan, spot, pieces, (w_out, w_up, w_down), sem)
+
     @pl.when(pl.program_id(0) == 0)
     def _():
         sums[...] = jnp.zeros_like(sums)
@@ -270,12 +288,15 @@
 
     grad_first = grad_sum[...]
     low = grad_low[...]
-    for start in range(0, w_up.shape[1], CHUNK):
+    wide = w_up.shape[-1]
+    width = wide // (w_down.shape[0] * w_down.shape[1])
+    for start in range(0, wide, CHUNK):
         at = slice(start, start + CHUNK)
-        part = (across(low, w_down[at, :]) * slope[:, at].astype(jnp.float32)).astype(jnp.bfloat16)
+        rows = block_of(w_down, start // width)[start % width : start % width + CHUNK]
+        part = (across(low, rows) * slope[:, at].astype(jnp.float32)).astype(jnp.bfloat16)
         grad_up[:, at] = part
         sums_up[:, at] += jnp.sum(part.astype(jnp.float32), axis=0, keepdims=True)
-        grad_first = grad_first + across(part, w_up[:, at])
+        grad_first = grad_first + across(part, columns_of(w_up, start, CHUNK))
     normed_one = normed[...]
     sums[0:1, :] += jnp.sum(grad_first * normed_one, axis=0, keepdims=True)
     sums[1:2, :] += jnp.sum(grad_first, axis=0, keepdims=True)
@@ -284,7 +305,7 @@
     rounded = hidden.astype(jnp.bfloat16)
     branch[...] = rounded
     sums[2:3, :] += jnp.sum(rounded.astype(jnp.float32), axis=0, keepdims=True)
-    grad_mixed[...] = across(rounded, w_out[...]).astype(jnp.bfloat16)
+    grad_mixed[...] = across(rounded, columns_of(w_out, 0, D)).astype(jnp.bfloat16)
 
 
 def tiled(columns):
@@ -299,12 +320,45 @@
     return pl.BlockSpec(shape, lambda i: (0,) * len(shape), pipeline_mode=pl.Buffered(1))
 
 
-def middle_forward(core, blocks, mixed, tokens, cotangent, w_out, w_up, w_down, vectors, bias_up):
-    rows, wide = tokens.shape[0], w_up.shape[1]
-    shapes = [
-        ((rows, D), jnp.bfloat16),
+def middle_call(kernel, grid, spot, weights, tiles, fixed, outs, sums, flops, exps=0):
+    arrays, plan, shapes = weights
+    rows = tiles[0].shape[-2]
+    lead = (grid.xs, CORES, grid.zs, grid.ys)
+
+    def spec(shape):
+        return parted(shape[2]) if len(shape) == 3 else tiled(shape[1])
+
+    return pl.pallas_call(
+        functools.partial(kernel, plan),
+        grid=(rows // TILE,),
+        out_shape=[jax.ShapeDtypeStruct(*o) for o in outs]
+        + [jax.ShapeDtypeStruct(o, jnp.float32) for o in sums],
+        in_specs=[pl.BlockSpec(memory_space=pltpu.SMEM)]
+        + [pl.BlockSpec(memory_space=pl.ANY)] * len(arrays)
+        + [spec(t.shape) for t in tiles]
+        + [resident(f.shape) for f in fixed],
+        out_specs=[spec(o[0]) for o in outs] + [pl.BlockSpec(o, lambda i: (0, 0)) for o in sums],
+        scratch_shapes=[pltpu.VMEM(lead + shape, jnp.bfloat16) for shape in shapes]
+        + [pltpu.SemaphoreType.DMA((len(plan),))],
+        cost_estimate=pl.CostEstimate(flops=flops, bytes_accessed=40 << 20, transcendentals=exps),
+        compiler_params=pltpu.CompilerParams(vmem_limit_bytes=60 << 20),
+    )(spot, *arrays, *tiles, *fixed)
+
+
+def joined(*weights):
+    arrays, plan, shapes = [], [], []
+    for some, steps, sizes in weights:
+        for source, flip, out, rows, columns, start in steps:
+            place = (source + len(arrays), flip, out + len(shapes), rows, columns, start)
+            plan.append(place)
+        arrays, shapes = arrays + list(some), shapes + list(sizes)
+    return arrays, plan, shapes
+
+
+def middle_up(grid, spot, weights, mixed, tokens, vectors, bias_up):
+    rows, wide = tokens.shape[0], bias_up.shape[1]
+    outs = [
         ((rows, D), jnp.float32),
-        ((rows, D), jnp.bfloat16),
         ((rows, D), jnp.float32),
         ((rows, 128), jnp.float32),
         ((2, rows, wide // 2), jnp.bfloat16),
@@ -312,48 +366,46 @@
         ((2, rows, D // 2), jnp.bfloat16),
         ((2, rows, D // 2), jnp.bfloat16),
         ((2, rows, D // 2), jnp.bfloat16),
-        ((8, D), jnp.float32),
     ]
-    specs = [parted(s[2]) if len(s) == 3 else tiled(s[1]) for s, _ in shapes[:-1]]
-    return pl.pallas_call(
-        functools.partial(middle_forward_kernel, blocks),
-        grid=(rows // TILE,),
-        out_shape=[jax.ShapeDtypeStruct(*s) for s in shapes],
-        in_specs=[pl.BlockSpec(memory_space=pltpu.SMEM)]
-        + [tiled(D)] * 3
-        + [resident(w.shape) for w in (w_out, w_up, w_down, vectors, bias_up)],
-        out_specs=specs + [pl.BlockSpec((8, D), lambda i: (0, 0))],
-        cost_estimate=pl.CostEstimate(
-            flops=2 * rows * (D * D + 2 * D * wide),
-            bytes_accessed=60 << 20,
-            transcendentals=2 * rows * wide,
-        ),
-        compiler_params=pltpu.CompilerParams(vmem_limit_bytes=60 << 20),
-    )(core, mixed, tokens, cotangent, w_out, w_up, w_down, vectors, bias_up)
-
-
-def middle_backward(grad_low, grad_sum, slope, normed, scale, w_out, w_up, w_down, vectors):
-    rows, wide = grad_low.shape[0], w_up.shape[1]
-    shapes = [
+
+    def kernel(plan, *refs):
+        middle_up_kernel(plan, grid.xs * CORES, len(weights[0]), *refs)
+
+    flops = 2 * rows * D * (D + wide)
+    return middle_call(
+        kernel, grid, spot, weights, [mixed, tokens], [vectors, bias_up], outs, [], flops, 2 * rows * wide
+    )
+
+
+def middle_down(grid, spot, weights, first_full, active_parts, cotangent, vectors):
+    rows, wide = first_full.shape[0], active_parts.shape[2] * 2
+    outs = [((rows, D), jnp.bfloat16), ((rows, D), jnp.float32), ((rows, D), jnp.bfloat16)]
+
+    def kernel(plan, *refs):
+        middle_down_kernel(plan, grid.xs * CORES, len(weights[0]), *refs)
+
+    tiles = [first_full, active_parts, cotangent]
+    flops = 2 * rows * D * wide
+    return middle_call(kernel, grid, spot, weights, tiles, [vectors], outs, [(8, D)], flops)
+
+
+def middle_backward(grid, spot, weights, grad_low, grad_sum, slope, normed, scale, vectors):
+    rows, wide = slope.shape
+    outs = [
         ((rows, wide), jnp.bfloat16),
         ((rows, D), jnp.float32),
         ((rows, D), jnp.bfloat16),
         ((rows, D), jnp.bfloat16),
     ]
-    last = [((8, D), jnp.float32), ((1, wide), jnp.float32)]
-    return pl.pallas_call(
-        middle_backward_kernel,
-        grid=(rows // TILE,),
-        out_shape=[jax.ShapeDtypeStruct(*s) for s in shapes + last],
-        in_specs=[tiled(v.shape[1]) for v in (grad_low, grad_sum, slope, normed, scale)]
-        + [resident(w.shape) for w in (w_out, w_up, w_down, vectors)],
-        out_specs=[tiled(s[1]) for s, _ in shapes]
-        + [pl.BlockSpec(s, lambda i: (0, 0)) for s, _ in last],
-        cost_estimate=pl.CostEstimate(
-            flops=2 * rows * (D * D + 2 * D * wide), bytes_accessed=60 << 20, transcendentals=0
-        ),
-        compiler_params=pltpu.CompilerParams(vmem_limit_bytes=60 << 20),
-    )(grad_low, grad_sum, slope, normed, scale, w_out, w_up, w_down, vectors)
+
+    def kernel(plan, *refs):
+        middle_backward_kernel(plan, len(weights[0]), *refs)
+
+    tiles = [grad_low, grad_sum, slope, normed, scale]
+    flops = 2 * rows * D * (D + 2 * wide)
+    return middle_call(
+        kernel, grid, spot, weights, tiles, [vectors], outs, [(8, D), (1, wide)], flops
+    )
 
 
 class Grid:
@@ -364,7 +416,7 @@
         self.zs = self.shape["fsdp"] // self.ys
         self.sizes = {"x": self.xs, "c": CORES, "z": self.zs, "y": self.ys}
         self.count = self.shape["dp"] * self.shape["fsdp"]
-        self.pairs = self.xs == 2 and self.ys == 2
+        self.pairs = self.xs == 2 and self.ys == 2 and self.zs == 4
 
     def at(self):
         dp, fsdp = lax.axis_index("dp"), lax.axis_index("fsdp")
@@ -395,13 +447,63 @@
         return lax.ppermute(values, AXES, self.shifted(axis, step, False))
 
 
-def line_gather(grid, at, shard):
-    up, down = [shard], [shard]
-    for _ in range(grid.zs - 1):
-        up.append(grid.along(up[-1], "z", 1))
-        down.append(grid.along(down[-1], "z", -1))
-    line = jnp.stack(up[:0:-1] + [shard] + down[1:])
-    return lax.dynamic_slice_in_dim(line, grid.zs - 1 - at["z"], grid.zs, 0)
+def place_kernel(steps, count, spot, *refs):
+    arrays, out, sem = refs[:count], refs[count], refs[count + 1]
+
+    def each(act):
+        for index, (source, select, target, valid) in enumerate(steps):
+            def run(index=index, source=source, select=select, target=target):
+                part = arrays[source] if select is None else arrays[source].at[select]
+                act(pltpu.make_async_copy(part, out.at[target(spot)], sem.at[index]))
+
+            if valid is None:
+                run()
+            else:
+                pl.when(valid(spot))(run)
+
+    each(lambda copy: copy.start())
+    each(lambda copy: copy.wait())
+
+
+def place(arrays, spot, steps, shape):
+    size = 4 * sum(a.size for a in arrays)
+    return pl.pallas_call(
+        functools.partial(place_kernel, steps, len(arrays)),
+        out_shape=jax.ShapeDtypeStruct(shape, jnp.bfloat16),
+        in_specs=[pl.BlockSpec(memory_space=pltpu.SMEM)]
+        + [pl.BlockSpec(memory_space=pl.ANY)] * len(arrays),
+        out_specs=pl.BlockSpec(memory_space=pl.ANY),
+        scratch_shapes=[pltpu.SemaphoreType.DMA((len(steps),))],
+        cost_estimate=pl.CostEstimate(flops=0, bytes_accessed=size, transcendentals=0),
+        compiler_params=pltpu.CompilerParams(vmem_limit_bytes=1 << 20),
+    )(spot, *arrays)
+
+
+def line_gather(grid, spot, shard):
+    arrays = [shard]
+    steps = [(0, None, lambda spot: spot[3], None)]
+    up = low = shard
+    for hop in range(1, grid.zs):
+        up, low = grid.along(up, "z", 1), grid.along(low, "z", -1)
+        arrays += [up, low]
+        last = grid.zs - 1
+        steps.append(
+            (
+                2 * hop - 1,
+                None,
+                lambda spot, hop=hop: jnp.maximum(spot[3] - hop, 0),
+                lambda spot, hop=hop: spot[3] >= hop,
+            )
+        )
+        steps.append(
+            (
+                2 * hop,
+                None,
+                lambda spot, hop=hop: jnp.minimum(spot[3] + hop, last),
+                lambda spot, hop=hop: spot[3] + hop <= last,
+            )
+        )
+    return place(arrays, spot, steps, (grid.zs,) + shard.shape)
 
 
 def own_swaps(grid, block, first, second):
@@ -419,54 +521,38 @@
     return found
 
 
-def assemble_kernel(plan, grid, count, outs, spot, *refs):
-    pieces, whole, sem = refs[:count], refs[count : count + outs], refs[-1]
-    copies = []
-    for source, (flip, out, rows, columns, start) in enumerate_plan(plan):
-        x, c, y = ((spot[i] + flip[i]) % 2 for i in range(3))
-        copies.append(
-            pltpu.make_async_copy(
-                pieces[source].at[:, pl.ds(start, rows), :],
-                whole[out].at[x, c, :, y, :, pl.ds(columns[0], columns[1])],
-                sem.at[len(copies)],
-            )
-        )
+def block_plan(parts):
+    plan, arrays = [], []
+    for pieces, targets in parts:
+        for flip, piece in pieces.items():
+            for out, rows, columns, start in targets:
+                plan.append((len(arrays), flip, out, rows, columns, start))
+            arrays.append(piece)
+    return arrays, plan
+
+
+def assemble_kernel(plan, count, spot, *refs):
+    copies = load(plan, spot, refs[:count], refs[count:-1], refs[-1])
     for copy in copies:
         copy.start()
     for copy in copies:
         copy.wait()
 
 
-def enumerate_plan(plan):
-    for source, (flip, targets) in enumerate(plan):
-        for out, rows, columns, start in targets:
-            yield source, (flip, out, rows, columns, start)
-
-
-def assemble(grid, at, parts, shapes):
-    plan, arrays = [], []
-    for pieces, targets in parts:
-        for flip, piece in pieces.items():
-            plan.append((flip, targets))
-            arrays.append(piece)
-    copies = sum(len(targets) for _, targets in plan)
-    spot = jnp.stack([at["x"], at["c"], at["y"]]).astype(jnp.int32)
-    outs = [
-        jax.ShapeDtypeStruct((grid.xs, CORES, grid.zs, grid.ys) + shape, jnp.bfloat16)
-        for shape in shapes
-    ]
+def assemble(grid, spot, parts, shape):
+    arrays, plan = block_plan(parts)
     size = sum(2 * piece.size for piece in arrays)
     whole = pl.pallas_call(
-        functools.partial(assemble_kernel, plan, grid, len(arrays), len(outs)),
-        out_shape=outs,
+        functools.partial(assemble_kernel, plan, len(arrays)),
+        out_shape=jax.ShapeDtypeStruct((grid.xs, CORES, grid.zs, grid.ys) + shape, jnp.bfloat16),
         in_specs=[pl.BlockSpec(memory_space=pltpu.SMEM)]
         + [pl.BlockSpec(memory_space=pl.ANY)] * len(arrays),
-        out_specs=[pl.BlockSpec(memory_space=pl.ANY)] * len(outs),
-        scratch_shapes=[pltpu.SemaphoreType.DMA((copies,))],
+        out_specs=pl.BlockSpec(memory_space=pl.ANY),
+        scratch_shapes=[pltpu.SemaphoreType.DMA((len(plan),))],
         cost_estimate=pl.CostEstimate(flops=0, bytes_accessed=2 * size, transcendentals=0),
         compiler_params=pltpu.CompilerParams(vmem_limit_bytes=1 << 20),
     )(spot, *arrays)
-    return [w.reshape(grid.count * s[0], s[1]) for w, s in zip(whole, shapes)]
+    return whole.reshape(grid.count * shape[0], shape[1])
 
 
 def take(values, index, axis):
@@ -485,56 +571,64 @@
         self.grid, self.at = grid, at
         got = grid.swap(sent, "c")
         shape = (grid.xs, grid.zs, grid.ys, -1, sent.shape[1])
-        self.terms = [kept.reshape(shape), got.reshape(shape)]
-        self.cut = sent.shape[1] // 256 * 128
-
-    def first(self):
-        self.left = [term[..., : self.cut] for term in self.terms]
-        self.right = [term[..., self.cut :] for term in self.terms]
-        return self.give("x", 0, "y", 2)
-
-    def give(self, left_name, left_axis, right_name, right_axis):
-        self.names = (left_name, left_axis, right_name, right_axis)
+        terms = [kept.reshape(shape), got.reshape(shape)]
+        cut = sent.shape[1] // 256 * 128
+        self.sides = [[t[..., :cut] for t in terms], [t[..., cut:] for t in terms]]
+
+    def give(self, *ways):
+        self.ways = ways
         sent = []
-        for terms, name, axis in (
-            (self.left, left_name, left_axis),
-            (self.right, right_name, right_axis),
-        ):
+        for terms, (name, axis) in zip(self.sides, ways):
             values = total([take(term, 1 - self.at[name], axis) for term in terms])
             sent.append(values.astype(jnp.bfloat16))
         return tuple(sent)
 
-    def get(self, sent):
-        left_name, left_axis, right_name, right_axis = self.names
-        self.left = [take(term, self.at[left_name], left_axis) for term in self.left]
-        self.left.append(self.grid.swap(sent[0], left_name))
-        self.right = [take(term, self.at[right_name], right_axis) for term in self.right]
-        self.right.append(self.grid.swap(sent[1], right_name))
-
-    def second(self, sent):
-        self.get(sent)
-        return self.give("y", 1, "x", 0)
-
-    def line(self, sent):
-        self.get(sent)
-        joined = jnp.concatenate([total(self.left), total(self.right)], axis=-1)
-        return joined.astype(jnp.bfloat16)
-
-
-def line_reduce(grid, at, block):
-    size = grid.zs
-
-    def own(index):
-        return take(block, jnp.clip(index, 0, size - 1), 0).astype(jnp.float32)
-
-    up = low = None
-    for step in range(1, size):
-        up_sum, low_sum = own(at["z"] + size - step), own(at["z"] - size + step)
-        if step > 1:
-            up_sum, low_sum = up_sum + up.astype(jnp.float32), low_sum + low.astype(jnp.float32)
-        up = grid.along(up_sum.astype(jnp.bfloat16), "z", 1)
-        low = grid.along(low_sum.astype(jnp.bfloat16), "z", -1)
-    return own(at["z"]) + up.astype(jnp.float32) + low.astype(jnp.float32)
+    def first(self):
+        return self.give(("x", 0), ("y", 2))
+
+    def swap(self, sent):
+        return tuple(self.grid.swap(values, way[0]) for values, way in zip(sent, self.ways))
+
+    def get(self, received):
+        self.sides = [
+            [take(term, self.at[name], axis) for term in terms] + [values]
+            for terms, (name, axis), values in zip(self.sides, self.ways, received)
+        ]
+
+    def second(self, received):
+        self.get(received)
+        return self.give(("y", 1), ("x", 0))
+
+    def block(self, received):
+        self.get(received)
+        return jnp.concatenate([total(terms) for terms in self.sides], axis=-1).astype(jnp.bfloat16)
+
+
+class Line:
+    def __init__(self, grid, at, block):
+        self.grid, self.at, self.block = grid, at, block
+
+    def own(self, index):
+        index = jnp.clip(index, 0, self.grid.zs - 1)
+        return take(self.block, index, 0).astype(jnp.float32)
+
+    def give(self, hop, received=None):
+        size = self.grid.zs
+        sums = [self.own(self.at["z"] + size - hop), self.own(self.at["z"] - size + hop)]
+        if received is not None:
+            sums = [own + more.astype(jnp.float32) for own, more in zip(sums, received)]
+        return tuple(values.astype(jnp.bfloat16) for values in sums)
+
+    def move(self, sent):
+        return tuple(self.grid.along(values, "z", step) for values, step in zip(sent, (1, -1)))
+
+    def end(self, received):
+        return total([self.own(self.at["z"]), *received])
+
+    def rest(self, received, hop):
+        for step in range(hop, self.grid.zs):
+            received = self.move(self.give(step, received))
+        return self.end(received)
 
 
 def by_halves(parts):
@@ -546,43 +640,67 @@
     return jnp.pad(flat, (0, rows * 128 - flat.size)).reshape(rows, 128)
 
 
-def gather_first(grid, at, attn, smalls):
-    rows = attn[0].shape[0]
-    line = line_gather(
-        grid, at, jnp.concatenate([by_halves(attn), pack_small(smalls, rows)], axis=1)
-    )
-    return line
-
-
-def gather_attention(grid, at, line, rows):
-    columns = line.shape[2]
-    cut = (columns // 256) * 128
-    left, right = line[:, :, :cut], line[:, :, cut:]
-    left = pair_gather(grid, left, own_swaps(grid, left, "y", "x"), "y", "x")
-    right = pair_gather(grid, right, own_swaps(grid, right, "x", "y"), "x", "y")
-    (full,) = assemble(
-        grid,
-        at,
-        [(left, [(0, rows, (0, cut), 0)]), (right, [(0, rows, (cut, columns - cut), 0)])],
-        [(rows, columns)],
-    )
-    return full[:, : 3 * D], full[:, 3 * D :].reshape(grid.count, -1)
-
-
-def gather_rest(grid, at, line, swaps, rows, lower, wide):
-    split = rows + lower
-    down_part = pair_gather(grid, line[:, :split], swaps[0], "y", "x")
-    up_part = pair_gather(grid, line[:, split:], swaps[1], "x", "y")
-    up_targets = [(1, rows, (i * D, D), i * rows) for i in range(wide // D)]
-    return assemble(
-        grid,
-        at,
-        [
-            (down_part, [(0, rows, (0, D), 0), (2, lower, (0, D), rows)]),
-            (up_part, up_targets),
-        ],
-        [(rows, D), (rows, wide), (lower, D)],
-    )
+def pack_first(spot, attn, small):
+    steps = []
+    for half in range(2):
+        for part in range(3):
+            start = (3 * half + part) * HALF
+            steps.append(
+                (
+                    part,
+                    (slice(None), pl.ds(half * HALF, HALF)),
+                    lambda spot, start=start: (slice(None), pl.ds(start, HALF)),
+                    None,
+                )
+            )
+    steps.append((3, None, lambda spot: (slice(None), pl.ds(3 * D, 128)), None))
+    return place([*attn, small], spot, steps, (attn[0].shape[0], 3 * D + 128))
+
+
+def pack_rest(spot, w_out, w_up, w_down):
+    rows, wide = w_up.shape
+    steps = [(0, None, lambda spot: (pl.ds(0, rows), slice(None)), None)]
+    for i in range(wide // D):
+        steps.append(
+            (
+                1,
+                (slice(None), pl.ds(i * D, D)),
+                lambda spot, i=i: (pl.ds((i + 1) * rows, rows), slice(None)),
+                None,
+            )
+        )
+    start = rows + rows * wide // D
+    steps.append((2, None, lambda spot: (pl.ds(start, w_down.shape[0]), slice(None)), None))
+    return place([w_out, w_up, w_down], spot, steps, (start + w_down.shape[0], D))
+
+
+class Gather:
+    orders = (("y", "x"), ("x", "y"))
+
+    def __init__(self, grid, line):
+        self.grid = grid
+        self.cut = line.shape[2] // 256 * 128
+        self.columns = line.shape[2]
+        self.sides = [line[:, :, : self.cut], line[:, :, self.cut :]]
+
+    def start(self):
+        self.swaps = [own_swaps(self.grid, v, *o) for v, o in zip(self.sides, self.orders)]
+
+    def blocks(self):
+        return [
+            pair_gather(self.grid, v, swapped, *order)
+            for v, swapped, order in zip(self.sides, self.swaps, self.orders)
+        ]
+
+    def parts(self, targets):
+        spans = [(0, self.cut), (self.cut, self.columns - self.cut)]
+        return [
+            (
+                pieces,
+                [(out, rows, (first + span[0], span[1]), start) for out, rows, first, start in targets],
+            )
+            for pieces, span in zip(self.blocks(), spans)
+        ]
 
 
 def split_small(small, widths):
@@ -635,18 +753,21 @@
     widths = [small.shape[0] for small in smalls]
     attn = (w_query, w_key, w_value)
     low_tokens = tokens
+    places = [at[name] for name in "xcyz"]
+    spot = jnp.stack(places).astype(jnp.int32)
     if grid.pairs:
-        first = gather_first(grid, at, attn, smalls)
-        rest = [w_out, w_down] + [w_up[:, i : i + D] for i in range(0, wide, D)]
-        rest, first = hold(jnp.concatenate(rest, axis=0), first)
-        line = line_gather(grid, at, rest)
-        full_qkv, small = gather_attention(grid, at, first, rows)
+        first = line_gather(grid, spot, pack_first(spot, attn, pack_small(smalls, rows)))
+        rest = pack_rest(spot, w_out, w_up, w_down)
+        rest, first = hold(rest, first)
+        gather = Gather(grid, first)
+        gather.start()
+        whole = assemble(grid, spot, gather.parts([(0, rows, 0, 0)]), (rows, 3 * D + 128))
+        full_qkv, small = whole[:, : 3 * D], whole[:, 3 * D :].reshape(grid.count, -1)
+        line = line_gather(grid, spot, rest)
         low_tokens, line = hold(tokens, line)
-        split = rows + lower
-        swaps = [
-            own_swaps(grid, line[:, :split], "y", "x"),
-            own_swaps(grid, line[:, split:], "x", "y"),
-        ]
+        split = rows + rows * wide // D
+        up_gather, down_gather = Gather(grid, line[:, :split]), Gather(grid, line[:, split:])
+        up_gather.start()
     else:
         full_qkv, full_out, full_up, full_down = (
             lax.all_gather(w, AXES, axis=0, tiled=True)
@@ -661,15 +782,25 @@
     bias_qkv = by_halves([bias[None] for bias in biases])
     qkv = (matmul(low_tokens, full_qkv) + bias_qkv).astype(jnp.bfloat16)
     mixed = attend_forward(qkv, doc_column, doc_row)
+    up_shapes, down_shapes = [(rows, D), (rows, wide)], [(lower, D)]
     if grid.pairs:
-        swaps, mixed = hold(swaps, mixed)
-        full_out, full_up, full_down = gather_rest(grid, at, line, swaps, rows, lower, wide)
-    core = at["c"] if grid.pairs else at["c"] * 0
-    blocks = grid.xs * CORES
+        up_gather.swaps, mixed = hold(up_gather.swaps, mixed)
+        targets = [(0, rows, 0, 0)]
+        targets += [(1, rows, i * D, (i + 1) * rows) for i in range(wide // D)]
+        up_weights = (*block_plan(up_gather.parts(targets)), up_shapes)
+        down_gather.sides, up_weights[0][:] = hold(down_gather.sides, up_weights[0])
+        down_gather.start()
+    else:
+        spot = spot * 0
+        lead = (grid.xs, CORES, grid.zs, grid.ys)
+        up_weights = (
+            [full_out.reshape(lead + (rows, D)), full_up.reshape(lead + (rows, wide))],
+            [(0, None, 0, rows, None, 0), (1, None, 1, rows, None, 0)],
+            up_shapes,
+        )
+    bias_wide = bias_up.reshape(1, -1)
     (
-        output,
-        grad_sum,
-        grad_low,
+        first_full,
         normed,
         scale,
         active_parts,
@@ -677,41 +808,56 @@
         first_parts,
         mixed_parts,
         token_parts,
-        sums_two,
-    ) = middle_forward(
-        core.reshape(1).astype(jnp.int32),
-        blocks,
-        mixed,
-        tokens,
-        out_cotangent,
-        full_out,
-        full_up,
-        full_down,
-        vectors,
-        bias_up.reshape(1, -1),
-    )
-    kept = (slope, normed, scale, full_out, full_up, full_down, vectors)
+    ) = middle_up(grid, spot, up_weights, mixed, tokens, vectors, bias_wide)
+    if grid.pairs:
+        down_gather.swaps, first_full = hold(down_gather.swaps, first_full)
+        down_parts = down_gather.parts([(0, lower, 0, 0)])
+        down_weights = (*block_plan(down_parts), down_shapes)
+    else:
+        down_weights = ([full_down.reshape(lead + (lower, D))], [(0, None, 0, lower, None, 0)], down_shapes)
+    output, grad_sum, grad_low, sums_two = middle_down(
+        grid, spot, down_weights, first_full, active_parts, out_cotangent, vectors
+    )
     if grid.pairs:
         down_chain = Chain(grid, at, *halves(active_parts, grad_low))
-        down_sent = down_chain.first()
-        grad_low, down_sent = hold(grad_low, down_sent)
-    grad_up, grad_hidden, branch, grad_mixed, sums_one, sums_up = middle_backward(
-        grad_low, grad_sum, *kept
-    )
+        grad_low, down_sent = hold(grad_low, down_chain.first())
+    made = middle_backward(
+        grid, spot, joined(up_weights, down_weights), grad_low, grad_sum, slope, normed, scale, vectors
+    )
+    grad_up, grad_hidden, branch, grad_mixed, sums_one, sums_up = made
     if grid.pairs:
+        received, grad_up, branch, grad_mixed = hold(
+            down_chain.swap(down_sent), grad_up, branch, grad_mixed
+        )
+        down_sent, grad_up = hold(down_chain.second(received), grad_up)
         up_chain = Chain(grid, at, *halves(first_parts, grad_up))
-        down_sent = down_chain.second(down_sent)
-        up_sent = up_chain.first()
-        grad_mixed, up_sent, down_sent = hold(grad_mixed, up_sent, down_sent)
+        up_sent, received = hold(up_chain.first(), down_chain.swap(down_sent))
+        down_line = Line(grid, at, down_chain.block(received))
+        down_sent, up_sent, grad_mixed = hold(down_line.give(1), up_sent, grad_mixed)
     one, sums_first = attend_backward(qkv, grad_mixed, doc_column, doc_row, 0)
     if grid.pairs:
-        up_sent = up_chain.second(up_sent)
+        received, down_got, one, branch, grad_mixed = hold(
+            up_chain.swap(up_sent), down_line.move(down_sent), one, branch, grad_mixed
+        )
+        up_sent, down_sent, one, branch = hold(
+            up_chain.second(received), down_line.give(2, down_got), one, branch
+        )
         of_qkv, of_out = halves(token_parts, one), halves(mixed_parts, branch)
         early = [jnp.concatenate([of_qkv[i], of_out[i]], axis=1) for i in range(2)]
         early_chain = Chain(grid, at, *early)
-        early_sent = early_chain.first()
-        grad_mixed, up_sent, early_sent = hold(grad_mixed, up_sent, early_sent)
+        early_sent, received, down_got = hold(
+            early_chain.first(), up_chain.swap(up_sent), down_line.move(down_sent)
+        )
+        up_line = Line(grid, at, up_chain.block(received))
+        up_sent, down_sent, early_sent, grad_mixed = hold(
+            up_line.give(1), down_line.give(3, down_got), early_sent, grad_mixed
+        )
     two, sums_second = attend_backward(qkv, grad_mixed, doc_column, doc_row, 1)
+    if grid.pairs:
+        received, up_got, down_got, two = hold(
+            early_chain.swap(early_sent), up_line.move(up_sent), down_line.move(down_sent), two
+        )
+        early_sent, up_sent, two = hold(early_chain.second(received), up_line.give(2, up_got), two)
     sums_first, sums_second = sums_first[0], sums_second[0]
     totals = [
         jnp.concatenate([sums_first[:HALF], sums_second[:HALF]]),
@@ -725,6 +871,7 @@
         sums_two[1],
     ]
     if grid.pairs:
+        share_down = down_line.rest(down_got, grid.zs)
         packed = jnp.concatenate([v.reshape(grid.count, -1) for v in totals], axis=1)
         widths = [v.size // grid.count for v in totals]
         packed = jnp.pad(packed, ((0, 0), (0, rows * 128 - sum(widths)))).astype(jnp.bfloat16)
@@ -733,17 +880,16 @@
         of_qkv = halves(token_parts, two)
         late = [jnp.concatenate([of_qkv[i], ends[i]], axis=1) for i in range(2)]
         late_chain = Chain(grid, at, *late)
-        late_sent = late_chain.first()
+        late_sent, received, up_got = hold(
+            late_chain.first(), early_chain.swap(early_sent), up_line.move(up_sent)
+        )
         two, late_sent = hold(two, late_sent)
-        down_block, up_block = down_chain.line(down_sent), up_chain.line(up_sent)
-        up_rows = [up_block[:, :, i : i + D] for i in range(0, wide, D)]
-        block = line_reduce(grid, at, jnp.concatenate([down_block] + up_rows, axis=1))
-        share_down = block[:lower]
-        up_rows = [block[i : i + rows] for i in range(lower, lower + rows * wide // D, rows)]
-        share_up = jnp.concatenate(up_rows, axis=1)
-        early_block = early_chain.line(early_chain.second(early_sent))
-        late_block = late_chain.line(late_chain.second(late_sent))
-        block = line_reduce(grid, at, jnp.concatenate([early_block, late_block], axis=2))
+        share_up = up_line.rest(up_got, 3)
+        early_block = early_chain.block(received)
+        late_sent = late_chain.second(late_chain.swap(late_sent))
+        late_block = late_chain.block(late_chain.swap(late_sent))
+        line = Line(grid, at, jnp.concatenate([early_block, late_block], axis=2))
+        block = line.rest(line.move(line.give(1)), 2)
         early, share_out = block[:, : 3 * HALF], block[:, 3 * HALF : 5 * HALF]
         late = block[:, 5 * HALF :]
         flat = late[:, 3 * HALF :].reshape(-1)

time: 601 us -> 554 us (0.922)
  waiting for transfers between devices: 155 us -> 81.3 us
  starting transfers between devices: 98.9 us -> 126 us
  local copies, waits for them, and re-layouts: 73.8 us -> 59.3 us
  other arithmetic: 33.7 us -> 47 us
  Pallas kernels: 156 us -> 165 us
    ppermute x48 -> x62, waiting for transfers between devices: 119 us -> 53.8 us  [swap(): return lax.ppermute(values, AXES, self.shifted(axis, 1, True))]
    ppermute x24 -> x30, starting transfers between devices: 68.7 us -> 85.2 us  [along(): return lax.ppermute(values, AXES, self.shifted(axis, step, False))]
    unnamed x163 -> x195, local copies, waits for them, and re-layouts: 44.7 us -> 28.2 us
    ppermute x48 -> x62, starting transfers between devices: 30.3 us -> 40.4 us  [swap(): return lax.ppermute(values, AXES, self.shifted(axis, 1, True))]
    pallas_call x4 -> x8, Pallas kernels: 86.4 us -> 95.8 us  [the longest x3 87.2 us: middle_call(): pl.pallas_call(functools.partial(kernel, plan), grid=(rows // TILE,), out...]
    ppermute x24 -> x30, waiting for transfers between devices: 35.6 us -> 27.5 us  [along(): return lax.ppermute(values, AXES, self.shifted(axis, step, False))]
    slice x16 -> x14, local copies, waits for them, and re-layouts: 13.2 us -> 15.1 us  [the longest x9 14.9 us: __init__(): self.sides = [[t[..., :cut] for t in terms], [t[..., cut:] for t in terms]]]
  transfers between devices with their start and end apart: 72 -> 92, of which waited for: 31 -> 28; matrix products, arithmetic and copies ran while one was open for 14% -> 14% of each run, Pallas kernels for 4% -> 25%
where the time goes in v3:
time: 554 us; the launch traced here: 547 us
  Pallas kernels  165 us (30%)
  starting transfers between devices  126 us (23%)
  waiting for transfers between devices  81.3 us (15%)
  matrix products  66.2 us (12%)
  local copies, waits for them, and re-layouts  59.3 us (11%)
  other arithmetic  47 us (8%)
    pallas_call x3, Pallas kernels, middle_call(): pl.pallas_call(functools.partial(kernel, plan), grid=(rows // TILE,), out...  87.2 us
    ppermute x30, starting transfers between devices, along(): return lax.ppermute(values, AXES, self.shifted(axis, step, False))  85.2 us
    ppermute x62, waiting for transfers between devices, swap(): return lax.ppermute(values, AXES, self.shifted(axis, 1, True))  53.8 us
    dot_general x10, matrix products, outer_sum(): lax.dot_general(operand, other, (((0,), (0,)), ((), ())), preferred_eleme...  51.1 us
    pallas_call x2, Pallas kernels, attend_backward(): pl.pallas_call(attend_backward_kernel, grid=(seqs, PAIRS), out_shape=[jax...  46.6 us
    ppermute x62, starting transfers between devices, swap(): return lax.ppermute(values, AXES, self.shifted(axis, 1, True))  40.4 us
    unnamed x195, local copies, waits for them, and re-layouts  28.2 us
    ppermute x30, waiting for transfers between devices, along(): return lax.ppermute(values, AXES, self.shifted(axis, step, False))  27.5 us
  transfers between devices with their start and end apart: 92, of which 28 were waited for; matrix products, arithmetic and copies ran while one was open for 14% of the time, Pallas kernels for 25%

profile of v3, /device:TPU:0, one launch (start us, length us, event | category | flops | bytes accessed | tf_op | source)
XLA Modules:
  0.0 547.5 jit_solution(11620609249982111906)
XLA Ops:
  0.7 6.1 %concatenate.70 = bf16[384]{0:T(512)(128)(2,1)S(1)} concatenate(bf16[32]{0:T(256)(128)(2,1)} %param.21, bf16[32]{0:T(256)(128)(2,1)} %param.24, bf16[32]{0:T(256)(128)(2,1)} %param.26, bf16[32]{0:T(256)(128)(2,1)} %param.27, bf16[32]{0:T(256)(128)(2,1)} %param.28, bf16[32]{0:T(256)(128)(2,1)} %param.32, bf16[32]{0:T(256)(128)(2,1)} %param.33, bf16[32]{0:T(256)(128)(2,1)} %param.34, ...), dimensions={0} | concatenate | bytes 1536 | tf_op jit(solution)/shard_map/concatenate | solution.py:639
  11.4 5.6 %collective-permute-start = (bf16[32,3200]{1,0:T(8,128)(2,1)S(1)}, bf16[32,3200]{1,0:T(8,128)(2,1)S(1)}, u32[]{:S(2)}, u32[]{:S(2)}) collective-permute-start(bf16[32,3200]{1,0:T(8,128)(2,1)S(1)} %shard_map.306.refs_0_), channel_id=1, source_target_pairs={{0,2},{1,3},{2,4},{3,5},{4,6},{5,7},{8,10},{9,11},{10,12},{11,13},... | collective-permute-start | bytes 614408 | tf_op jit(solution)/shard_map/ppermute | solution.py:447
  21.4 4.6 collective-permute-start.2
  29.5 4.6 collective-permute-start.4
  43.7 7.1 %collective-permute-done.20.refs_4_ = bf16[4,32,1536]{2,1,0:T(8,128)(2,1)S(1)} collective-permute-done((bf16[4,32,1536]{2,1,0:T(8,128)(2,1)S(1)}, bf16[4,32,1536]{2,1,0:T(8,128)(2,1)S(1)}, u32[]{:S(2)}, u32[]{:S(2)}) %collective-permute-start.20) | collective-permute-done | bytes 393248 | tf_op jit(solution)/shard_map/ppermute | solution.py:444
  70.7 4.4 collective-permute-start.8
  78.2 5.8 %collective-permute-done.9.refs_4_ = bf16[288,1024]{1,0:T(8,128)(2,1)S(1)} collective-permute-done((bf16[288,1024]{1,0:T(8,128)(2,1)S(1)}, bf16[288,1024]{1,0:T(8,128)(2,1)S(1)}, u32[]{:S(2)}, u32[]{:S(2)}) %collective-permute-start.9) | collective-permute-done | bytes 589856 | tf_op jit(solution)/shard_map/ppermute | solution.py:447
  86.7 5.3 collective-permute-start.10
  116.0 7.1 %add_convert_fusion.query.key.value = bf16[1024,3072]{1,0:T(8,128)(2,1)S(1)} fusion(f32[3072]{0:T(1024)S(1)} %bitcast.347, bf16[1024,1024]{1,0:T(8,128)(2,1)S(1)} %copy-done.65, bf16[1024,3200]{1,0:T(8,128)(2,1)S(1)} %bitcast.328), kind=kOutput, calls=%fused_computation | convolution fusion | flops 6448742400 | bytes 14692352 | tf_op jit(solution)/shard_map/dot_general | solution.py:19
  123.0 23.0 %shard_map.310.refs_17_ = bf16[1024,1024]{1,0:T(8,128)(2,1)S(1)} custom-call(bf16[1024,3072]{1,0:T(8,128)(2,1)S(1)} %add_convert_fusion.query.key.value, bf16[1024,3072]{1,0:T(8,128)(2,1)S(1)} %add_convert_fusion.query.key.value, bf16[1024,3072]{1,0:T(8,128)(2,1)S(1)} %add_convert_fusion.query.key.value, s32[2,512,1]{2,1,0:T(8,128)S(1)} %copy-done.6, ...), custom_call_target="tpu_custom_call" | custom-call | flops 8589934592 | bytes 25165824 | tf_op jit(solution)/shard_map/pallas_call | solution.py:132
  150.7 14.4 %collective-permute-done.33.refs_7_ = bf16[4,160,512]{2,1,0:T(8,128)(2,1)} collective-permute-done((bf16[4,160,512]{2,1,0:T(8,128)(2,1)}, bf16[4,160,512]{2,1,0:T(8,128)(2,1)}, u32[]{:S(2)}, u32[]{:S(2)}) %collective-permute-start.33) | collective-permute-done | bytes 655392 | tf_op jit(solution)/shard_map/ppermute | solution.py:444
  176.7 28.7 %shard_map.311 = (f32[1024,1024]{1,0:T(8,128)}, f32[1024,1024]{1,0:T(8,128)}, f32[1024,128]{1,0:T(8,128)}, bf16[2,1024,2048]{2,1,0:T(8,128)(2,1)}, bf16[1024,409...) custom-call(s32[4]{0:T(128)} %copy-done.29, ...), custom_call_target="tpu_custom_call" | custom-call | flops 10737418240 | bytes 41943040 | tf_op jit(solution)/shard_map/pallas_call | solution.py:331
  209.3 10.7 %collective-permute-done.47.refs_7_.refs_23_ = bf16[4,128,512]{2,1,0:T(8,128)(2,1)S(1)} collective-permute-done((bf16[4,128,512]{2,1,0:T(8,128)(2,1)S(1)}, bf16[4,128,512]{2,1,0:T(8,128)(2,1)S(1)}, u32[]{:S(2)}, u32[]{:S(2)}) %collective-permute-start.47) | collective-permute-done | bytes 524320 | tf_op jit(solution)/shard_map/ppermute | solution.py:444
  223.8 21.5 %shard_map.312 = (bf16[1024,1024]{1,0:T(8,128)(2,1)}, f32[1024,1024]{1,0:T(8,128)}, bf16[1024,1024]{1,0:T(8,128)(2,1)}, f32[8,1024]{1,0:T(8,128)}) custom-call(s32[4]{0:T(128)} %copy-done.29, bf16[4,128,512]{2,1,0:T(8,128)(2,1)} %copy-done.59, bf16[4,128,512]{2,1,0:T(8,128)(2,1)} %copy-done.72, bf16[4,128,512]{2,1,0:T(8,128)(2,1)} %copy-done.71, ...), custom_call_target="tpu_custom_call" | custom-call | flops 8589934592 | bytes 41943040 | tf_op jit(solution)/shard_map/pallas_call | solution.py:331
  245.4 9.5 %fusion.13 = bf16[2048,1024]{1,0:T(8,128)(2,1)} fusion(bf16[1024,1024]{1,0:T(8,128)(2,1)} %get-tuple-element.174.refs_33_, bf16[2,1024,2048]{2,1,0:T(8,128)(2,1)} %get-tuple-element.171.refs_18_), kind=kOutput, calls=%fused_computation.13 | convolution fusion | flops 4297064448 | bytes 10485760 | tf_op jit(solution)/shard_map/dot_general | solution.py:29
  255.1 7.0 %fusion.10 = bf16[2048,1024]{1,0:T(8,128)(2,1)S(1)} fusion(bf16[1024,1024]{1,0:T(8,128)(2,1)S(1)} %copy-done.91, bf16[2,1024,2048]{2,1,0:T(8,128)(2,1)} %get-tuple-element.171.refs_18_), kind=kOutput, calls=%fused_computation.12 | convolution fusion | flops 4297064448 | bytes 10485760 | tf_op jit(solution)/shard_map/dot_general | solution.py:29
  271.6 37.0 %shard_map.313 = (bf16[1024,4096]{1,0:T(8,128)(2,1)}, f32[1024,1024]{1,0:T(8,128)}, bf16[1024,1024]{1,0:T(8,128)(2,1)}, bf16[1024,1024]{1,0:T(8,128)(2,1)}, f32[8,1024]{1,0:T(8,128)}, /*index=5*/f32[1,4096]{1,0:T(1,128)}) custom-call(s32[4]{0:T(128)} %copy-done.29, bf16[4,160,512]{2,1,0:T(8,128)(2,1)} %copy-done.57, bf16[4,160,512]{2,1,0:T(8,128)(2,1)} %copy-done.68, ...), custom_call_target="tpu_custom_call" | custom-call | flops 19327352832 | bytes 41943040 | tf_op jit(solution)/shard_map/pallas_call | solution.py:331
  313.4 9.7 %convolution_convert_fusion = bf16[512,4096]{1,0:T(8,128)(2,1)} fusion(bf16[1024,4096]{1,0:T(8,128)(2,1)} %get-tuple-element.189, bf16[2,1024,512]{2,1,0:T(8,128)(2,1)S(1)} %copy-done.89), kind=kOutput, calls=%fused_computation.3 | convolution fusion | flops 4297064448 | bytes 13631488 | tf_op jit(solution)/shard_map/dot_general | solution.py:29
  324.8 8.4 %convolution_convert_fusion.1 = bf16[512,4096]{1,0:T(8,128)(2,1)S(1)} fusion(bf16[1024,4096]{1,0:T(8,128)(2,1)} %get-tuple-element.189, bf16[2,1024,512]{2,1,0:T(8,128)(2,1)S(1)} %copy-done.90), kind=kOutput, calls=%fused_computation.4 | convolution fusion | flops 4297064448 | bytes 13631488 | tf_op jit(solution)/shard_map/dot_general | solution.py:29
  333.8 4.2 fusion.120
  350.4 23.4 %shard_map.314 = (bf16[1024,1536]{1,0:T(8,128)(2,1)}, f32[1,1536]{1,0:T(1,128)S(1)}) custom-call(bf16[1024,3072]{1,0:T(8,128)(2,1)} %copy-done.30, bf16[1024,3072]{1,0:T(8,128)(2,1)} %copy-done.30, bf16[1024,3072]{1,0:T(8,128)(2,1)} %copy-done.30, bf16[1024,1024]{1,0:T(8,128)(2,1)S(1)} %copy-done.32, s32[2,512,1]{2,1,0:T(8,128)S(1)} %copy-done.6, ...), custom_call_target="tpu_custom_call" | custom-call | flops 10737418240 | bytes 25165824 | tf_op jit(solution)/shard_map/pallas_call | solution.py:149
  386.0 5.4 collective-permute-start.67
  413.1 5.2 collective-permute-start.71
  421.0 23.2 %shard_map.315 = (bf16[1024,1536]{1,0:T(8,128)(2,1)}, f32[1,1536]{1,0:T(1,128)S(1)}) custom-call(bf16[1024,3072]{1,0:T(8,128)(2,1)} %copy-done.30, bf16[1024,3072]{1,0:T(8,128)(2,1)} %copy-done.30, bf16[1024,3072]{1,0:T(8,128)(2,1)} %copy-done.30, bf16[1024,1024]{1,0:T(8,128)(2,1)S(1)} %copy-done.32, s32[2,512,1]{2,1,0:T(8,128)S(1)} %copy-done.6, ...), custom_call_target="tpu_custom_call" | custom-call | flops 10737418240 | bytes 25165824 | tf_op jit(solution)/shard_map/pallas_call | solution.py:149
  445.8 5.3 collective-permute-start.73
  454.5 5.1 collective-permute-done.74
  487.0 6.8 %collective-permute-done.80 = bf16[4,2,32,768]{3,2,0,1:T(8,128)(2,1)S(1)} collective-permute-done((bf16[4,2,32,768]{3,2,0,1:T(8,128)(2,1)S(1)}, bf16[4,2,32,768]{3,2,0,1:T(8,128)(2,1)S(1)}, u32[]{:S(2)}, u32[]{:S(2)}) %collective-permute-start.80) | collective-permute-done | bytes 393248 | tf_op jit(solution)/shard_map/ppermute | solution.py:444
  503.0 4.5 collective-permute-start.84
  514.6 4.6 collective-permute-start.85
  525.2 4.6 add_convert_fusion.1
  529.8 5.0 collective-permute-start.86
  538.8 4.5 collective-permute-done.89
  (478 shorter events, 222.8 us)
Async XLA Ops:
  65.6 18.3 %collective-permute-start.9 = (bf16[288,1024]{1,0:T(8,128)(2,1)S(1)}, bf16[288,1024]{1,0:T(8,128)(2,1)S(1)}, u32[]{:S(2)}, u32[]{:S(2)}) collective-permute-start(bf16[288,1024]{1,0:T(8,128)(2,1)S(1)} %collective-permute-done.7.refs_2_), channel_id=1, source_target_pairs={{2,0},{3,1},{4,2},{5,3},{6,4},{7,5},{10,8},{11,9},{12,10},{13,11},... | collective-permute-start | bytes 1769480 | tf_op jit(solution)/shard_map/ppermute | solution.py:447
  84.0 22.6 %collective-permute-start.11 = (bf16[288,1024]{1,0:T(8,128)(2,1)S(1)}, bf16[288,1024]{1,0:T(8,128)(2,1)}, u32[]{:S(2)}, u32[]{:S(2)}) collective-permute-start(bf16[288,1024]{1,0:T(8,128)(2,1)S(1)} %collective-permute-done.9.refs_4_), channel_id=1, source_target_pairs={{2,0},{3,1},{4,2},{5,3},{6,4},{7,5},{10,8},{11,9},{12,10},{13,11},... | collective-permute-start | bytes 1769480 | tf_op jit(solution)/shard_map/ppermute | solution.py:447
  86.7 19.8 %collective-permute-start.10 = (bf16[288,1024]{1,0:T(8,128)(2,1)}, bf16[288,1024]{1,0:T(8,128)(2,1)}, u32[]{:S(2)}, u32[]{:S(2)}) collective-permute-start(bf16[288,1024]{1,0:T(8,128)(2,1)} %collective-permute-done.8.refs_3_), channel_id=1, source_target_pairs={{0,2},{1,3},{2,4},{3,5},{4,6},{5,7},{8,10},{9,11},{10,12},{11,13},... | collective-permute-start | bytes 1769480 | tf_op jit(solution)/shard_map/ppermute | solution.py:447
  111.7 38.3 %collective-permute-start.35 = (bf16[4,160,512]{2,1,0:T(8,128)(2,1)S(1)}, bf16[4,160,512]{2,1,0:T(8,128)(2,1)S(1)}, u32[]{:S(2)}, u32[]{:S(2)}) collective-permute-start(bf16[4,160,512]{2,1,0:T(8,128)(2,1)S(1)} %get-tuple-element.156.refs_9_), channel_id=1, source_target_pairs={{0,8},{1,9},{2,10},{3,11},{4,12},{5,13},{6,14},{7,15},{8,0},{9,1},... | collective-permute-start | bytes 1966088 | tf_op jit(solution)/shard_map/ppermute | solution.py:444
  111.8 35.6 %collective-permute-start.16 = (bf16[4,160,512]{2,1,0:T(8,128)(2,1)S(1)}, bf16[4,160,512]{2,1,0:T(8,128)(2,1)}, u32[]{:S(2)}, u32[]{:S(2)}) collective-permute-start(bf16[4,160,512]{2,1,0:T(8,128)(2,1)S(1)} %get-tuple-element.156.refs_9_), channel_id=1, source_target_pairs={{0,1},{1,0},{2,3},{3,2},{4,5},{5,4},{6,7},{7,6},{8,9},{9,8},{10,11... | collective-permute-start | bytes 1966088 | tf_op jit(solution)/shard_map/ppermute | solution.py:444
  113.4 34.0 %collective-permute-start.15 = (bf16[4,160,512]{2,1,0:T(8,128)(2,1)S(1)}, bf16[4,160,512]{2,1,0:T(8,128)(2,1)}, u32[]{:S(2)}, u32[]{:S(2)}) collective-permute-start(bf16[4,160,512]{2,1,0:T(8,128)(2,1)S(1)} %get-tuple-element.156.refs_9_), channel_id=1, source_target_pairs={{0,16},{1,17},{2,18},{3,19},{4,20},{5,21},{6,22},{7,23},{8,24},{9,... | collective-permute-start | bytes 1966088 | tf_op jit(solution)/shard_map/ppermute | solution.py:444
  113.9 33.5 %collective-permute-start.14 = (bf16[4,160,512]{2,1,0:T(8,128)(2,1)S(1)}, bf16[4,160,512]{2,1,0:T(8,128)(2,1)S(1)}, u32[]{:S(2)}, u32[]{:S(2)}) collective-permute-start(bf16[4,160,512]{2,1,0:T(8,128)(2,1)S(1)} %get-tuple-element.148.refs_1_), channel_id=1, source_target_pairs={{0,16},{1,17},{2,18},{3,19},{4,20},{5,21},{6,22},{7,23},{8,24},{9,... | collective-permute-start | bytes 1966088 | tf_op jit(solution)/shard_map/ppermute | solution.py:444
  115.4 32.0 %collective-permute-start.13 = (bf16[4,160,512]{2,1,0:T(8,128)(2,1)S(1)}, bf16[4,160,512]{2,1,0:T(8,128)(2,1)}, u32[]{:S(2)}, u32[]{:S(2)}) collective-permute-start(bf16[4,160,512]{2,1,0:T(8,128)(2,1)S(1)} %get-tuple-element.148.refs_1_), channel_id=1, source_target_pairs={{0,1},{1,0},{2,3},{3,2},{4,5},{5,4},{6,7},{7,6},{8,9},{9,8},{10,11... | collective-permute-start | bytes 1966088 | tf_op jit(solution)/shard_map/ppermute | solution.py:444
  148.0 17.0 %collective-permute-start.33 = (bf16[4,160,512]{2,1,0:T(8,128)(2,1)}, bf16[4,160,512]{2,1,0:T(8,128)(2,1)}, u32[]{:S(2)}, u32[]{:S(2)}) collective-permute-start(bf16[4,160,512]{2,1,0:T(8,128)(2,1)} %collective-permute-done.13.refs_3_), channel_id=1, source_target_pairs={{0,16},{1,17},{2,18},{3,19},{4,20},{5,21},{6,22},{7,23},{8,24},{9,... | collective-permute-start | bytes 1966088 | tf_op jit(solution)/shard_map/ppermute | solution.py:444
  148.9 16.8 %collective-permute-start.38 = (bf16[4,160,512]{2,1,0:T(8,128)(2,1)}, bf16[4,160,512]{2,1,0:T(8,128)(2,1)}, u32[]{:S(2)}, u32[]{:S(2)}) collective-permute-start(bf16[4,160,512]{2,1,0:T(8,128)(2,1)} %collective-permute-done.15.refs_11_), channel_id=1, source_target_pairs={{0,1},{1,0},{2,3},{3,2},{4,5},{5,4},{6,7},{7,6},{8,9},{9,8},{10,11... | collective-permute-start | bytes 1966088 | tf_op jit(solution)/shard_map/ppermute | solution.py:444
  150.0 22.5 %collective-permute-start.31 = (bf16[4,160,512]{2,1,0:T(8,128)(2,1)}, bf16[4,160,512]{2,1,0:T(8,128)(2,1)}, u32[]{:S(2)}, u32[]{:S(2)}) collective-permute-start(bf16[4,160,512]{2,1,0:T(8,128)(2,1)} %collective-permute-done.13.refs_3_), channel_id=1, source_target_pairs={{0,8},{1,9},{2,10},{3,11},{4,12},{5,13},{6,14},{7,15},{8,0},{9,1},... | collective-permute-start | bytes 1966088 | tf_op jit(solution)/shard_map/ppermute | solution.py:444
  150.1 22.5 %collective-permute-start.36 = (bf16[4,160,512]{2,1,0:T(8,128)(2,1)}, bf16[4,160,512]{2,1,0:T(8,128)(2,1)}, u32[]{:S(2)}, u32[]{:S(2)}) collective-permute-start(bf16[4,160,512]{2,1,0:T(8,128)(2,1)} %collective-permute-done.15.refs_11_), channel_id=1, source_target_pairs={{0,8},{1,9},{2,10},{3,11},{4,12},{5,13},{6,14},{7,15},{8,0},{9,1},... | collective-permute-start | bytes 1966088 | tf_op jit(solution)/shard_map/ppermute | solution.py:444
  150.6 22.0 %collective-permute-start.37 = (bf16[4,160,512]{2,1,0:T(8,128)(2,1)}, bf16[4,160,512]{2,1,0:T(8,128)(2,1)}, u32[]{:S(2)}, u32[]{:S(2)}) collective-permute-start(bf16[4,160,512]{2,1,0:T(8,128)(2,1)} %collective-permute-done.16.refs_13_), channel_id=1, source_target_pairs={{0,8},{1,9},{2,10},{3,11},{4,12},{5,13},{6,14},{7,15},{8,0},{9,1},... | collective-permute-start | bytes 1966088 | tf_op jit(solution)/shard_map/ppermute | solution.py:444
  172.6 32.8 %collective-permute-start.42 = (bf16[4,128,512]{2,1,0:T(8,128)(2,1)S(1)}, bf16[4,128,512]{2,1,0:T(8,128)(2,1)S(1)}, u32[]{:S(2)}, u32[]{:S(2)}) collective-permute-start(bf16[4,128,512]{2,1,0:T(8,128)(2,1)S(1)} %get-tuple-element.146.refs_1_.refs_17_), channel_id=1, source_target_pairs={{0,16},{1,17},{2,18},{3,19},{4,20},{5,21},{6,22},{7,23},{8,24},{9,... | collective-permute-start | bytes 1572872 | tf_op jit(solution)/shard_map/ppermute | solution.py:444
  173.8 31.7 %collective-permute-start.41 = (bf16[4,128,512]{2,1,0:T(8,128)(2,1)S(1)}, bf16[4,128,512]{2,1,0:T(8,128)(2,1)S(1)}, u32[]{:S(2)}, u32[]{:S(2)}) collective-permute-start(bf16[4,128,512]{2,1,0:T(8,128)(2,1)S(1)} %get-tuple-element.146.refs_1_.refs_17_), channel_id=1, source_target_pairs={{0,1},{1,0},{2,3},{3,2},{4,5},{5,4},{6,7},{7,6},{8,9},{9,8},{10,11... | collective-permute-start | bytes 1572872 | tf_op jit(solution)/shard_map/ppermute | solution.py:444
  175.3 33.4 %collective-permute-start.40 = (bf16[4,128,512]{2,1,0:T(8,128)(2,1)S(1)}, bf16[4,128,512]{2,1,0:T(8,128)(2,1)S(1)}, u32[]{:S(2)}, u32[]{:S(2)}) collective-permute-start(bf16[4,128,512]{2,1,0:T(8,128)(2,1)S(1)} %get-tuple-element.146.refs_1_.refs_17_), channel_id=1, source_target_pairs={{0,8},{1,9},{2,10},{3,11},{4,12},{5,13},{6,14},{7,15},{8,0},{9,1},... | collective-permute-start | bytes 1572872 | tf_op jit(solution)/shard_map/ppermute | solution.py:444
  175.3 30.2 %collective-permute-start.44 = (bf16[4,128,512]{2,1,0:T(8,128)(2,1)S(1)}, bf16[4,128,512]{2,1,0:T(8,128)(2,1)S(1)}, u32[]{:S(2)}, u32[]{:S(2)}) collective-permute-start(bf16[4,128,512]{2,1,0:T(8,128)(2,1)S(1)} %get-tuple-element.147.refs_9_.refs_25_), channel_id=1, source_target_pairs={{0,1},{1,0},{2,3},{3,2},{4,5},{5,4},{6,7},{7,6},{8,9},{9,8},{10,11... | collective-permute-start | bytes 1572872 | tf_op jit(solution)/shard_map/ppermute | solution.py:444
  175.8 29.7 %collective-permute-start.43 = (bf16[4,128,512]{2,1,0:T(8,128)(2,1)S(1)}, bf16[4,128,512]{2,1,0:T(8,128)(2,1)}, u32[]{:S(2)}, u32[]{:S(2)}) collective-permute-start(bf16[4,128,512]{2,1,0:T(8,128)(2,1)S(1)} %get-tuple-element.147.refs_9_.refs_25_), channel_id=1, source_target_pairs={{0,16},{1,17},{2,18},{3,19},{4,20},{5,21},{6,22},{7,23},{8,24},{9,... | collective-permute-start | bytes 1572872 | tf_op jit(solution)/shard_map/ppermute | solution.py:444
  269.3 39.4 %collective-permute-start.55 = (bf16[4,2,128,512]{3,2,0,1:T(8,128)(2,1)}, bf16[4,2,128,512]{3,2,0,1:T(8,128)(2,1)}, u32[]{:S(2)}, u32[]{:S(2)}) collective-permute-start(bf16[4,2,128,512]{3,2,0,1:T(8,128)(2,1)} %fusion.22), channel_id=1, source_target_pairs={{0,16},{1,17},{2,18},{3,19},{4,20},{5,21},{6,22},{7,23},{8,24},{9,... | collective-permute-start | bytes 3145736 | tf_op jit(solution)/shard_map/ppermute | solution.py:444
  270.2 38.4 %collective-permute-start.56 = (bf16[2,4,128,512]{3,2,1,0:T(8,128)(2,1)}, bf16[2,4,128,512]{3,2,1,0:T(8,128)(2,1)}, u32[]{:S(2)}, u32[]{:S(2)}) collective-permute-start(bf16[2,4,128,512]{3,2,1,0:T(8,128)(2,1)} %fusion.23), channel_id=1, source_target_pairs={{0,1},{1,0},{2,3},{3,2},{4,5},{5,4},{6,7},{7,6},{8,9},{9,8},{10,11... | collective-permute-start | bytes 3145736 | tf_op jit(solution)/shard_map/ppermute | solution.py:444
  323.1 18.2 %collective-permute-start.58 = (bf16[4,128,512]{2,1,0:T(8,128)(2,1)}, bf16[4,128,512]{2,1,0:T(8,128)(2,1)S(1)}, u32[]{:S(2)}, u32[]{:S(2)}) collective-permute-start(bf16[4,128,512]{2,1,0:T(8,128)(2,1)} %fusion.37), channel_id=1, source_target_pairs={{0,1},{1,0},{2,3},{3,2},{4,5},{5,4},{6,7},{7,6},{8,9},{9,8},{10,11... | collective-permute-start | bytes 1572872 | tf_op jit(solution)/shard_map/ppermute | solution.py:444
  323.7 17.7 %collective-permute-start.59 = (bf16[4,128,512]{2,1,0:T(8,128)(2,1)}, bf16[4,128,512]{2,1,0:T(8,128)(2,1)S(1)}, u32[]{:S(2)}, u32[]{:S(2)}) collective-permute-start(bf16[4,128,512]{2,1,0:T(8,128)(2,1)} %fusion.36), channel_id=1, source_target_pairs={{0,16},{1,17},{2,18},{3,19},{4,20},{5,21},{6,22},{7,23},{8,24},{9,... | collective-permute-start | bytes 1572872 | tf_op jit(solution)/shard_map/ppermute | solution.py:444
  345.4 28.4 %collective-permute-start.60 = (bf16[4,2,32,2048]{3,2,0,1:T(8,128)(2,1)}, bf16[4,2,32,2048]{3,2,0,1:T(8,128)(2,1)}, u32[]{:S(2)}, u32[]{:S(2)}) collective-permute-start(bf16[4,2,32,2048]{3,2,0,1:T(8,128)(2,1)} %fusion.24), channel_id=1, source_target_pairs={{0,16},{1,17},{2,18},{3,19},{4,20},{5,21},{6,22},{7,23},{8,24},{9,... | collective-permute-start | bytes 3145736 | tf_op jit(solution)/shard_map/ppermute | solution.py:444
  346.3 27.5 %collective-permute-start.61 = (bf16[2,4,32,2048]{3,2,1,0:T(8,128)(2,1)}, bf16[2,4,32,2048]{3,2,1,0:T(8,128)(2,1)}, u32[]{:S(2)}, u32[]{:S(2)}) collective-permute-start(bf16[2,4,32,2048]{3,2,1,0:T(8,128)(2,1)} %fusion.25), channel_id=1, source_target_pairs={{0,1},{1,0},{2,3},{3,2},{4,5},{5,4},{6,7},{7,6},{8,9},{9,8},{10,11... | collective-permute-start | bytes 3145736 | tf_op jit(solution)/shard_map/ppermute | solution.py:444
  347.7 26.0 %collective-permute-start.62 = (bf16[128,1024]{1,0:T(8,128)(2,1)}, bf16[128,1024]{1,0:T(8,128)(2,1)S(1)}, u32[]{:S(2)}, u32[]{:S(2)}) collective-permute-start(bf16[128,1024]{1,0:T(8,128)(2,1)} %get-tuple-element.199), channel_id=1, source_target_pairs={{0,2},{1,3},{2,4},{3,5},{4,6},{5,7},{8,10},{9,11},{10,12},{11,13},... | collective-permute-start | bytes 786440 | tf_op jit(solution)/shard_map/ppermute | solution.py:447
  349.0 24.7 %collective-permute-start.63 = (bf16[128,1024]{1,0:T(8,128)(2,1)S(1)}, bf16[128,1024]{1,0:T(8,128)(2,1)S(1)}, u32[]{:S(2)}, u32[]{:S(2)}) collective-permute-start(bf16[128,1024]{1,0:T(8,128)(2,1)S(1)} %get-tuple-element.200), channel_id=1, source_target_pairs={{2,0},{3,1},{4,2},{5,3},{6,4},{7,5},{10,8},{11,9},{12,10},{13,11},... | collective-permute-start | bytes 786440 | tf_op jit(solution)/shard_map/ppermute | solution.py:447
  385.2 16.5 %collective-permute-start.64 = (bf16[512,2560]{1,0:T(8,128)(2,1)}, bf16[512,2560]{1,0:T(8,128)(2,1)}, u32[]{:S(2)}, u32[]{:S(2)}) collective-permute-start(bf16[512,2560]{1,0:T(8,128)(2,1)} %pad_maximum_fusion.1), channel_id=1, source_target_pairs={{0,8},{1,9},{2,10},{3,11},{4,12},{5,13},{6,14},{7,15},{8,0},{9,1},... | collective-permute-start | bytes 7864328 | tf_op jit(solution)/shard_map/ppermute | solution.py:444
  386.0 20.8 %collective-permute-start.67 = (bf16[128,1024]{1,0:T(8,128)(2,1)}, bf16[128,1024]{1,0:T(8,128)(2,1)S(1)}, u32[]{:S(2)}, u32[]{:S(2)}) collective-permute-start(bf16[128,1024]{1,0:T(8,128)(2,1)} %get-tuple-element.216), channel_id=1, source_target_pairs={{0,2},{1,3},{2,4},{3,5},{4,6},{5,7},{8,10},{9,11},{10,12},{11,13},... | collective-permute-start | bytes 786440 | tf_op jit(solution)/shard_map/ppermute | solution.py:447
  413.1 37.9 %collective-permute-start.71 = (bf16[32,4096]{1,0:T(8,128)(2,1)S(1)}, bf16[32,4096]{1,0:T(8,128)(2,1)}, u32[]{:S(2)}, u32[]{:S(2)}) collective-permute-start(bf16[32,4096]{1,0:T(8,128)(2,1)S(1)} %get-tuple-element.227), channel_id=1, source_target_pairs={{0,2},{1,3},{2,4},{3,5},{4,6},{5,7},{8,10},{9,11},{10,12},{11,13},... | collective-permute-start | bytes 786440 | tf_op jit(solution)/shard_map/ppermute | solution.py:447
  418.3 41.3 %collective-permute-start.69 = (bf16[4,2,32,1280]{3,2,0,1:T(8,128)(2,1)}, bf16[4,2,32,1280]{3,2,0,1:T(8,128)(2,1)}, u32[]{:S(2)}, u32[]{:S(2)}) collective-permute-start(bf16[4,2,32,1280]{3,2,0,1:T(8,128)(2,1)} %fusion.54), channel_id=1, source_target_pairs={{0,16},{1,17},{2,18},{3,19},{4,20},{5,21},{6,22},{7,23},{8,24},{9,... | collective-permute-start | bytes 1966088 | tf_op jit(solution)/shard_map/ppermute | solution.py:444
  419.5 40.1 %collective-permute-start.70 = (bf16[2,4,32,1280]{3,2,1,0:T(8,128)(2,1)}, bf16[2,4,32,1280]{3,2,1,0:T(8,128)(2,1)}, u32[]{:S(2)}, u32[]{:S(2)}) collective-permute-start(bf16[2,4,32,1280]{3,2,1,0:T(8,128)(2,1)} %fusion.55), channel_id=1, source_target_pairs={{0,1},{1,0},{2,3},{3,2},{4,5},{5,4},{6,7},{7,6},{8,9},{9,8},{10,11... | collective-permute-start | bytes 1966088 | tf_op jit(solution)/shard_map/ppermute | solution.py:444
  519.3 17.0 %collective-permute-start.90 = (bf16[32,4096]{1,0:T(8,128)(2,1)S(1)}, bf16[32,4096]{1,0:T(8,128)(2,1)S(1)}, u32[]{:S(2)}, u32[]{:S(2)}) collective-permute-start(bf16[32,4096]{1,0:T(8,128)(2,1)S(1)} %get-tuple-element.289), channel_id=1, source_target_pairs={{0,2},{1,3},{2,4},{3,5},{4,6},{5,7},{8,10},{9,11},{10,12},{11,13},... | collective-permute-start | bytes 786440 | tf_op jit(solution)/shard_map/ppermute | solution.py:447
  (155 other events, 1506.3 us)

commit v4 on v3

--- a/solution.py
+++ b/solution.py
@@ -635,9 +635,21 @@
     return jnp.concatenate([p[:, i : i + HALF] for i in (0, HALF) for p in parts], axis=1)
 
 
+def small_kernel(*refs):
+    rows = []
+    for ref in refs[:-1]:
+        row = ref[...].astype(jnp.float32)
+        if row.shape[1] < 128:
+            row = jnp.concatenate([row, jnp.zeros((1, 128 - row.shape[1]), jnp.float32)], axis=1)
+        rows.append(row)
+    rows.append(jnp.zeros((refs[-1].shape[0] - len(rows), 128), jnp.float32))
+    refs[-1][...] = jnp.concatenate(rows, axis=0).astype(jnp.bfloat16)
+
+
 def pack_small(smalls, rows):
-    flat = jnp.concatenate(smalls)
-    return jnp.pad(flat, (0, rows * 128 - flat.size)).reshape(rows, 128)
+    return pl.pallas_call(
+        small_kernel, out_shape=jax.ShapeDtypeStruct((rows, 128), jnp.bfloat16)
+    )(*[small[None] for small in smalls])
 
 
 def pack_first(spot, attn, small):
@@ -704,11 +716,9 @@
 
 
 def split_small(small, widths):
-    results, start = [], 0
-    for width in widths:
-        results.append(small[:, start : start + width].reshape(-1).astype(jnp.float32))
-        start += width
-    return results
+    return [
+        small[:, i, :width].reshape(-1).astype(jnp.float32) for i, width in enumerate(widths)
+    ]
 
 
 def hold(later, *ready):
@@ -762,7 +772,7 @@
         gather = Gather(grid, first)
         gather.start()
         whole = assemble(grid, spot, gather.parts([(0, rows, 0, 0)]), (rows, 3 * D + 128))
-        full_qkv, small = whole[:, : 3 * D], whole[:, 3 * D :].reshape(grid.count, -1)
+        full_qkv, small = whole[:, : 3 * D], whole[:, 3 * D :].reshape(grid.count, rows, 128)
         line = line_gather(grid, spot, rest)
         low_tokens, line = hold(tokens, line)
         split = rows + rows * wide // D
@@ -773,8 +783,8 @@
             lax.all_gather(w, AXES, axis=0, tiled=True)
             for w in (by_halves(attn), w_out, w_up, w_down)
         )
-        small = lax.all_gather(jnp.concatenate(smalls), AXES, axis=0, tiled=True)
-        small = small.reshape(grid.count, -1)
+        small = jnp.stack([jnp.pad(v, (0, max(widths) - v.shape[0])) for v in smalls])
+        small = lax.all_gather(small[None], AXES, axis=0, tiled=True)
     bias_query, bias_value, *others, bias_up = split_small(small, widths)
     vectors = jnp.stack(others + [jnp.zeros_like(bias_query)] * 2)
     doc_row, doc_column = segment_ids[:, None, :], segment_ids[:, :, None]

time: 554 us -> 550 us (level)
  local copies, waits for them, and re-layouts: 59.3 us -> 53.7 us
    concatenate x1 -> x0, local copies, waits for them, and re-layouts: 6.09 us -> none  [pack_small(): flat = jnp.concatenate(smalls)]
    unnamed x195 -> x197, local copies, waits for them, and re-layouts: 28.2 us -> 28.8 us
  transfers between devices with their start and end apart: 92 -> 92, of which waited for: 28 -> 29; matrix products, arithmetic and copies ran while one was open for 14% -> 14% of each run, Pallas kernels for 25% -> 25%
where the time goes in v4:
time: 550 us; the launch traced here: 544 us
  Pallas kernels  167 us (30%)
  starting transfers between devices  126 us (23%)
  waiting for transfers between devices  81.3 us (15%)
  matrix products  66.3 us (12%)
  local copies, waits for them, and re-layouts  53.7 us (10%)
  other arithmetic  47.4 us (9%)
    pallas_call x3, Pallas kernels, middle_call(): pl.pallas_call(functools.partial(kernel, plan), grid=(rows // TILE,), out...  87.2 us
    ppermute x30, starting transfers between devices, along(): return lax.ppermute(values, AXES, self.shifted(axis, step, False))  85.2 us
    ppermute x62, waiting for transfers between devices, swap(): return lax.ppermute(values, AXES, self.shifted(axis, 1, True))  53.7 us
    dot_general x10, matrix products, outer_sum(): lax.dot_general(operand, other, (((0,), (0,)), ((), ())), preferred_eleme...  51.1 us
    pallas_call x2, Pallas kernels, attend_backward(): pl.pallas_call(attend_backward_kernel, grid=(seqs, PAIRS), out_shape=[jax...  46.6 us
    ppermute x62, starting transfers between devices, swap(): return lax.ppermute(values, AXES, self.shifted(axis, 1, True))  40.3 us
    unnamed x197, local copies, waits for them, and re-layouts  28.8 us
    ppermute x30, waiting for transfers between devices, along(): return lax.ppermute(values, AXES, self.shifted(axis, step, False))  27.6 us
  transfers between devices with their start and end apart: 92, of which 29 were waited for; matrix products, arithmetic and copies ran while one was open for 14% of the time, Pallas kernels for 25%

profile of v4, /device:TPU:0, one launch (start us, length us, event | category | flops | bytes accessed | tf_op | source)
XLA Modules:
  0.0 543.8 jit_solution(8585444269123679786)
XLA Ops:
  7.4 5.6 %collective-permute-start = (bf16[32,3200]{1,0:T(8,128)(2,1)S(1)}, bf16[32,3200]{1,0:T(8,128)(2,1)S(1)}, u32[]{:S(2)}, u32[]{:S(2)}) collective-permute-start(bf16[32,3200]{1,0:T(8,128)(2,1)S(1)} %shard_map.307.refs_0_), channel_id=1, source_target_pairs={{0,2},{1,3},{2,4},{3,5},{4,6},{5,7},{8,10},{9,11},{10,12},{11,13},... | collective-permute-start | bytes 614408 | tf_op jit(solution)/shard_map/ppermute | solution.py:447
  17.4 4.6 collective-permute-start.2
  25.5 4.6 collective-permute-start.4
  39.7 7.1 %collective-permute-done.20.refs_4_ = bf16[4,32,1536]{2,1,0:T(8,128)(2,1)S(1)} collective-permute-done((bf16[4,32,1536]{2,1,0:T(8,128)(2,1)S(1)}, bf16[4,32,1536]{2,1,0:T(8,128)(2,1)S(1)}, u32[]{:S(2)}, u32[]{:S(2)}) %collective-permute-start.20) | collective-permute-done | bytes 393248 | tf_op jit(solution)/shard_map/ppermute | solution.py:444
  48.5 4.1 collective-permute-start.6
  66.6 4.4 collective-permute-start.8
  74.1 5.9 %collective-permute-done.9.refs_4_ = bf16[288,1024]{1,0:T(8,128)(2,1)S(1)} collective-permute-done((bf16[288,1024]{1,0:T(8,128)(2,1)S(1)}, bf16[288,1024]{1,0:T(8,128)(2,1)S(1)}, u32[]{:S(2)}, u32[]{:S(2)}) %collective-permute-start.9) | collective-permute-done | bytes 589856 | tf_op jit(solution)/shard_map/ppermute | solution.py:447
  82.6 5.3 collective-permute-start.10
  111.9 7.1 %add_convert_fusion.query.key.value = bf16[1024,3072]{1,0:T(8,128)(2,1)S(1)} fusion(f32[3072]{0:T(1024)S(1)} %bitcast.369, bf16[1024,1024]{1,0:T(8,128)(2,1)S(1)} %copy-done.66, bf16[1024,3200]{1,0:T(8,128)(2,1)S(1)} %bitcast.340), kind=kOutput, calls=%fused_computation | convolution fusion | flops 6448742400 | bytes 14692352 | tf_op jit(solution)/shard_map/dot_general | solution.py:19
  119.0 23.0 %shard_map.311.refs_17_ = bf16[1024,1024]{1,0:T(8,128)(2,1)S(1)} custom-call(bf16[1024,3072]{1,0:T(8,128)(2,1)S(1)} %add_convert_fusion.query.key.value, bf16[1024,3072]{1,0:T(8,128)(2,1)S(1)} %add_convert_fusion.query.key.value, bf16[1024,3072]{1,0:T(8,128)(2,1)S(1)} %add_convert_fusion.query.key.value, s32[2,512,1]{2,1,0:T(8,128)S(1)} %copy-done.6, ...), custom_call_target="tpu_custom_call" | custom-call | flops 8589934592 | bytes 25165824 | tf_op jit(solution)/shard_map/pallas_call | solution.py:132
  146.6 14.4 %collective-permute-done.33.refs_7_ = bf16[4,160,512]{2,1,0:T(8,128)(2,1)} collective-permute-done((bf16[4,160,512]{2,1,0:T(8,128)(2,1)}, bf16[4,160,512]{2,1,0:T(8,128)(2,1)}, u32[]{:S(2)}, u32[]{:S(2)}) %collective-permute-start.33) | collective-permute-done | bytes 655392 | tf_op jit(solution)/shard_map/ppermute | solution.py:444
  172.8 28.8 %shard_map.312 = (f32[1024,1024]{1,0:T(8,128)}, f32[1024,1024]{1,0:T(8,128)}, f32[1024,128]{1,0:T(8,128)}, bf16[2,1024,2048]{2,1,0:T(8,128)(2,1)}, bf16[1024,409...) custom-call(s32[4]{0:T(128)} %copy-done.30, ...), custom_call_target="tpu_custom_call" | custom-call | flops 10737418240 | bytes 41943040 | tf_op jit(solution)/shard_map/pallas_call | solution.py:331
  205.6 10.6 %collective-permute-done.47.refs_7_.refs_23_ = bf16[4,128,512]{2,1,0:T(8,128)(2,1)S(1)} collective-permute-done((bf16[4,128,512]{2,1,0:T(8,128)(2,1)S(1)}, bf16[4,128,512]{2,1,0:T(8,128)(2,1)S(1)}, u32[]{:S(2)}, u32[]{:S(2)}) %collective-permute-start.47) | collective-permute-done | bytes 524320 | tf_op jit(solution)/shard_map/ppermute | solution.py:444
  220.1 21.5 %shard_map.313 = (bf16[1024,1024]{1,0:T(8,128)(2,1)}, f32[1024,1024]{1,0:T(8,128)}, bf16[1024,1024]{1,0:T(8,128)(2,1)}, f32[8,1024]{1,0:T(8,128)}) custom-call(s32[4]{0:T(128)} %copy-done.30, bf16[4,128,512]{2,1,0:T(8,128)(2,1)} %copy-done.61, bf16[4,128,512]{2,1,0:T(8,128)(2,1)} %copy-done.73, bf16[4,128,512]{2,1,0:T(8,128)(2,1)} %copy-done.72, ...), custom_call_target="tpu_custom_call" | custom-call | flops 8589934592 | bytes 41943040 | tf_op jit(solution)/shard_map/pallas_call | solution.py:331
  241.6 9.6 %fusion.13 = bf16[2048,1024]{1,0:T(8,128)(2,1)} fusion(bf16[1024,1024]{1,0:T(8,128)(2,1)} %get-tuple-element.174.refs_33_, bf16[2,1024,2048]{2,1,0:T(8,128)(2,1)} %get-tuple-element.171.refs_18_), kind=kOutput, calls=%fused_computation.13 | convolution fusion | flops 4297064448 | bytes 10485760 | tf_op jit(solution)/shard_map/dot_general | solution.py:29
  251.4 7.0 %fusion.10 = bf16[2048,1024]{1,0:T(8,128)(2,1)S(1)} fusion(bf16[1024,1024]{1,0:T(8,128)(2,1)S(1)} %copy-done.92, bf16[2,1024,2048]{2,1,0:T(8,128)(2,1)} %get-tuple-element.171.refs_18_), kind=kOutput, calls=%fused_computation.12 | convolution fusion | flops 4297064448 | bytes 10485760 | tf_op jit(solution)/shard_map/dot_general | solution.py:29
  268.0 36.9 %shard_map.314 = (bf16[1024,4096]{1,0:T(8,128)(2,1)}, f32[1024,1024]{1,0:T(8,128)}, bf16[1024,1024]{1,0:T(8,128)(2,1)}, bf16[1024,1024]{1,0:T(8,128)(2,1)}, f32[8,1024]{1,0:T(8,128)}, /*index=5*/f32[1,4096]{1,0:T(1,128)}) custom-call(s32[4]{0:T(128)} %copy-done.30, bf16[4,160,512]{2,1,0:T(8,128)(2,1)} %copy-done.58, bf16[4,160,512]{2,1,0:T(8,128)(2,1)} %copy-done.69, ...), custom_call_target="tpu_custom_call" | custom-call | flops 19327352832 | bytes 41943040 | tf_op jit(solution)/shard_map/pallas_call | solution.py:331
  309.7 9.7 %convolution_convert_fusion = bf16[512,4096]{1,0:T(8,128)(2,1)} fusion(bf16[1024,4096]{1,0:T(8,128)(2,1)} %get-tuple-element.189, bf16[2,1024,512]{2,1,0:T(8,128)(2,1)S(1)} %copy-done.90), kind=kOutput, calls=%fused_computation.3 | convolution fusion | flops 4297064448 | bytes 13631488 | tf_op jit(solution)/shard_map/dot_general | solution.py:29
  321.1 8.4 %convolution_convert_fusion.1 = bf16[512,4096]{1,0:T(8,128)(2,1)S(1)} fusion(bf16[1024,4096]{1,0:T(8,128)(2,1)} %get-tuple-element.189, bf16[2,1024,512]{2,1,0:T(8,128)(2,1)S(1)} %copy-done.91), kind=kOutput, calls=%fused_computation.4 | convolution fusion | flops 4297064448 | bytes 13631488 | tf_op jit(solution)/shard_map/dot_general | solution.py:29
  330.1 4.2 fusion.129
  346.7 23.4 %shard_map.315 = (bf16[1024,1536]{1,0:T(8,128)(2,1)}, f32[1,1536]{1,0:T(1,128)S(1)}) custom-call(bf16[1024,3072]{1,0:T(8,128)(2,1)} %copy-done.31, bf16[1024,3072]{1,0:T(8,128)(2,1)} %copy-done.31, bf16[1024,3072]{1,0:T(8,128)(2,1)} %copy-done.31, bf16[1024,1024]{1,0:T(8,128)(2,1)S(1)} %copy-done.33, s32[2,512,1]{2,1,0:T(8,128)S(1)} %copy-done.6, ...), custom_call_target="tpu_custom_call" | custom-call | flops 10737418240 | bytes 25165824 | tf_op jit(solution)/shard_map/pallas_call | solution.py:149
  382.3 5.3 collective-permute-start.67
  409.4 5.2 collective-permute-start.71
  417.3 23.2 %shard_map.316 = (bf16[1024,1536]{1,0:T(8,128)(2,1)}, f32[1,1536]{1,0:T(1,128)S(1)}) custom-call(bf16[1024,3072]{1,0:T(8,128)(2,1)} %copy-done.31, bf16[1024,3072]{1,0:T(8,128)(2,1)} %copy-done.31, bf16[1024,3072]{1,0:T(8,128)(2,1)} %copy-done.31, bf16[1024,1024]{1,0:T(8,128)(2,1)S(1)} %copy-done.33, s32[2,512,1]{2,1,0:T(8,128)S(1)} %copy-done.6, ...), custom_call_target="tpu_custom_call" | custom-call | flops 10737418240 | bytes 25165824 | tf_op jit(solution)/shard_map/pallas_call | solution.py:149
  442.1 5.3 collective-permute-start.73
  450.8 5.1 collective-permute-done.74
  483.3 6.8 %collective-permute-done.80 = bf16[4,2,32,768]{3,2,0,1:T(8,128)(2,1)S(1)} collective-permute-done((bf16[4,2,32,768]{3,2,0,1:T(8,128)(2,1)S(1)}, bf16[4,2,32,768]{3,2,0,1:T(8,128)(2,1)S(1)}, u32[]{:S(2)}, u32[]{:S(2)}) %collective-permute-start.80) | collective-permute-done | bytes 393248 | tf_op jit(solution)/shard_map/ppermute | solution.py:444
  499.3 4.5 collective-permute-start.84
  510.9 4.6 collective-permute-start.85
  521.5 4.6 add_convert_fusion.1
  526.1 5.0 collective-permute-start.86
  535.1 4.5 collective-permute-done.89
  (478 shorter events, 220.8 us)
Async XLA Ops:
  61.7 18.3 %collective-permute-start.9 = (bf16[288,1024]{1,0:T(8,128)(2,1)S(1)}, bf16[288,1024]{1,0:T(8,128)(2,1)S(1)}, u32[]{:S(2)}, u32[]{:S(2)}) collective-permute-start(bf16[288,1024]{1,0:T(8,128)(2,1)S(1)} %collective-permute-done.7.refs_2_), channel_id=1, source_target_pairs={{2,0},{3,1},{4,2},{5,3},{6,4},{7,5},{10,8},{11,9},{12,10},{13,11},... | collective-permute-start | bytes 1769480 | tf_op jit(solution)/shard_map/ppermute | solution.py:447
  80.0 22.5 %collective-permute-start.11 = (bf16[288,1024]{1,0:T(8,128)(2,1)S(1)}, bf16[288,1024]{1,0:T(8,128)(2,1)}, u32[]{:S(2)}, u32[]{:S(2)}) collective-permute-start(bf16[288,1024]{1,0:T(8,128)(2,1)S(1)} %collective-permute-done.9.refs_4_), channel_id=1, source_target_pairs={{2,0},{3,1},{4,2},{5,3},{6,4},{7,5},{10,8},{11,9},{12,10},{13,11},... | collective-permute-start | bytes 1769480 | tf_op jit(solution)/shard_map/ppermute | solution.py:447
  82.6 19.9 %collective-permute-start.10 = (bf16[288,1024]{1,0:T(8,128)(2,1)}, bf16[288,1024]{1,0:T(8,128)(2,1)}, u32[]{:S(2)}, u32[]{:S(2)}) collective-permute-start(bf16[288,1024]{1,0:T(8,128)(2,1)} %collective-permute-done.8.refs_3_), channel_id=1, source_target_pairs={{0,2},{1,3},{2,4},{3,5},{4,6},{5,7},{8,10},{9,11},{10,12},{11,13},... | collective-permute-start | bytes 1769480 | tf_op jit(solution)/shard_map/ppermute | solution.py:447
  107.7 38.3 %collective-permute-start.35 = (bf16[4,160,512]{2,1,0:T(8,128)(2,1)S(1)}, bf16[4,160,512]{2,1,0:T(8,128)(2,1)S(1)}, u32[]{:S(2)}, u32[]{:S(2)}) collective-permute-start(bf16[4,160,512]{2,1,0:T(8,128)(2,1)S(1)} %get-tuple-element.156.refs_9_), channel_id=1, source_target_pairs={{0,8},{1,9},{2,10},{3,11},{4,12},{5,13},{6,14},{7,15},{8,0},{9,1},... | collective-permute-start | bytes 1966088 | tf_op jit(solution)/shard_map/ppermute | solution.py:444
  107.8 35.6 %collective-permute-start.16 = (bf16[4,160,512]{2,1,0:T(8,128)(2,1)S(1)}, bf16[4,160,512]{2,1,0:T(8,128)(2,1)}, u32[]{:S(2)}, u32[]{:S(2)}) collective-permute-start(bf16[4,160,512]{2,1,0:T(8,128)(2,1)S(1)} %get-tuple-element.156.refs_9_), channel_id=1, source_target_pairs={{0,1},{1,0},{2,3},{3,2},{4,5},{5,4},{6,7},{7,6},{8,9},{9,8},{10,11... | collective-permute-start | bytes 1966088 | tf_op jit(solution)/shard_map/ppermute | solution.py:444
  109.4 34.0 %collective-permute-start.15 = (bf16[4,160,512]{2,1,0:T(8,128)(2,1)S(1)}, bf16[4,160,512]{2,1,0:T(8,128)(2,1)}, u32[]{:S(2)}, u32[]{:S(2)}) collective-permute-start(bf16[4,160,512]{2,1,0:T(8,128)(2,1)S(1)} %get-tuple-element.156.refs_9_), channel_id=1, source_target_pairs={{0,16},{1,17},{2,18},{3,19},{4,20},{5,21},{6,22},{7,23},{8,24},{9,... | collective-permute-start | bytes 1966088 | tf_op jit(solution)/shard_map/ppermute | solution.py:444
  109.9 33.5 %collective-permute-start.14 = (bf16[4,160,512]{2,1,0:T(8,128)(2,1)S(1)}, bf16[4,160,512]{2,1,0:T(8,128)(2,1)S(1)}, u32[]{:S(2)}, u32[]{:S(2)}) collective-permute-start(bf16[4,160,512]{2,1,0:T(8,128)(2,1)S(1)} %get-tuple-element.148.refs_1_), channel_id=1, source_target_pairs={{0,16},{1,17},{2,18},{3,19},{4,20},{5,21},{6,22},{7,23},{8,24},{9,... | collective-permute-start | bytes 1966088 | tf_op jit(solution)/shard_map/ppermute | solution.py:444
  111.4 32.0 %collective-permute-start.13 = (bf16[4,160,512]{2,1,0:T(8,128)(2,1)S(1)}, bf16[4,160,512]{2,1,0:T(8,128)(2,1)}, u32[]{:S(2)}, u32[]{:S(2)}) collective-permute-start(bf16[4,160,512]{2,1,0:T(8,128)(2,1)S(1)} %get-tuple-element.148.refs_1_), channel_id=1, source_target_pairs={{0,1},{1,0},{2,3},{3,2},{4,5},{5,4},{6,7},{7,6},{8,9},{9,8},{10,11... | collective-permute-start | bytes 1966088 | tf_op jit(solution)/shard_map/ppermute | solution.py:444
  143.9 17.0 %collective-permute-start.33 = (bf16[4,160,512]{2,1,0:T(8,128)(2,1)}, bf16[4,160,512]{2,1,0:T(8,128)(2,1)}, u32[]{:S(2)}, u32[]{:S(2)}) collective-permute-start(bf16[4,160,512]{2,1,0:T(8,128)(2,1)} %collective-permute-done.13.refs_3_), channel_id=1, source_target_pairs={{0,16},{1,17},{2,18},{3,19},{4,20},{5,21},{6,22},{7,23},{8,24},{9,... | collective-permute-start | bytes 1966088 | tf_op jit(solution)/shard_map/ppermute | solution.py:444
  144.8 16.8 %collective-permute-start.38 = (bf16[4,160,512]{2,1,0:T(8,128)(2,1)}, bf16[4,160,512]{2,1,0:T(8,128)(2,1)}, u32[]{:S(2)}, u32[]{:S(2)}) collective-permute-start(bf16[4,160,512]{2,1,0:T(8,128)(2,1)} %collective-permute-done.15.refs_11_), channel_id=1, source_target_pairs={{0,1},{1,0},{2,3},{3,2},{4,5},{5,4},{6,7},{7,6},{8,9},{9,8},{10,11... | collective-permute-start | bytes 1966088 | tf_op jit(solution)/shard_map/ppermute | solution.py:444
  146.0 22.6 %collective-permute-start.31 = (bf16[4,160,512]{2,1,0:T(8,128)(2,1)}, bf16[4,160,512]{2,1,0:T(8,128)(2,1)}, u32[]{:S(2)}, u32[]{:S(2)}) collective-permute-start(bf16[4,160,512]{2,1,0:T(8,128)(2,1)} %collective-permute-done.13.refs_3_), channel_id=1, source_target_pairs={{0,8},{1,9},{2,10},{3,11},{4,12},{5,13},{6,14},{7,15},{8,0},{9,1},... | collective-permute-start | bytes 1966088 | tf_op jit(solution)/shard_map/ppermute | solution.py:444
  146.0 22.6 %collective-permute-start.36 = (bf16[4,160,512]{2,1,0:T(8,128)(2,1)}, bf16[4,160,512]{2,1,0:T(8,128)(2,1)}, u32[]{:S(2)}, u32[]{:S(2)}) collective-permute-start(bf16[4,160,512]{2,1,0:T(8,128)(2,1)} %collective-permute-done.15.refs_11_), channel_id=1, source_target_pairs={{0,8},{1,9},{2,10},{3,11},{4,12},{5,13},{6,14},{7,15},{8,0},{9,1},... | collective-permute-start | bytes 1966088 | tf_op jit(solution)/shard_map/ppermute | solution.py:444
  146.5 22.1 %collective-permute-start.37 = (bf16[4,160,512]{2,1,0:T(8,128)(2,1)}, bf16[4,160,512]{2,1,0:T(8,128)(2,1)}, u32[]{:S(2)}, u32[]{:S(2)}) collective-permute-start(bf16[4,160,512]{2,1,0:T(8,128)(2,1)} %collective-permute-done.16.refs_13_), channel_id=1, source_target_pairs={{0,8},{1,9},{2,10},{3,11},{4,12},{5,13},{6,14},{7,15},{8,0},{9,1},... | collective-permute-start | bytes 1966088 | tf_op jit(solution)/shard_map/ppermute | solution.py:444
  168.7 33.0 %collective-permute-start.42 = (bf16[4,128,512]{2,1,0:T(8,128)(2,1)S(1)}, bf16[4,128,512]{2,1,0:T(8,128)(2,1)S(1)}, u32[]{:S(2)}, u32[]{:S(2)}) collective-permute-start(bf16[4,128,512]{2,1,0:T(8,128)(2,1)S(1)} %get-tuple-element.146.refs_1_.refs_17_), channel_id=1, source_target_pairs={{0,16},{1,17},{2,18},{3,19},{4,20},{5,21},{6,22},{7,23},{8,24},{9,... | collective-permute-start | bytes 1572872 | tf_op jit(solution)/shard_map/ppermute | solution.py:444
  169.9 31.9 %collective-permute-start.41 = (bf16[4,128,512]{2,1,0:T(8,128)(2,1)S(1)}, bf16[4,128,512]{2,1,0:T(8,128)(2,1)S(1)}, u32[]{:S(2)}, u32[]{:S(2)}) collective-permute-start(bf16[4,128,512]{2,1,0:T(8,128)(2,1)S(1)} %get-tuple-element.146.refs_1_.refs_17_), channel_id=1, source_target_pairs={{0,1},{1,0},{2,3},{3,2},{4,5},{5,4},{6,7},{7,6},{8,9},{9,8},{10,11... | collective-permute-start | bytes 1572872 | tf_op jit(solution)/shard_map/ppermute | solution.py:444
  171.4 33.6 %collective-permute-start.40 = (bf16[4,128,512]{2,1,0:T(8,128)(2,1)S(1)}, bf16[4,128,512]{2,1,0:T(8,128)(2,1)S(1)}, u32[]{:S(2)}, u32[]{:S(2)}) collective-permute-start(bf16[4,128,512]{2,1,0:T(8,128)(2,1)S(1)} %get-tuple-element.146.refs_1_.refs_17_), channel_id=1, source_target_pairs={{0,8},{1,9},{2,10},{3,11},{4,12},{5,13},{6,14},{7,15},{8,0},{9,1},... | collective-permute-start | bytes 1572872 | tf_op jit(solution)/shard_map/ppermute | solution.py:444
  171.4 30.4 %collective-permute-start.44 = (bf16[4,128,512]{2,1,0:T(8,128)(2,1)S(1)}, bf16[4,128,512]{2,1,0:T(8,128)(2,1)S(1)}, u32[]{:S(2)}, u32[]{:S(2)}) collective-permute-start(bf16[4,128,512]{2,1,0:T(8,128)(2,1)S(1)} %get-tuple-element.147.refs_9_.refs_25_), channel_id=1, source_target_pairs={{0,1},{1,0},{2,3},{3,2},{4,5},{5,4},{6,7},{7,6},{8,9},{9,8},{10,11... | collective-permute-start | bytes 1572872 | tf_op jit(solution)/shard_map/ppermute | solution.py:444
  171.9 29.9 %collective-permute-start.43 = (bf16[4,128,512]{2,1,0:T(8,128)(2,1)S(1)}, bf16[4,128,512]{2,1,0:T(8,128)(2,1)}, u32[]{:S(2)}, u32[]{:S(2)}) collective-permute-start(bf16[4,128,512]{2,1,0:T(8,128)(2,1)S(1)} %get-tuple-element.147.refs_9_.refs_25_), channel_id=1, source_target_pairs={{0,16},{1,17},{2,18},{3,19},{4,20},{5,21},{6,22},{7,23},{8,24},{9,... | collective-permute-start | bytes 1572872 | tf_op jit(solution)/shard_map/ppermute | solution.py:444
  265.6 39.2 %collective-permute-start.55 = (bf16[4,2,128,512]{3,2,0,1:T(8,128)(2,1)}, bf16[4,2,128,512]{3,2,0,1:T(8,128)(2,1)}, u32[]{:S(2)}, u32[]{:S(2)}) collective-permute-start(bf16[4,2,128,512]{3,2,0,1:T(8,128)(2,1)} %fusion.22), channel_id=1, source_target_pairs={{0,16},{1,17},{2,18},{3,19},{4,20},{5,21},{6,22},{7,23},{8,24},{9,... | collective-permute-start | bytes 3145736 | tf_op jit(solution)/shard_map/ppermute | solution.py:444
  266.5 38.4 %collective-permute-start.56 = (bf16[2,4,128,512]{3,2,1,0:T(8,128)(2,1)}, bf16[2,4,128,512]{3,2,1,0:T(8,128)(2,1)}, u32[]{:S(2)}, u32[]{:S(2)}) collective-permute-start(bf16[2,4,128,512]{3,2,1,0:T(8,128)(2,1)} %fusion.23), channel_id=1, source_target_pairs={{0,1},{1,0},{2,3},{3,2},{4,5},{5,4},{6,7},{7,6},{8,9},{9,8},{10,11... | collective-permute-start | bytes 3145736 | tf_op jit(solution)/shard_map/ppermute | solution.py:444
  319.4 18.3 %collective-permute-start.58 = (bf16[4,128,512]{2,1,0:T(8,128)(2,1)}, bf16[4,128,512]{2,1,0:T(8,128)(2,1)S(1)}, u32[]{:S(2)}, u32[]{:S(2)}) collective-permute-start(bf16[4,128,512]{2,1,0:T(8,128)(2,1)} %fusion.37), channel_id=1, source_target_pairs={{0,1},{1,0},{2,3},{3,2},{4,5},{5,4},{6,7},{7,6},{8,9},{9,8},{10,11... | collective-permute-start | bytes 1572872 | tf_op jit(solution)/shard_map/ppermute | solution.py:444
  319.9 17.8 %collective-permute-start.59 = (bf16[4,128,512]{2,1,0:T(8,128)(2,1)}, bf16[4,128,512]{2,1,0:T(8,128)(2,1)S(1)}, u32[]{:S(2)}, u32[]{:S(2)}) collective-permute-start(bf16[4,128,512]{2,1,0:T(8,128)(2,1)} %fusion.36), channel_id=1, source_target_pairs={{0,16},{1,17},{2,18},{3,19},{4,20},{5,21},{6,22},{7,23},{8,24},{9,... | collective-permute-start | bytes 1572872 | tf_op jit(solution)/shard_map/ppermute | solution.py:444
  341.7 28.3 %collective-permute-start.60 = (bf16[4,2,32,2048]{3,2,0,1:T(8,128)(2,1)}, bf16[4,2,32,2048]{3,2,0,1:T(8,128)(2,1)}, u32[]{:S(2)}, u32[]{:S(2)}) collective-permute-start(bf16[4,2,32,2048]{3,2,0,1:T(8,128)(2,1)} %fusion.24), channel_id=1, source_target_pairs={{0,16},{1,17},{2,18},{3,19},{4,20},{5,21},{6,22},{7,23},{8,24},{9,... | collective-permute-start | bytes 3145736 | tf_op jit(solution)/shard_map/ppermute | solution.py:444
  342.6 27.5 %collective-permute-start.61 = (bf16[2,4,32,2048]{3,2,1,0:T(8,128)(2,1)}, bf16[2,4,32,2048]{3,2,1,0:T(8,128)(2,1)}, u32[]{:S(2)}, u32[]{:S(2)}) collective-permute-start(bf16[2,4,32,2048]{3,2,1,0:T(8,128)(2,1)} %fusion.25), channel_id=1, source_target_pairs={{0,1},{1,0},{2,3},{3,2},{4,5},{5,4},{6,7},{7,6},{8,9},{9,8},{10,11... | collective-permute-start | bytes 3145736 | tf_op jit(solution)/shard_map/ppermute | solution.py:444
  344.0 26.0 %collective-permute-start.62 = (bf16[128,1024]{1,0:T(8,128)(2,1)}, bf16[128,1024]{1,0:T(8,128)(2,1)S(1)}, u32[]{:S(2)}, u32[]{:S(2)}) collective-permute-start(bf16[128,1024]{1,0:T(8,128)(2,1)} %get-tuple-element.199), channel_id=1, source_target_pairs={{0,2},{1,3},{2,4},{3,5},{4,6},{5,7},{8,10},{9,11},{10,12},{11,13},... | collective-permute-start | bytes 786440 | tf_op jit(solution)/shard_map/ppermute | solution.py:447
  345.3 24.7 %collective-permute-start.63 = (bf16[128,1024]{1,0:T(8,128)(2,1)S(1)}, bf16[128,1024]{1,0:T(8,128)(2,1)S(1)}, u32[]{:S(2)}, u32[]{:S(2)}) collective-permute-start(bf16[128,1024]{1,0:T(8,128)(2,1)S(1)} %get-tuple-element.200), channel_id=1, source_target_pairs={{2,0},{3,1},{4,2},{5,3},{6,4},{7,5},{10,8},{11,9},{12,10},{13,11},... | collective-permute-start | bytes 786440 | tf_op jit(solution)/shard_map/ppermute | solution.py:447
  381.4 16.5 %collective-permute-start.64 = (bf16[512,2560]{1,0:T(8,128)(2,1)}, bf16[512,2560]{1,0:T(8,128)(2,1)}, u32[]{:S(2)}, u32[]{:S(2)}) collective-permute-start(bf16[512,2560]{1,0:T(8,128)(2,1)} %pad_maximum_fusion.1), channel_id=1, source_target_pairs={{0,8},{1,9},{2,10},{3,11},{4,12},{5,13},{6,14},{7,15},{8,0},{9,1},... | collective-permute-start | bytes 7864328 | tf_op jit(solution)/shard_map/ppermute | solution.py:444
  382.3 20.8 %collective-permute-start.67 = (bf16[128,1024]{1,0:T(8,128)(2,1)}, bf16[128,1024]{1,0:T(8,128)(2,1)S(1)}, u32[]{:S(2)}, u32[]{:S(2)}) collective-permute-start(bf16[128,1024]{1,0:T(8,128)(2,1)} %get-tuple-element.216), channel_id=1, source_target_pairs={{0,2},{1,3},{2,4},{3,5},{4,6},{5,7},{8,10},{9,11},{10,12},{11,13},... | collective-permute-start | bytes 786440 | tf_op jit(solution)/shard_map/ppermute | solution.py:447
  409.4 38.0 %collective-permute-start.71 = (bf16[32,4096]{1,0:T(8,128)(2,1)S(1)}, bf16[32,4096]{1,0:T(8,128)(2,1)}, u32[]{:S(2)}, u32[]{:S(2)}) collective-permute-start(bf16[32,4096]{1,0:T(8,128)(2,1)S(1)} %get-tuple-element.227), channel_id=1, source_target_pairs={{0,2},{1,3},{2,4},{3,5},{4,6},{5,7},{8,10},{9,11},{10,12},{11,13},... | collective-permute-start | bytes 786440 | tf_op jit(solution)/shard_map/ppermute | solution.py:447
  414.6 41.3 %collective-permute-start.69 = (bf16[4,2,32,1280]{3,2,0,1:T(8,128)(2,1)}, bf16[4,2,32,1280]{3,2,0,1:T(8,128)(2,1)}, u32[]{:S(2)}, u32[]{:S(2)}) collective-permute-start(bf16[4,2,32,1280]{3,2,0,1:T(8,128)(2,1)} %fusion.54), channel_id=1, source_target_pairs={{0,16},{1,17},{2,18},{3,19},{4,20},{5,21},{6,22},{7,23},{8,24},{9,... | collective-permute-start | bytes 1966088 | tf_op jit(solution)/shard_map/ppermute | solution.py:444
  415.8 40.2 %collective-permute-start.70 = (bf16[2,4,32,1280]{3,2,1,0:T(8,128)(2,1)}, bf16[2,4,32,1280]{3,2,1,0:T(8,128)(2,1)}, u32[]{:S(2)}, u32[]{:S(2)}) collective-permute-start(bf16[2,4,32,1280]{3,2,1,0:T(8,128)(2,1)} %fusion.55), channel_id=1, source_target_pairs={{0,1},{1,0},{2,3},{3,2},{4,5},{5,4},{6,7},{7,6},{8,9},{9,8},{10,11... | collective-permute-start | bytes 1966088 | tf_op jit(solution)/shard_map/ppermute | solution.py:444
  515.6 17.0 %collective-permute-start.90 = (bf16[32,4096]{1,0:T(8,128)(2,1)S(1)}, bf16[32,4096]{1,0:T(8,128)(2,1)S(1)}, u32[]{:S(2)}, u32[]{:S(2)}) collective-permute-start(bf16[32,4096]{1,0:T(8,128)(2,1)S(1)} %get-tuple-element.297), channel_id=1, source_target_pairs={{0,2},{1,3},{2,4},{3,5},{4,6},{5,7},{8,10},{9,11},{10,12},{11,13},... | collective-permute-start | bytes 786440 | tf_op jit(solution)/shard_map/ppermute | solution.py:447
  (156 other events, 1518.5 us)

commit v5 on v4

--- a/solution.py
+++ b/solution.py
@@ -894,9 +894,15 @@
             late_chain.first(), early_chain.swap(early_sent), up_line.move(up_sent)
         )
         two, late_sent = hold(two, late_sent)
+        tokens_grad = (
+            grad_hidden
+            + back_matmul(one, full_qkv[:, : 3 * HALF])
+            + back_matmul(two, full_qkv[:, 3 * HALF :])
+        ).astype(jnp.bfloat16)
+        late_got, tokens_grad = hold(late_chain.swap(late_sent), tokens_grad)
         share_up = up_line.rest(up_got, 3)
         early_block = early_chain.block(received)
-        late_sent = late_chain.second(late_chain.swap(late_sent))
+        late_sent = late_chain.second(late_got)
         late_block = late_chain.block(late_chain.swap(late_sent))
         line = Line(grid, at, jnp.concatenate([early_block, late_block], axis=2))
         block = line.rest(line.move(line.give(1)), 2)
@@ -913,15 +919,15 @@
         share_out = plain_reduce(grid, mixed_parts, branch)
         early, late = plain_reduce(grid, token_parts, one), plain_reduce(grid, token_parts, two)
         shares = [lax.psum_scatter(v, AXES, scatter_dimension=0, tiled=True) for v in totals]
+        tokens_grad = (
+            grad_hidden
+            + back_matmul(one, full_qkv[:, : 3 * HALF])
+            + back_matmul(two, full_qkv[:, 3 * HALF :])
+        ).astype(jnp.bfloat16)
     share_query, share_key, share_value = (
         jnp.concatenate([part[:, i : i + HALF] for part in (early, late)], axis=1)
         for i in range(0, 3 * HALF, HALF)
     )
-    tokens_grad = (
-        grad_hidden
-        + back_matmul(one, full_qkv[:, : 3 * HALF])
-        + back_matmul(two, full_qkv[:, 3 * HALF :])
-    ).astype(jnp.bfloat16)
     return (
         output,
         tokens_grad,

time: 550 us -> 557 us (1.013)
  waiting for transfers between devices: 81.3 us -> 88.9 us
    ppermute x30, waiting for transfers between devices: 27.6 us -> 38.3 us  [along(): return lax.ppermute(values, AXES, self.shifted(axis, step, False))]
    unnamed x197 -> x205, local copies, waits for them, and re-layouts: 28.8 us -> 30.4 us
  transfers between devices with their start and end apart: 92 -> 92, of which waited for: 29 -> 33; matrix products, arithmetic and copies ran while one was open for 14% -> 13% of each run, Pallas kernels for 25% -> 25%
where the time goes in v5:
time: 557 us; the launch traced here: 551 us
  Pallas kernels  167 us (30%)
  starting transfers between devices  128 us (23%)
  waiting for transfers between devices  88.9 us (16%)
  matrix products  65.2 us (12%)
  local copies, waits for them, and re-layouts  53.1 us (10%)
  other arithmetic  46.3 us (8%)
    ppermute x30, starting transfers between devices, along(): return lax.ppermute(values, AXES, self.shifted(axis, step, False))  87.3 us
    pallas_call x3, Pallas kernels, middle_call(): pl.pallas_call(functools.partial(kernel, plan), grid=(rows // TILE,), out...  87.2 us
    ppermute x62, waiting for transfers between devices, swap(): return lax.ppermute(values, AXES, self.shifted(axis, 1, True))  50.6 us
    dot_general x10, matrix products, outer_sum(): lax.dot_general(operand, other, (((0,), (0,)), ((), ())), preferred_eleme...  50.1 us
    pallas_call x2, Pallas kernels, attend_backward(): pl.pallas_call(attend_backward_kernel, grid=(seqs, PAIRS), out_shape=[jax...  46.6 us
    ppermute x62, starting transfers between devices, swap(): return lax.ppermute(values, AXES, self.shifted(axis, 1, True))  40.5 us
    ppermute x30, waiting for transfers between devices, along(): return lax.ppermute(values, AXES, self.shifted(axis, step, False))  38.3 us
    unnamed x205, local copies, waits for them, and re-layouts  30.4 us
  transfers between devices with their start and end apart: 92, of which 33 were waited for; matrix products, arithmetic and copies ran while one was open for 13% of the time, Pallas kernels for 25%

profile of v5, /device:TPU:0, one launch (start us, length us, event | category | flops | bytes accessed | tf_op | source)
XLA Modules:
  0.0 550.7 jit_solution(15932776056838051968)
XLA Ops:
  7.4 5.6 %collective-permute-start = (bf16[32,3200]{1,0:T(8,128)(2,1)S(1)}, bf16[32,3200]{1,0:T(8,128)(2,1)S(1)}, u32[]{:S(2)}, u32[]{:S(2)}) collective-permute-start(bf16[32,3200]{1,0:T(8,128)(2,1)S(1)} %shard_map.307.refs_0_), channel_id=1, source_target_pairs={{0,2},{1,3},{2,4},{3,5},{4,6},{5,7},{8,10},{9,11},{10,12},{11,13},... | collective-permute-start | bytes 614408 | tf_op jit(solution)/shard_map/ppermute | solution.py:447
  17.4 4.6 collective-permute-start.2
  25.5 4.6 collective-permute-start.4
  39.7 7.1 %collective-permute-done.20.refs_4_ = bf16[4,32,1536]{2,1,0:T(8,128)(2,1)S(1)} collective-permute-done((bf16[4,32,1536]{2,1,0:T(8,128)(2,1)S(1)}, bf16[4,32,1536]{2,1,0:T(8,128)(2,1)S(1)}, u32[]{:S(2)}, u32[]{:S(2)}) %collective-permute-start.20) | collective-permute-done | bytes 393248 | tf_op jit(solution)/shard_map/ppermute | solution.py:444
  66.6 4.4 collective-permute-start.8
  74.1 5.9 %collective-permute-done.9.refs_4_ = bf16[288,1024]{1,0:T(8,128)(2,1)S(1)} collective-permute-done((bf16[288,1024]{1,0:T(8,128)(2,1)S(1)}, bf16[288,1024]{1,0:T(8,128)(2,1)S(1)}, u32[]{:S(2)}, u32[]{:S(2)}) %collective-permute-start.9) | collective-permute-done | bytes 589856 | tf_op jit(solution)/shard_map/ppermute | solution.py:447
  82.6 5.3 collective-permute-start.10
  111.9 7.1 %add_convert_fusion.query.key.value = bf16[1024,3072]{1,0:T(8,128)(2,1)S(1)} fusion(f32[3072]{0:T(1024)S(1)} %bitcast.371, bf16[1024,1024]{1,0:T(8,128)(2,1)S(1)} %copy-done.70, bf16[1024,3200]{1,0:T(8,128)(2,1)S(1)} %bitcast.340), kind=kOutput, calls=%fused_computation | convolution fusion | flops 6448742400 | bytes 14692352 | tf_op jit(solution)/shard_map/dot_general | solution.py:19
  119.0 23.0 %shard_map.311.refs_17_ = bf16[1024,1024]{1,0:T(8,128)(2,1)S(1)} custom-call(bf16[1024,3072]{1,0:T(8,128)(2,1)S(1)} %add_convert_fusion.query.key.value, bf16[1024,3072]{1,0:T(8,128)(2,1)S(1)} %add_convert_fusion.query.key.value, bf16[1024,3072]{1,0:T(8,128)(2,1)S(1)} %add_convert_fusion.query.key.value, s32[2,512,1]{2,1,0:T(8,128)S(1)} %copy-done.6, ...), custom_call_target="tpu_custom_call" | custom-call | flops 8589934592 | bytes 25165824 | tf_op jit(solution)/shard_map/pallas_call | solution.py:132
  146.6 14.4 %collective-permute-done.33.refs_7_ = bf16[4,160,512]{2,1,0:T(8,128)(2,1)} collective-permute-done((bf16[4,160,512]{2,1,0:T(8,128)(2,1)}, bf16[4,160,512]{2,1,0:T(8,128)(2,1)}, u32[]{:S(2)}, u32[]{:S(2)}) %collective-permute-start.33) | collective-permute-done | bytes 655392 | tf_op jit(solution)/shard_map/ppermute | solution.py:444
  172.8 28.8 %shard_map.312 = (f32[1024,1024]{1,0:T(8,128)}, f32[1024,1024]{1,0:T(8,128)}, f32[1024,128]{1,0:T(8,128)}, bf16[2,1024,2048]{2,1,0:T(8,128)(2,1)}, bf16[1024,409...) custom-call(s32[4]{0:T(128)} %copy-done.30, ...), custom_call_target="tpu_custom_call" | custom-call | flops 10737418240 | bytes 41943040 | tf_op jit(solution)/shard_map/pallas_call | solution.py:331
  205.6 10.7 %collective-permute-done.47.refs_7_.refs_23_ = bf16[4,128,512]{2,1,0:T(8,128)(2,1)S(1)} collective-permute-done((bf16[4,128,512]{2,1,0:T(8,128)(2,1)S(1)}, bf16[4,128,512]{2,1,0:T(8,128)(2,1)S(1)}, u32[]{:S(2)}, u32[]{:S(2)}) %collective-permute-start.47) | collective-permute-done | bytes 524320 | tf_op jit(solution)/shard_map/ppermute | solution.py:444
  220.1 21.5 %shard_map.313 = (bf16[1024,1024]{1,0:T(8,128)(2,1)}, f32[1024,1024]{1,0:T(8,128)}, bf16[1024,1024]{1,0:T(8,128)(2,1)}, f32[8,1024]{1,0:T(8,128)}) custom-call(s32[4]{0:T(128)} %copy-done.30, bf16[4,128,512]{2,1,0:T(8,128)(2,1)} %copy-done.61, bf16[4,128,512]{2,1,0:T(8,128)(2,1)} %copy-done.77, bf16[4,128,512]{2,1,0:T(8,128)(2,1)} %copy-done.76, ...), custom_call_target="tpu_custom_call" | custom-call | flops 8589934592 | bytes 41943040 | tf_op jit(solution)/shard_map/pallas_call | solution.py:331
  241.6 9.6 %fusion.13 = bf16[2048,1024]{1,0:T(8,128)(2,1)} fusion(bf16[1024,1024]{1,0:T(8,128)(2,1)} %get-tuple-element.181.refs_33_, bf16[2,1024,2048]{2,1,0:T(8,128)(2,1)} %get-tuple-element.174.refs_18_), kind=kOutput, calls=%fused_computation.13 | convolution fusion | flops 4297064448 | bytes 10485760 | tf_op jit(solution)/shard_map/dot_general | solution.py:29
  251.3 7.0 %fusion.10 = bf16[2048,1024]{1,0:T(8,128)(2,1)S(1)} fusion(bf16[1024,1024]{1,0:T(8,128)(2,1)S(1)} %copy-done.96, bf16[2,1024,2048]{2,1,0:T(8,128)(2,1)} %get-tuple-element.174.refs_18_), kind=kOutput, calls=%fused_computation.12 | convolution fusion | flops 4297064448 | bytes 10485760 | tf_op jit(solution)/shard_map/dot_general | solution.py:29
  268.0 36.9 %shard_map.314 = (bf16[1024,4096]{1,0:T(8,128)(2,1)}, f32[1024,1024]{1,0:T(8,128)}, bf16[1024,1024]{1,0:T(8,128)(2,1)}, bf16[1024,1024]{1,0:T(8,128)(2,1)}, f32[8,1024]{1,0:T(8,128)}, /*index=5*/f32[1,4096]{1,0:T(1,128)}) custom-call(s32[4]{0:T(128)} %copy-done.30, bf16[4,160,512]{2,1,0:T(8,128)(2,1)} %copy-done.58, bf16[4,160,512]{2,1,0:T(8,128)(2,1)} %copy-done.73, ...), custom_call_target="tpu_custom_call" | custom-call | flops 19327352832 | bytes 41943040 | tf_op jit(solution)/shard_map/pallas_call | solution.py:331
  309.7 9.7 %convolution_convert_fusion = bf16[512,4096]{1,0:T(8,128)(2,1)} fusion(bf16[1024,4096]{1,0:T(8,128)(2,1)} %get-tuple-element.192, bf16[2,1024,512]{2,1,0:T(8,128)(2,1)S(1)} %copy-done.94), kind=kOutput, calls=%fused_computation.3 | convolution fusion | flops 4297064448 | bytes 13631488 | tf_op jit(solution)/shard_map/dot_general | solution.py:29
  321.1 8.4 %convolution_convert_fusion.1 = bf16[512,4096]{1,0:T(8,128)(2,1)S(1)} fusion(bf16[1024,4096]{1,0:T(8,128)(2,1)} %get-tuple-element.192, bf16[2,1024,512]{2,1,0:T(8,128)(2,1)S(1)} %copy-done.95), kind=kOutput, calls=%fused_computation.4 | convolution fusion | flops 4297064448 | bytes 13631488 | tf_op jit(solution)/shard_map/dot_general | solution.py:29
  330.1 4.2 fusion.129
  346.8 23.4 %shard_map.315 = (bf16[1024,1536]{1,0:T(8,128)(2,1)}, f32[1,1536]{1,0:T(1,128)S(1)}) custom-call(bf16[1024,3072]{1,0:T(8,128)(2,1)} %copy-done.31, bf16[1024,3072]{1,0:T(8,128)(2,1)} %copy-done.31, bf16[1024,3072]{1,0:T(8,128)(2,1)} %copy-done.31, bf16[1024,1024]{1,0:T(8,128)(2,1)S(1)} %copy-done.33, s32[2,512,1]{2,1,0:T(8,128)S(1)} %copy-done.6, ...), custom_call_target="tpu_custom_call" | custom-call | flops 10737418240 | bytes 25165824 | tf_op jit(solution)/shard_map/pallas_call | solution.py:149
  382.4 5.3 collective-permute-start.67
  409.4 5.3 collective-permute-start.71
  417.4 23.2 %shard_map.316 = (bf16[1024,1536]{1,0:T(8,128)(2,1)}, f32[1,1536]{1,0:T(1,128)S(1)}) custom-call(bf16[1024,3072]{1,0:T(8,128)(2,1)} %copy-done.31, bf16[1024,3072]{1,0:T(8,128)(2,1)} %copy-done.31, bf16[1024,3072]{1,0:T(8,128)(2,1)} %copy-done.31, bf16[1024,1024]{1,0:T(8,128)(2,1)S(1)} %copy-done.33, s32[2,512,1]{2,1,0:T(8,128)S(1)} %copy-done.6, ...), custom_call_target="tpu_custom_call" | custom-call | flops 10737418240 | bytes 25165824 | tf_op jit(solution)/shard_map/pallas_call | solution.py:149
  442.1 5.2 collective-permute-start.73
  450.9 5.1 collective-permute-done.74
  484.0 4.6 add_convert_fusion.1
  502.5 4.5 collective-permute-start.84
  508.3 5.4 collective-permute-done.84
  514.5 5.1 collective-permute-start.85
  527.2 5.0 collective-permute-start.90
  533.5 4.6 collective-permute-start.86
  542.0 4.5 collective-permute-done.89
  (486 shorter events, 228.1 us)
Async XLA Ops:
  61.6 18.3 %collective-permute-start.9 = (bf16[288,1024]{1,0:T(8,128)(2,1)S(1)}, bf16[288,1024]{1,0:T(8,128)(2,1)S(1)}, u32[]{:S(2)}, u32[]{:S(2)}) collective-permute-start(bf16[288,1024]{1,0:T(8,128)(2,1)S(1)} %collective-permute-done.7.refs_2_), channel_id=1, source_target_pairs={{2,0},{3,1},{4,2},{5,3},{6,4},{7,5},{10,8},{11,9},{12,10},{13,11},... | collective-permute-start | bytes 1769480 | tf_op jit(solution)/shard_map/ppermute | solution.py:447
  71.8 16.2 %collective-permute-start.26 = (bf16[4,32,1664]{2,1,0:T(8,128)(2,1)}, bf16[4,32,1664]{2,1,0:T(8,128)(2,1)}, u32[]{:S(2)}, u32[]{:S(2)}) collective-permute-start(bf16[4,32,1664]{2,1,0:T(8,128)(2,1)} %collective-permute-done.25.refs_10_), channel_id=1, source_target_pairs={{0,8},{1,9},{2,10},{3,11},{4,12},{5,13},{6,14},{7,15},{8,0},{9,1},... | collective-permute-start | bytes 1277960 | tf_op jit(solution)/shard_map/ppermute | solution.py:444
  80.0 22.5 %collective-permute-start.11 = (bf16[288,1024]{1,0:T(8,128)(2,1)S(1)}, bf16[288,1024]{1,0:T(8,128)(2,1)}, u32[]{:S(2)}, u32[]{:S(2)}) collective-permute-start(bf16[288,1024]{1,0:T(8,128)(2,1)S(1)} %collective-permute-done.9.refs_4_), channel_id=1, source_target_pairs={{2,0},{3,1},{4,2},{5,3},{6,4},{7,5},{10,8},{11,9},{12,10},{13,11},... | collective-permute-start | bytes 1769480 | tf_op jit(solution)/shard_map/ppermute | solution.py:447
  82.6 19.9 %collective-permute-start.10 = (bf16[288,1024]{1,0:T(8,128)(2,1)}, bf16[288,1024]{1,0:T(8,128)(2,1)}, u32[]{:S(2)}, u32[]{:S(2)}) collective-permute-start(bf16[288,1024]{1,0:T(8,128)(2,1)} %collective-permute-done.8.refs_3_), channel_id=1, source_target_pairs={{0,2},{1,3},{2,4},{3,5},{4,6},{5,7},{8,10},{9,11},{10,12},{11,13},... | collective-permute-start | bytes 1769480 | tf_op jit(solution)/shard_map/ppermute | solution.py:447
  107.7 38.3 %collective-permute-start.35 = (bf16[4,160,512]{2,1,0:T(8,128)(2,1)S(1)}, bf16[4,160,512]{2,1,0:T(8,128)(2,1)S(1)}, u32[]{:S(2)}, u32[]{:S(2)}) collective-permute-start(bf16[4,160,512]{2,1,0:T(8,128)(2,1)S(1)} %get-tuple-element.159.refs_9_), channel_id=1, source_target_pairs={{0,8},{1,9},{2,10},{3,11},{4,12},{5,13},{6,14},{7,15},{8,0},{9,1},... | collective-permute-start | bytes 1966088 | tf_op jit(solution)/shard_map/ppermute | solution.py:444
  107.8 35.6 %collective-permute-start.16 = (bf16[4,160,512]{2,1,0:T(8,128)(2,1)S(1)}, bf16[4,160,512]{2,1,0:T(8,128)(2,1)}, u32[]{:S(2)}, u32[]{:S(2)}) collective-permute-start(bf16[4,160,512]{2,1,0:T(8,128)(2,1)S(1)} %get-tuple-element.159.refs_9_), channel_id=1, source_target_pairs={{0,1},{1,0},{2,3},{3,2},{4,5},{5,4},{6,7},{7,6},{8,9},{9,8},{10,11... | collective-permute-start | bytes 1966088 | tf_op jit(solution)/shard_map/ppermute | solution.py:444
  109.4 34.0 %collective-permute-start.15 = (bf16[4,160,512]{2,1,0:T(8,128)(2,1)S(1)}, bf16[4,160,512]{2,1,0:T(8,128)(2,1)}, u32[]{:S(2)}, u32[]{:S(2)}) collective-permute-start(bf16[4,160,512]{2,1,0:T(8,128)(2,1)S(1)} %get-tuple-element.159.refs_9_), channel_id=1, source_target_pairs={{0,16},{1,17},{2,18},{3,19},{4,20},{5,21},{6,22},{7,23},{8,24},{9,... | collective-permute-start | bytes 1966088 | tf_op jit(solution)/shard_map/ppermute | solution.py:444
  109.9 33.5 %collective-permute-start.14 = (bf16[4,160,512]{2,1,0:T(8,128)(2,1)S(1)}, bf16[4,160,512]{2,1,0:T(8,128)(2,1)S(1)}, u32[]{:S(2)}, u32[]{:S(2)}) collective-permute-start(bf16[4,160,512]{2,1,0:T(8,128)(2,1)S(1)} %get-tuple-element.151.refs_1_), channel_id=1, source_target_pairs={{0,16},{1,17},{2,18},{3,19},{4,20},{5,21},{6,22},{7,23},{8,24},{9,... | collective-permute-start | bytes 1966088 | tf_op jit(solution)/shard_map/ppermute | solution.py:444
  111.4 32.0 %collective-permute-start.13 = (bf16[4,160,512]{2,1,0:T(8,128)(2,1)S(1)}, bf16[4,160,512]{2,1,0:T(8,128)(2,1)}, u32[]{:S(2)}, u32[]{:S(2)}) collective-permute-start(bf16[4,160,512]{2,1,0:T(8,128)(2,1)S(1)} %get-tuple-element.151.refs_1_), channel_id=1, source_target_pairs={{0,1},{1,0},{2,3},{3,2},{4,5},{5,4},{6,7},{7,6},{8,9},{9,8},{10,11... | collective-permute-start | bytes 1966088 | tf_op jit(solution)/shard_map/ppermute | solution.py:444
  143.9 17.0 %collective-permute-start.33 = (bf16[4,160,512]{2,1,0:T(8,128)(2,1)}, bf16[4,160,512]{2,1,0:T(8,128)(2,1)}, u32[]{:S(2)}, u32[]{:S(2)}) collective-permute-start(bf16[4,160,512]{2,1,0:T(8,128)(2,1)} %collective-permute-done.13.refs_3_), channel_id=1, source_target_pairs={{0,16},{1,17},{2,18},{3,19},{4,20},{5,21},{6,22},{7,23},{8,24},{9,... | collective-permute-start | bytes 1966088 | tf_op jit(solution)/shard_map/ppermute | solution.py:444
  144.8 16.8 %collective-permute-start.38 = (bf16[4,160,512]{2,1,0:T(8,128)(2,1)}, bf16[4,160,512]{2,1,0:T(8,128)(2,1)}, u32[]{:S(2)}, u32[]{:S(2)}) collective-permute-start(bf16[4,160,512]{2,1,0:T(8,128)(2,1)} %collective-permute-done.15.refs_11_), channel_id=1, source_target_pairs={{0,1},{1,0},{2,3},{3,2},{4,5},{5,4},{6,7},{7,6},{8,9},{9,8},{10,11... | collective-permute-start | bytes 1966088 | tf_op jit(solution)/shard_map/ppermute | solution.py:444
  146.0 22.6 %collective-permute-start.31 = (bf16[4,160,512]{2,1,0:T(8,128)(2,1)}, bf16[4,160,512]{2,1,0:T(8,128)(2,1)}, u32[]{:S(2)}, u32[]{:S(2)}) collective-permute-start(bf16[4,160,512]{2,1,0:T(8,128)(2,1)} %collective-permute-done.13.refs_3_), channel_id=1, source_target_pairs={{0,8},{1,9},{2,10},{3,11},{4,12},{5,13},{6,14},{7,15},{8,0},{9,1},... | collective-permute-start | bytes 1966088 | tf_op jit(solution)/shard_map/ppermute | solution.py:444
  146.0 22.6 %collective-permute-start.36 = (bf16[4,160,512]{2,1,0:T(8,128)(2,1)}, bf16[4,160,512]{2,1,0:T(8,128)(2,1)}, u32[]{:S(2)}, u32[]{:S(2)}) collective-permute-start(bf16[4,160,512]{2,1,0:T(8,128)(2,1)} %collective-permute-done.15.refs_11_), channel_id=1, source_target_pairs={{0,8},{1,9},{2,10},{3,11},{4,12},{5,13},{6,14},{7,15},{8,0},{9,1},... | collective-permute-start | bytes 1966088 | tf_op jit(solution)/shard_map/ppermute | solution.py:444
  146.5 22.1 %collective-permute-start.37 = (bf16[4,160,512]{2,1,0:T(8,128)(2,1)}, bf16[4,160,512]{2,1,0:T(8,128)(2,1)}, u32[]{:S(2)}, u32[]{:S(2)}) collective-permute-start(bf16[4,160,512]{2,1,0:T(8,128)(2,1)} %collective-permute-done.16.refs_13_), channel_id=1, source_target_pairs={{0,8},{1,9},{2,10},{3,11},{4,12},{5,13},{6,14},{7,15},{8,0},{9,1},... | collective-permute-start | bytes 1966088 | tf_op jit(solution)/shard_map/ppermute | solution.py:444
  168.7 33.0 %collective-permute-start.42 = (bf16[4,128,512]{2,1,0:T(8,128)(2,1)S(1)}, bf16[4,128,512]{2,1,0:T(8,128)(2,1)S(1)}, u32[]{:S(2)}, u32[]{:S(2)}) collective-permute-start(bf16[4,128,512]{2,1,0:T(8,128)(2,1)S(1)} %get-tuple-element.149.refs_1_.refs_17_), channel_id=1, source_target_pairs={{0,16},{1,17},{2,18},{3,19},{4,20},{5,21},{6,22},{7,23},{8,24},{9,... | collective-permute-start | bytes 1572872 | tf_op jit(solution)/shard_map/ppermute | solution.py:444
  169.9 31.9 %collective-permute-start.41 = (bf16[4,128,512]{2,1,0:T(8,128)(2,1)S(1)}, bf16[4,128,512]{2,1,0:T(8,128)(2,1)S(1)}, u32[]{:S(2)}, u32[]{:S(2)}) collective-permute-start(bf16[4,128,512]{2,1,0:T(8,128)(2,1)S(1)} %get-tuple-element.149.refs_1_.refs_17_), channel_id=1, source_target_pairs={{0,1},{1,0},{2,3},{3,2},{4,5},{5,4},{6,7},{7,6},{8,9},{9,8},{10,11... | collective-permute-start | bytes 1572872 | tf_op jit(solution)/shard_map/ppermute | solution.py:444
  171.4 33.6 %collective-permute-start.40 = (bf16[4,128,512]{2,1,0:T(8,128)(2,1)S(1)}, bf16[4,128,512]{2,1,0:T(8,128)(2,1)S(1)}, u32[]{:S(2)}, u32[]{:S(2)}) collective-permute-start(bf16[4,128,512]{2,1,0:T(8,128)(2,1)S(1)} %get-tuple-element.149.refs_1_.refs_17_), channel_id=1, source_target_pairs={{0,8},{1,9},{2,10},{3,11},{4,12},{5,13},{6,14},{7,15},{8,0},{9,1},... | collective-permute-start | bytes 1572872 | tf_op jit(solution)/shard_map/ppermute | solution.py:444
  171.4 30.4 %collective-permute-start.44 = (bf16[4,128,512]{2,1,0:T(8,128)(2,1)S(1)}, bf16[4,128,512]{2,1,0:T(8,128)(2,1)S(1)}, u32[]{:S(2)}, u32[]{:S(2)}) collective-permute-start(bf16[4,128,512]{2,1,0:T(8,128)(2,1)S(1)} %get-tuple-element.150.refs_9_.refs_25_), channel_id=1, source_target_pairs={{0,1},{1,0},{2,3},{3,2},{4,5},{5,4},{6,7},{7,6},{8,9},{9,8},{10,11... | collective-permute-start | bytes 1572872 | tf_op jit(solution)/shard_map/ppermute | solution.py:444
  171.9 29.9 %collective-permute-start.43 = (bf16[4,128,512]{2,1,0:T(8,128)(2,1)S(1)}, bf16[4,128,512]{2,1,0:T(8,128)(2,1)}, u32[]{:S(2)}, u32[]{:S(2)}) collective-permute-start(bf16[4,128,512]{2,1,0:T(8,128)(2,1)S(1)} %get-tuple-element.150.refs_9_.refs_25_), channel_id=1, source_target_pairs={{0,16},{1,17},{2,18},{3,19},{4,20},{5,21},{6,22},{7,23},{8,24},{9,... | collective-permute-start | bytes 1572872 | tf_op jit(solution)/shard_map/ppermute | solution.py:444
  265.6 39.3 %collective-permute-start.55 = (bf16[4,2,128,512]{3,2,0,1:T(8,128)(2,1)}, bf16[4,2,128,512]{3,2,0,1:T(8,128)(2,1)}, u32[]{:S(2)}, u32[]{:S(2)}) collective-permute-start(bf16[4,2,128,512]{3,2,0,1:T(8,128)(2,1)} %fusion.22), channel_id=1, source_target_pairs={{0,16},{1,17},{2,18},{3,19},{4,20},{5,21},{6,22},{7,23},{8,24},{9,... | collective-permute-start | bytes 3145736 | tf_op jit(solution)/shard_map/ppermute | solution.py:444
  266.5 38.4 %collective-permute-start.56 = (bf16[2,4,128,512]{3,2,1,0:T(8,128)(2,1)}, bf16[2,4,128,512]{3,2,1,0:T(8,128)(2,1)}, u32[]{:S(2)}, u32[]{:S(2)}) collective-permute-start(bf16[2,4,128,512]{3,2,1,0:T(8,128)(2,1)} %fusion.23), channel_id=1, source_target_pairs={{0,1},{1,0},{2,3},{3,2},{4,5},{5,4},{6,7},{7,6},{8,9},{9,8},{10,11... | collective-permute-start | bytes 3145736 | tf_op jit(solution)/shard_map/ppermute | solution.py:444
  319.4 18.3 %collective-permute-start.58 = (bf16[4,128,512]{2,1,0:T(8,128)(2,1)}, bf16[4,128,512]{2,1,0:T(8,128)(2,1)S(1)}, u32[]{:S(2)}, u32[]{:S(2)}) collective-permute-start(bf16[4,128,512]{2,1,0:T(8,128)(2,1)} %fusion.37), channel_id=1, source_target_pairs={{0,1},{1,0},{2,3},{3,2},{4,5},{5,4},{6,7},{7,6},{8,9},{9,8},{10,11... | collective-permute-start | bytes 1572872 | tf_op jit(solution)/shard_map/ppermute | solution.py:444
  320.0 17.8 %collective-permute-start.59 = (bf16[4,128,512]{2,1,0:T(8,128)(2,1)}, bf16[4,128,512]{2,1,0:T(8,128)(2,1)S(1)}, u32[]{:S(2)}, u32[]{:S(2)}) collective-permute-start(bf16[4,128,512]{2,1,0:T(8,128)(2,1)} %fusion.36), channel_id=1, source_target_pairs={{0,16},{1,17},{2,18},{3,19},{4,20},{5,21},{6,22},{7,23},{8,24},{9,... | collective-permute-start | bytes 1572872 | tf_op jit(solution)/shard_map/ppermute | solution.py:444
  341.8 28.4 %collective-permute-start.60 = (bf16[4,2,32,2048]{3,2,0,1:T(8,128)(2,1)}, bf16[4,2,32,2048]{3,2,0,1:T(8,128)(2,1)}, u32[]{:S(2)}, u32[]{:S(2)}) collective-permute-start(bf16[4,2,32,2048]{3,2,0,1:T(8,128)(2,1)} %fusion.24), channel_id=1, source_target_pairs={{0,16},{1,17},{2,18},{3,19},{4,20},{5,21},{6,22},{7,23},{8,24},{9,... | collective-permute-start | bytes 3145736 | tf_op jit(solution)/shard_map/ppermute | solution.py:444
  342.7 27.5 %collective-permute-start.61 = (bf16[2,4,32,2048]{3,2,1,0:T(8,128)(2,1)}, bf16[2,4,32,2048]{3,2,1,0:T(8,128)(2,1)}, u32[]{:S(2)}, u32[]{:S(2)}) collective-permute-start(bf16[2,4,32,2048]{3,2,1,0:T(8,128)(2,1)} %fusion.25), channel_id=1, source_target_pairs={{0,1},{1,0},{2,3},{3,2},{4,5},{5,4},{6,7},{7,6},{8,9},{9,8},{10,11... | collective-permute-start | bytes 3145736 | tf_op jit(solution)/shard_map/ppermute | solution.py:444
  344.1 26.0 %collective-permute-start.62 = (bf16[128,1024]{1,0:T(8,128)(2,1)}, bf16[128,1024]{1,0:T(8,128)(2,1)S(1)}, u32[]{:S(2)}, u32[]{:S(2)}) collective-permute-start(bf16[128,1024]{1,0:T(8,128)(2,1)} %get-tuple-element.202), channel_id=1, source_target_pairs={{0,2},{1,3},{2,4},{3,5},{4,6},{5,7},{8,10},{9,11},{10,12},{11,13},... | collective-permute-start | bytes 786440 | tf_op jit(solution)/shard_map/ppermute | solution.py:447
  345.4 24.7 %collective-permute-start.63 = (bf16[128,1024]{1,0:T(8,128)(2,1)S(1)}, bf16[128,1024]{1,0:T(8,128)(2,1)S(1)}, u32[]{:S(2)}, u32[]{:S(2)}) collective-permute-start(bf16[128,1024]{1,0:T(8,128)(2,1)S(1)} %get-tuple-element.203), channel_id=1, source_target_pairs={{2,0},{3,1},{4,2},{5,3},{6,4},{7,5},{10,8},{11,9},{12,10},{13,11},... | collective-permute-start | bytes 786440 | tf_op jit(solution)/shard_map/ppermute | solution.py:447
  381.5 16.5 %collective-permute-start.64 = (bf16[512,2560]{1,0:T(8,128)(2,1)}, bf16[512,2560]{1,0:T(8,128)(2,1)}, u32[]{:S(2)}, u32[]{:S(2)}) collective-permute-start(bf16[512,2560]{1,0:T(8,128)(2,1)} %pad_maximum_fusion.1), channel_id=1, source_target_pairs={{0,8},{1,9},{2,10},{3,11},{4,12},{5,13},{6,14},{7,15},{8,0},{9,1},... | collective-permute-start | bytes 7864328 | tf_op jit(solution)/shard_map/ppermute | solution.py:444
  382.4 20.8 %collective-permute-start.67 = (bf16[128,1024]{1,0:T(8,128)(2,1)}, bf16[128,1024]{1,0:T(8,128)(2,1)S(1)}, u32[]{:S(2)}, u32[]{:S(2)}) collective-permute-start(bf16[128,1024]{1,0:T(8,128)(2,1)} %get-tuple-element.218), channel_id=1, source_target_pairs={{0,2},{1,3},{2,4},{3,5},{4,6},{5,7},{8,10},{9,11},{10,12},{11,13},... | collective-permute-start | bytes 786440 | tf_op jit(solution)/shard_map/ppermute | solution.py:447
  409.4 38.0 %collective-permute-start.71 = (bf16[32,4096]{1,0:T(8,128)(2,1)S(1)}, bf16[32,4096]{1,0:T(8,128)(2,1)}, u32[]{:S(2)}, u32[]{:S(2)}) collective-permute-start(bf16[32,4096]{1,0:T(8,128)(2,1)S(1)} %get-tuple-element.229), channel_id=1, source_target_pairs={{0,2},{1,3},{2,4},{3,5},{4,6},{5,7},{8,10},{9,11},{10,12},{11,13},... | collective-permute-start | bytes 786440 | tf_op jit(solution)/shard_map/ppermute | solution.py:447
  414.7 41.3 %collective-permute-start.69 = (bf16[4,2,32,1280]{3,2,0,1:T(8,128)(2,1)}, bf16[4,2,32,1280]{3,2,0,1:T(8,128)(2,1)}, u32[]{:S(2)}, u32[]{:S(2)}) collective-permute-start(bf16[4,2,32,1280]{3,2,0,1:T(8,128)(2,1)} %fusion.54), channel_id=1, source_target_pairs={{0,16},{1,17},{2,18},{3,19},{4,20},{5,21},{6,22},{7,23},{8,24},{9,... | collective-permute-start | bytes 1966088 | tf_op jit(solution)/shard_map/ppermute | solution.py:444
  415.8 40.1 %collective-permute-start.70 = (bf16[2,4,32,1280]{3,2,1,0:T(8,128)(2,1)}, bf16[2,4,32,1280]{3,2,1,0:T(8,128)(2,1)}, u32[]{:S(2)}, u32[]{:S(2)}) collective-permute-start(bf16[2,4,32,1280]{3,2,1,0:T(8,128)(2,1)} %fusion.55), channel_id=1, source_target_pairs={{0,1},{1,0},{2,3},{3,2},{4,5},{5,4},{6,7},{7,6},{8,9},{9,8},{10,11... | collective-permute-start | bytes 1966088 | tf_op jit(solution)/shard_map/ppermute | solution.py:444
  (160 other events, 1503.0 us)
